TPU v7x, 32 devices: a whole 2x2x4 slice. The times are simulated.
32 devices in a mesh: seq: 8 (over z, y), batch: 4 (over x, core).
Axes of the slice: x: 2, y: 2, z: 4, core: 2. Of those that a mesh axis runs over, the one named last changes fastest.
Arguments:
- stream_in: bfloat16 [8, 1024, 512], P('batch', 'seq'), may hold values from -6 to 6
- out_grad: bfloat16 [8, 1024, 512], P('batch', 'seq'), may hold values from -6 to 6
- doc_lengths: int32 [8, 16], P('batch'), may hold values from 0 to 897, as said below
- mats: float32 [2, 4, 2048, 512], P(None, 'batch', 'seq')
- mat_momenta: float32 [2, 4, 2048, 512], P(None, 'batch', 'seq')
- mat_averages: float32 [2, 4, 2048, 512], P(None, 'batch', 'seq')
- vectors: float32 [2, 3072], replicated
- vec_momenta: float32 [2, 3072], replicated
- vec_averages: float32 [2, 3072], replicated
Outputs:
- activations: bfloat16 [8, 1024, 512], P('batch', 'seq')
- input_grad: float32 [8, 1024, 512], P('batch', 'seq')
- mat_grads: float32 [2, 4, 2048, 512], P(None, 'batch', 'seq')
- new_momenta: float32 [2, 4, 2048, 512], P(None, 'batch')
- new_mats: float32 [2, 4, 2048, 512], P(None, 'batch', 'seq')
- new_averages: float32 [2, 4, 2048, 512], P(None, 'batch', 'seq')
- vec_grads: float32 [2, 3072], replicated
- new_vec_momenta: float32 [2, 3072], replicated
- new_vectors: float32 [2, 3072], replicated
- new_vec_averages: float32 [2, 3072], replicated
Inputs may be any that keep to these rules, and one draw needn't show every extreme that they name: `doc_lengths`: each row sums to 1024; in every group of 2 consecutive streams one stream holds a document of exactly 897 tokens.
All inputs are finite; a program needn't handle non-finite values.
Results may differ from a plain program's by a relative error of at most 0.0085.
The roundings to bfloat16 on the way count: a program that leaves them out, or rounds other values in their place, can miss the bound.
Values may be sent and summed in bfloat16 or wider, within the bound.
A program may use at most 192 MiB of HBM per device.

v0:
```python
import math

import jax
import jax.numpy as jnp
from jax import lax
from jax.sharding import PartitionSpec as P

H = 1024
FF = 2048
NS_STEPS = 2


EPSILON = 1e-05
MOMENTUM_DECAY = 0.5
AVERAGE_DECAY = 0.9
MATRIX_RATE = 0.3
SEGMENT_RATES = (0.3, 0.3, 0.5, 2.0)
QUINTIC = (3.4445, -4.775, 2.0315)


def carried_in(x, axis, combine, identity, reverse):
    devices, index = (lax.axis_size(axis), lax.axis_index(axis))
    everything = jax.tree.map(lambda part: lax.all_gather(part, axis), x)
    start = jax.tree.map(
        lambda part, zero: jnp.broadcast_to(jnp.asarray(zero, part.dtype), part.shape), x, identity
    )

    def hop(k, before):
        at = devices - 1 - k if reverse else k
        reached = at > index if reverse else at < index
        new = combine(before, jax.tree.map(lambda part: part[at], everything))
        return jax.tree.map(lambda a, b: jnp.where(reached, a, b), new, before)

    return lax.fori_loop(0, devices, hop, start)


def row_offsets(hid_block, ffn_block):
    return [
        0,
        hid_block,
        2 * hid_block,
        3 * hid_block,
        4 * hid_block,
        4 * hid_block + ffn_block,
        4 * hid_block + 2 * ffn_block,
    ]


def split_block(gathered, layer_idx, offsets):
    blocks = gathered.shape[1]
    return [
        gathered[layer_idx, :, offsets[member] : offsets[member + 1], :].reshape(
            blocks * (offsets[member + 1] - offsets[member]), gathered.shape[3]
        )
        for member in range(6)
    ]


def pack_rows(per_layer, blocks):
    return jnp.stack(
        [
            jnp.concatenate(
                [
                    matrix.reshape(blocks, matrix.shape[0] // blocks, matrix.shape[1])
                    for matrix in matrices
                ],
                axis=1,
            )
            for matrices in per_layer
        ]
    )


def rms_scale(values):
    return lax.rsqrt(jnp.mean(values * values, axis=-1, keepdims=True) + EPSILON)


def linked(earlier, latter):
    return (earlier[0] * latter[0], latter[0] * earlier[1] + latter[1])


def gelu_tanh(values):
    return jax.nn.gelu(values, approximate=True)


def vector_steps(moments, model_width, hidden):
    edge_list = [
        0,
        model_width,
        2 * model_width,
        2 * model_width + hidden,
        2 * model_width + 2 * hidden,
    ]
    pieces = []
    for member in range(4):
        segment = moments[:, edge_list[member] : edge_list[member + 1]]
        pieces.append(
            SEGMENT_RATES[member]
            * segment
            * lax.rsqrt(jnp.mean(segment * segment, axis=1, keepdims=True) + 1e-06)
        )
    return jnp.concatenate(pieces, axis=1)


def layer_front(residual, weights, vector_row, carry_mask, model_width, hidden):
    gain_one = vector_row[:model_width]
    bias_forget = vector_row[2 * model_width : 2 * model_width + hidden]
    bias_input = vector_row[2 * model_width + hidden :]
    scale_one = rms_scale(residual)
    gated_in = (residual * scale_one * gain_one).astype(jnp.bfloat16)
    pre_forget = (
        jnp.einsum("scd,hd->sch", gated_in, weights[0], preferred_element_type=jnp.float32)
        + bias_forget
    )
    pre_input = (
        jnp.einsum("scd,hd->sch", gated_in, weights[1], preferred_element_type=jnp.float32)
        + bias_input
    )
    candidate = jnp.einsum("scd,hd->sch", gated_in, weights[2], preferred_element_type=jnp.float32)
    forget_gate = jax.nn.sigmoid(pre_forget)
    input_gate = jax.nn.sigmoid(pre_input)
    gate_total = forget_gate + input_gate
    decay_coef = forget_gate / gate_total * carry_mask[:, :, None]
    input_term = input_gate / gate_total * candidate
    decay_prod, local_states = lax.associative_scan(linked, (decay_coef, input_term), axis=1)
    return (
        scale_one,
        gated_in,
        forget_gate,
        input_gate,
        gate_total,
        candidate,
        decay_coef,
        decay_prod,
        local_states,
    )


def forward_carry(front_parts):
    decay_prod = front_parts[7]
    local_states = front_parts[8]
    identity = (jnp.ones_like(decay_prod[:, -1]), jnp.zeros_like(local_states[:, -1]))
    return carried_in((decay_prod[:, -1], local_states[:, -1]), "seq", linked, identity, False)[1]


def layer_rear(residual, front_parts, state_in, weights, vector_row, model_width):
    gain_two = vector_row[model_width : 2 * model_width]
    decay_prod = front_parts[7]
    local_states = front_parts[8]
    states = local_states + decay_prod * state_in[:, None, :]
    states_low = states.astype(jnp.bfloat16)
    middle = residual + jnp.einsum(
        "sch,hd->scd", states_low, weights[3], preferred_element_type=jnp.float32
    )
    scale_two = rms_scale(middle)
    normed = (middle * scale_two * gain_two).astype(jnp.bfloat16)
    inner_pre = jnp.einsum("scd,fd->scf", normed, weights[4], preferred_element_type=jnp.float32)
    active = gelu_tanh(inner_pre).astype(jnp.bfloat16)
    output = middle + jnp.einsum(
        "scf,fd->scd", active, weights[5], preferred_element_type=jnp.float32
    )
    return (states, states_low, middle, scale_two, normed, inner_pre, active, output)


def layer_back(
    grad_out,
    residual,
    front_parts,
    rear_parts,
    state_in,
    weights,
    vector_row,
    carry_mask,
    model_width,
):
    (
        scale_one,
        gated_in,
        forget_gate,
        input_gate,
        gate_total,
        candidate,
        decay_coef,
        decay_prod,
        local_states,
    ) = front_parts
    states, states_low, middle, scale_two, normed, inner_pre, active, output = rear_parts
    gain_one = vector_row[:model_width]
    gain_two = vector_row[model_width : 2 * model_width]
    grad_mlp = grad_out.astype(jnp.bfloat16)
    grad_down = jnp.einsum("scf,scd->fd", active, grad_mlp, preferred_element_type=jnp.float32)
    grad_active = jnp.einsum(
        "scd,fd->scf", grad_mlp, weights[5], preferred_element_type=jnp.float32
    )
    gelu_vals, gelu_pull = jax.vjp(gelu_tanh, inner_pre)
    grad_inner = gelu_pull(grad_active)[0].astype(jnp.bfloat16)
    grad_up = jnp.einsum("scf,scd->fd", grad_inner, normed, preferred_element_type=jnp.float32)
    grad_normed = jnp.einsum(
        "scf,fd->scd", grad_inner, weights[4], preferred_element_type=jnp.float32
    )
    unit_two = middle * scale_two
    grad_gain_two = jnp.sum(grad_normed * unit_two, axis=(0, 1))
    grad_unit_two = grad_normed * gain_two
    grad_middle = grad_out + scale_two * (
        grad_unit_two - unit_two * jnp.mean(grad_unit_two * unit_two, axis=-1, keepdims=True)
    )
    grad_y = grad_middle.astype(jnp.bfloat16)
    grad_wout = jnp.einsum("sch,scd->hd", states_low, grad_y, preferred_element_type=jnp.float32)
    grad_states = jnp.einsum("scd,hd->sch", grad_y, weights[3], preferred_element_type=jnp.float32)
    next_coef = jnp.concatenate([decay_coef[:, 1:], jnp.ones_like(decay_coef[:, :1])], axis=1)
    prod_next, local_delta = lax.associative_scan(
        linked, (next_coef, grad_states), reverse=True, axis=1
    )
    summary = (decay_coef[:, 0] * prod_next[:, 0], decay_coef[:, 0] * local_delta[:, 0])
    identity = (jnp.ones_like(summary[0]), jnp.zeros_like(summary[1]))
    incoming = carried_in(summary, "seq", linked, identity, True)[1]
    delta = local_delta + prod_next * incoming[:, None, :]
    prev_states = jnp.concatenate([state_in[:, None, :], states[:, :-1]], axis=1)
    fnorm = forget_gate / gate_total
    inorm = input_gate / gate_total
    grad_a = delta * prev_states * carry_mask[:, :, None]
    grad_i = delta * candidate
    grad_forget = (
        (grad_a - grad_i) * inorm / gate_total * forget_gate * (1.0 - forget_gate)
    ).astype(jnp.bfloat16)
    grad_input = ((grad_i - grad_a) * fnorm / gate_total * input_gate * (1.0 - input_gate)).astype(
        jnp.bfloat16
    )
    grad_cand = (delta * inorm).astype(jnp.bfloat16)
    grad_wf = jnp.einsum("sch,scd->hd", grad_forget, gated_in, preferred_element_type=jnp.float32)
    grad_wi = jnp.einsum("sch,scd->hd", grad_input, gated_in, preferred_element_type=jnp.float32)
    grad_wc = jnp.einsum("sch,scd->hd", grad_cand, gated_in, preferred_element_type=jnp.float32)
    grad_bias_forget = jnp.sum(grad_forget, axis=(0, 1), dtype=jnp.float32)
    grad_bias_input = jnp.sum(grad_input, axis=(0, 1), dtype=jnp.float32)
    grad_gated = jnp.einsum(
        "sch,hd->scd", grad_forget, weights[0], preferred_element_type=jnp.float32
    )
    grad_gated = grad_gated + jnp.einsum(
        "sch,hd->scd", grad_input, weights[1], preferred_element_type=jnp.float32
    )
    grad_gated = grad_gated + jnp.einsum(
        "sch,hd->scd", grad_cand, weights[2], preferred_element_type=jnp.float32
    )
    unit_one = residual * scale_one
    grad_gain_one = jnp.sum(grad_gated * unit_one, axis=(0, 1))
    grad_unit_one = grad_gated * gain_one
    grad_resid = grad_middle + scale_one * (
        grad_unit_one - unit_one * jnp.mean(grad_unit_one * unit_one, axis=-1, keepdims=True)
    )
    vector_grad = jnp.concatenate([grad_gain_one, grad_gain_two, grad_bias_forget, grad_bias_input])
    return (grad_resid, [grad_wf, grad_wi, grad_wc, grad_wout, grad_up, grad_down], vector_grad)


def per_device(
    stream_in,
    out_grad,
    doc_lengths,
    mats,
    mat_momenta,
    mat_averages,
    vectors,
    vec_momenta,
    vec_averages,
):
    batch_count = lax.axis_size("batch")
    layer_count, single_block, shard_rows, model_width = mats.shape
    streams, span_len, feature_count = stream_in.shape
    hidden = H
    offsets = row_offsets(hidden // batch_count, FF // batch_count)
    block_rows = offsets[6]
    positions = lax.axis_index("seq") * span_len + jnp.arange(span_len, dtype=jnp.int32)
    doc_starts = jnp.cumsum(doc_lengths, axis=1) - doc_lengths
    carry_mask = 1.0 - jnp.any(positions[None, :, None] == doc_starts[:, None, :], axis=2).astype(
        jnp.float32
    )
    flat_low = mats.reshape(layer_count, shard_rows, model_width).astype(jnp.bfloat16)
    gathered = lax.all_gather(flat_low, ("batch", "seq"), axis=1, tiled=True).reshape(
        layer_count, batch_count, block_rows, model_width
    )
    layer_weights = [split_block(gathered, layer_idx, offsets) for layer_idx in range(layer_count)]
    residual = stream_in.astype(jnp.float32)
    stored = []
    for layer_idx in range(layer_count):
        weights = layer_weights[layer_idx]
        vector_row = vectors[layer_idx]
        front_parts = layer_front(residual, weights, vector_row, carry_mask, model_width, hidden)
        state_in = forward_carry(front_parts)
        rear_parts = layer_rear(residual, front_parts, state_in, weights, vector_row, model_width)
        stored.append((residual, front_parts, rear_parts, state_in))
        residual = rear_parts[7]
    activations = residual.astype(jnp.bfloat16)
    gathered_back = lax.all_gather(flat_low, ("batch", "seq"), axis=1, tiled=True).reshape(
        layer_count, batch_count, block_rows, model_width
    )
    back_weights = [
        split_block(gathered_back, layer_idx, offsets) for layer_idx in range(layer_count)
    ]
    grad_resid = out_grad.astype(jnp.float32)
    mat_grad_list = [None] * layer_count
    vector_rows = [None] * layer_count
    for layer_idx in reversed(range(layer_count)):
        weights = back_weights[layer_idx]
        vector_row = vectors[layer_idx]
        residual_in, front_parts, rear_parts, state_in = stored[layer_idx]
        grad_resid, mat_grad_list[layer_idx], vector_rows[layer_idx] = layer_back(
            grad_resid,
            residual_in,
            front_parts,
            rear_parts,
            state_in,
            weights,
            vector_row,
            carry_mask,
            model_width,
        )
    full_grads = pack_rows(mat_grad_list, batch_count)
    grad_shard = lax.psum_scatter(
        full_grads.reshape(layer_count, batch_count * block_rows, model_width),
        ("batch", "seq"),
        scatter_dimension=1,
        tiled=True,
    )
    vec_grads = lax.psum(jnp.stack(vector_rows), ("batch", "seq"))
    mom_shard = (
        MOMENTUM_DECAY * mat_momenta.reshape(layer_count, shard_rows, model_width) + grad_shard
    )
    mom_block = lax.all_gather(mom_shard.astype(jnp.bfloat16), "seq", axis=1, tiled=True).astype(
        mom_shard.dtype
    )
    pieces = [
        mom_block[layer_idx, offsets[member] : offsets[member + 1]]
        for layer_idx in range(layer_count)
        for member in range(6)
    ]
    local_squares = jnp.stack([jnp.sum(piece * piece) for piece in pieces])
    frob_norms = jnp.sqrt(lax.psum(local_squares, "batch"))
    iterates = [
        (piece / (frob_norms[number] + 1e-07)).astype(jnp.bfloat16)
        for number, piece in enumerate(pieces)
    ]
    for step_idx in range(NS_STEPS):
        partials = jnp.stack(
            [
                jnp.einsum("rd,re->de", iterate, iterate, preferred_element_type=jnp.float32)
                for iterate in iterates
            ]
        )
        gram_sums = lax.psum(partials.astype(jnp.bfloat16), "batch").astype(jnp.float32)
        gram_low = gram_sums.astype(jnp.bfloat16)
        polynomial = QUINTIC[1] * gram_sums + QUINTIC[2] * jnp.einsum(
            "nde,nef->ndf", gram_low, gram_low, preferred_element_type=jnp.float32
        )
        poly_low = polynomial.astype(jnp.bfloat16)
        iterates = [
            (
                QUINTIC[0] * iterate.astype(jnp.float32)
                + jnp.dot(iterate, poly_low[number], preferred_element_type=jnp.float32)
            ).astype(jnp.bfloat16)
            for number, iterate in enumerate(iterates)
        ]
    row_counts = [hidden, hidden, hidden, hidden, FF, FF]
    factors = [0.2 * math.sqrt(max(row_count, model_width)) for row_count in row_counts]
    ortho_block = jnp.stack(
        [
            jnp.concatenate(
                [
                    iterates[6 * layer_idx + member].astype(jnp.float32) * factors[member]
                    for member in range(6)
                ],
                axis=0,
            )
            for layer_idx in range(layer_count)
        ]
    )
    own_rows = lax.dynamic_slice_in_dim(
        ortho_block, lax.axis_index("seq") * shard_rows, shard_rows, axis=1
    )
    new_flat = mats.reshape(layer_count, shard_rows, model_width) - MATRIX_RATE * own_rows
    new_avg_flat = (
        AVERAGE_DECAY * mat_averages.reshape(layer_count, shard_rows, model_width)
        + (1.0 - AVERAGE_DECAY) * new_flat
    )
    new_vec_momenta = MOMENTUM_DECAY * vec_momenta + vec_grads
    new_vectors = vectors - vector_steps(new_vec_momenta, model_width, hidden)
    new_vec_averages = AVERAGE_DECAY * vec_averages + (1.0 - AVERAGE_DECAY) * new_vectors
    out_shape = (layer_count, 1, shard_rows, model_width)
    block_shape = (layer_count, 1, block_rows, model_width)
    return (
        activations,
        grad_resid,
        grad_shard.reshape(out_shape),
        mom_block.reshape(block_shape),
        new_flat.reshape(out_shape),
        new_avg_flat.reshape(out_shape),
        vec_grads,
        new_vec_momenta,
        new_vectors,
        new_vec_averages,
    )


def solution(mesh):
    placed = (
        P("batch", "seq", None),
        P("batch", "seq", None),
        P("batch", None),
        P(None, "batch", "seq", None),
        P(None, "batch", "seq", None),
        P(None, "batch", "seq", None),
        P(),
        P(),
        P(),
    )
    return jax.shard_map(
        per_device,
        mesh=mesh,
        in_specs=placed,
        out_specs=(
            P("batch", "seq", None),
            P("batch", "seq", None),
            P(None, "batch", "seq", None),
            P(None, "batch", None, None),
            P(None, "batch", "seq", None),
            P(None, "batch", "seq", None),
            P(),
            P(),
            P(),
            P(),
        ),
        check_vma=False,
    )
```

profile of v0, /device:TPU:26, one launch (start us, length us, event | category | flops | bytes accessed | tf_op | source)
XLA Modules:
  0.0 2278.3 jit_solution(214989154867584772)
XLA Ops:
  14.9 110.5 %all-gather.11.cloned.1.call-done = bf16[2,8192,512]{2,1,0:T(8,128)(2,1)} async-done(((bf16[2,256,512]{2,1,0:T(8,128)(2,1)}), bf16[2,8192,512]{2,1,0:T(8,128)(2,1)}) %all-gather.11.cloned.1.call-update) | async-done | bytes 16777232 | tf_op jit(solution)/shard_map/all_gather | solution.py:277
  234.8 29.6 %all-gather = f32[16,1,1024]{2,1,0:T(1,128)S(1)} all-gather(f32[2,1,1024]{2,1,0:T(1,128)S(1)} %slice_add_fusion.9), channel_id=2, replica_groups=mesh['seq'=8,'batch'=4] {'seq'}, dimensions={0}, use_global_device_ids=true | all-gather | bytes 73728 | tf_op jit(solution)/shard_map/all_gather | solution.py:23
  266.2 30.8 %all-gather.1 = f32[16,1,1024]{2,1,0:T(1,128)S(1)} all-gather(f32[2,1,1024]{2,1,0:T(1,128)S(1)} %slice_add_fusion.8), channel_id=3, replica_groups=mesh['seq'=8,'batch'=4] {'seq'}, dimensions={0}, use_global_device_ids=true | all-gather | bytes 73728 | tf_op jit(solution)/shard_map/all_gather | solution.py:23
  442.4 30.5 %all-gather.2 = f32[16,1,1024]{2,1,0:T(1,128)S(1)} all-gather(f32[2,1,1024]{2,1,0:T(1,128)S(1)} %slice_add_fusion.5), channel_id=4, replica_groups=mesh['seq'=8,'batch'=4] {'seq'}, dimensions={0}, use_global_device_ids=true | all-gather | bytes 73728 | tf_op jit(solution)/shard_map/all_gather | solution.py:23
  474.6 31.0 %all-gather.3 = f32[16,1,1024]{2,1,0:T(1,128)S(1)} all-gather(f32[2,1,1024]{2,1,0:T(1,128)S(1)} %slice_add_fusion.4), channel_id=5, replica_groups=mesh['seq'=8,'batch'=4] {'seq'}, dimensions={0}, use_global_device_ids=true | all-gather | bytes 73728 | tf_op jit(solution)/shard_map/all_gather | solution.py:23
  743.5 8.9 rev.16
  752.3 8.9 rev.17
  761.2 30.5 %all-gather.4 = f32[16,1,1024]{2,1,0:T(1,128)S(1)} all-gather(f32[2,1,1024]{2,1,0:T(1,128)S(1)} %get-tuple-element.669), channel_id=6, replica_groups=mesh['seq'=8,'batch'=4] {'seq'}, dimensions={0}, use_global_device_ids=true | all-gather | bytes 73728 | tf_op jit(solution)/shard_map/all_gather | solution.py:23
  792.5 30.9 %all-gather.5 = f32[16,1,1024]{2,1,0:T(1,128)S(1)} all-gather(f32[2,1,1024]{2,1,0:T(1,128)} %get-tuple-element.668), channel_id=7, replica_groups=mesh['seq'=8,'batch'=4] {'seq'}, dimensions={0}, use_global_device_ids=true | all-gather | bytes 73728 | tf_op jit(solution)/shard_map/all_gather | solution.py:23
  1020.1 30.6 %all-gather.6 = f32[16,1,1024]{2,1,0:T(1,128)S(1)} all-gather(f32[2,1,1024]{2,1,0:T(1,128)S(1)} %get-tuple-element.667), channel_id=8, replica_groups=mesh['seq'=8,'batch'=4] {'seq'}, dimensions={0}, use_global_device_ids=true | all-gather | bytes 73728 | tf_op jit(solution)/shard_map/all_gather | solution.py:23
  1051.6 30.7 %all-gather.7 = f32[16,1,1024]{2,1,0:T(1,128)S(1)} all-gather(f32[2,1,1024]{2,1,0:T(1,128)} %get-tuple-element.666), channel_id=9, replica_groups=mesh['seq'=8,'batch'=4] {'seq'}, dimensions={0}, use_global_device_ids=true | all-gather | bytes 73728 | tf_op jit(solution)/shard_map/all_gather | solution.py:23
  1082.5 6.3 while.63
  1098.2 6.6 copy-done.5
  1121.5 11.7 pad_maximum_fusion
  1133.3 706.9 %reduce-scatter.2.cloned.1.call-done = f32[2,256,512]{2,1,0:T(8,128)} async-done(((f32[2,8192,512]{2,1,0:T(8,128)}), f32[2,256,512]{2,1,0:T(8,128)}) %reduce-scatter.2.cloned.1.call-update) | async-done | bytes 1048592 | tf_op jit(solution)/shard_map/reduce_scatter | solution.py:317
  1842.5 72.1 %all-gather.13.cloned.1.call-done = bf16[2,2048,512]{2,1,0:T(8,128)(2,1)} async-done(((bf16[2,256,512]{2,1,0:T(8,128)(2,1)}), bf16[2,2048,512]{2,1,0:T(8,128)(2,1)}) %all-gather.13.cloned.1.call-update) | async-done | bytes 4194320 | tf_op jit(solution)/shard_map/all_gather | solution.py:327
  1914.6 7.9 fusion.254
  1926.9 7.5 stack.185
  1934.4 17.8 psum.28
  1985.1 41.5 %psum.31 = f32[2,3072]{1,0:T(2,128)S(1)} all-reduce(f32[2,3072]{1,0:T(2,128)S(1)} %pad_maximum_fusion.39), channel_id=1, replica_groups=mesh['seq'=8,'batch'=4] {'batch','seq'}, use_global_device_ids=true, to_apply=%region_42.43 | all-reduce | flops 6144 | bytes 49152 | tf_op jit(solution)/shard_map/psum | solution.py:323
  2026.7 74.0 %all-reduce.119.cloned.1.call-done = bf16[12,512,512]{2,1,0:T(8,128)(2,1)} async-done(((bf16[12,512,512]{2,1,0:T(8,128)(2,1)}), bf16[12,512,512]{2,1,0:T(8,128)(2,1)}) %all-reduce.119.cloned.1.call-update) | async-done | bytes 6291472 | tf_op jit(solution)/shard_map/psum | solution.py:348
  2100.7 10.0 add_convert_fusion.1
  2141.2 113.6 %all-reduce.121.cloned.1.call-done = bf16[12,512,512]{2,1,0:T(8,128)(2,1)} async-done(((bf16[12,512,512]{2,1,0:T(8,128)(2,1)}), bf16[12,512,512]{2,1,0:T(8,128)(2,1)}) %all-reduce.121.cloned.1.call-update) | async-done | bytes 6291472 | tf_op jit(solution)/shard_map/psum | solution.py:348
  2254.7 10.5 add_convert_fusion
  (1027 shorter events, 816.8 us)
Async XLA Ops:
  7.2 118.3 %all-gather.11.cloned.1.call-start = ((), (), s32[]{:S(2)}) async-start(), calls=%async_computation.1 | async-start | bytes 17301504 | tf_op jit(solution)/shard_map/all_gather | solution.py:277
  9.3 1830.8 %reduce-scatter.2.cloned.1.call-start = ((), (), s32[]{:S(2)}) async-start(), calls=%async_computation.2 | async-start | bytes 34603008 | tf_op jit(solution)/shard_map/reduce_scatter | solution.py:317
  12.2 119.9 %copy-start.114 = (f32[2,128]{1,0:T(2,128)}, f32[2,128]{1,0:T(2,128)S(1)}, u32[]{:S(2)}) copy-start(f32[2,128]{1,0:T(2,128)S(1)} %get-tuple-element.827) | copy-start | bytes 3076
  12.2 119.9 %copy-start.139 = (f32[2,128]{1,0:T(2,128)}, f32[2,128]{1,0:T(2,128)S(1)}, u32[]{:S(2)}) copy-start(f32[2,128]{1,0:T(2,128)S(1)} %get-tuple-element.826) | copy-start | bytes 3076
  13.6 118.5 %copy-start.108 = (f32[1,512]{1,0:T(1,128)}, f32[1,512]{1,0:T(1,128)S(1)}, u32[]{:S(2)}) copy-start(f32[1,512]{1,0:T(1,128)S(1)} %get-tuple-element.773) | copy-start | bytes 6148
  134.1 70.7 %copy-start.39 = (f32[2,128,1024]{2,1,0:T(8,128)}, f32[2,128,1024]{2,1,0:T(8,128)S(1)}, u32[]{:S(2)}) copy-start(f32[2,128,1024]{2,1,0:T(8,128)S(1)} %get-tuple-element.665) | copy-start | bytes 3145732
  226.6 76.5 %copy-start.57 = (f32[2,128,1024]{2,1,0:T(8,128)}, f32[2,128,1024]{2,1,0:T(8,128)S(1)}, u32[]{:S(2)}) copy-start(f32[2,128,1024]{2,1,0:T(8,128)S(1)} %pad.375) | copy-start | bytes 3145732
  430.7 81.1 %copy-start.56 = (f32[2,128,1024]{2,1,0:T(8,128)}, f32[2,128,1024]{2,1,0:T(8,128)S(1)}, u32[]{:S(2)}) copy-start(f32[2,128,1024]{2,1,0:T(8,128)S(1)} %pad.402) | copy-start | bytes 3145732
  730.3 93.3 %copy-start.100 = (f32[2,1024]{1,0:T(2,128)S(1)}, f32[2,1024]{1,0:T(2,128)}, u32[]{:S(2)}) copy-start(f32[2,1024]{1,0:T(2,128)} %custom-call.2) | copy-start | bytes 24580
  732.5 97.1 %copy-start.111 = (f32[2,1,1024]{2,1,0:T(1,128)S(1)}, f32[2,1,1024]{2,1,0:T(1,128)}, u32[]{:S(2)}) copy-start(f32[2,1,1024]{2,1,0:T(1,128)} %broadcast_in_dim.4) | copy-start | bytes 24580
  862.5 62.0 %copy-start.41 = (f32[2,128,1024]{2,1,0:T(8,128)S(1)}, f32[2,128,1024]{2,1,0:T(8,128)}, u32[]{:S(2)}) copy-start(f32[2,128,1024]{2,1,0:T(8,128)} %fusion.202) | copy-start | bytes 3145732
  1011.3 71.2 %copy-start.99 = (f32[2,1024]{1,0:T(2,128)S(1)}, f32[2,1024]{1,0:T(2,128)}, u32[]{:S(2)}) copy-start(f32[2,1024]{1,0:T(2,128)} %custom-call.3) | copy-start | bytes 24580
  1011.3 77.5 %copy-start.110 = (f32[2,1,1024]{2,1,0:T(1,128)S(1)}, f32[2,1,1024]{2,1,0:T(1,128)}, u32[]{:S(2)}) copy-start(f32[2,1,1024]{2,1,0:T(1,128)} %broadcast_in_dim.5) | copy-start | bytes 24580
  1020.1 72.0 %copy-start.72 = (f32[2,128,1024]{2,1,0:T(8,128)S(1)}, f32[2,128,1024]{2,1,0:T(8,128)}, u32[]{:S(2)}) copy-start(f32[2,128,1024]{2,1,0:T(8,128)} %copy-done.71) | copy-start | bytes 3145732
  1133.2 706.9 %copy-start.93 = (f32[2,1,256,512]{3,2,1,0:T(8,128)S(1)}, f32[2,1,256,512]{3,2,1,0:T(8,128)}, u32[]{:S(2)}) copy-start(f32[2,1,256,512]{3,2,1,0:T(8,128)} %param.21) | copy-start | bytes 3145732
  1133.2 781.3 %all-gather.13.cloned.1.call-start = ((), (), s32[]{:S(2)}) async-start(), calls=%async_computation.3 | async-start | bytes 4718592 | tf_op jit(solution)/shard_map/all_gather | solution.py:327
  1842.4 258.2 %all-reduce.119.cloned.1.call-start = ((), (), s32[]{:S(2)}) async-start(), calls=%async_computation.4 | async-start | bytes 12582912 | tf_op jit(solution)/shard_map/psum | solution.py:348
  1980.2 274.5 %all-reduce.121.cloned.1.call-start = ((), (), s32[]{:S(2)}) async-start(), calls=%async_computation.5 | async-start | bytes 12582912 | tf_op jit(solution)/shard_map/psum | solution.py:348
  2026.6 84.1 %copy-start.106 = (f32[2,3072]{1,0:T(2,128)}, f32[2,3072]{1,0:T(2,128)S(1)}, u32[]{:S(2)}) copy-start(f32[2,3072]{1,0:T(2,128)S(1)} %psum.31) | copy-start | bytes 73732
  2026.7 108.6 %copy-start.103 = (f32[2,3072]{1,0:T(2,128)}, f32[2,3072]{1,0:T(2,128)S(1)}, u32[]{:S(2)}) copy-start(f32[2,3072]{1,0:T(2,128)S(1)} %multiply_add_fusion.28) | copy-start | bytes 73732
  2141.1 124.1 %copy-start.166 = (bf16[256,512]{1,0:T(8,128)(2,1)S(1)}, bf16[256,512]{1,0:T(8,128)(2,1)}, u32[]{:S(2)}) copy-start(bf16[256,512]{1,0:T(8,128)(2,1)} %copy-done.165) | copy-start | bytes 786436
  2141.2 124.5 %copy-start.174 = (bf16[256,512]{1,0:T(8,128)(2,1)S(1)}, bf16[256,512]{1,0:T(8,128)(2,1)}, u32[]{:S(2)}) copy-start(bf16[256,512]{1,0:T(8,128)(2,1)} %copy-done.173) | copy-start | bytes 786436
  2141.2 124.8 %copy-start.172 = (bf16[256,512]{1,0:T(8,128)(2,1)S(1)}, bf16[256,512]{1,0:T(8,128)(2,1)}, u32[]{:S(2)}) copy-start(bf16[256,512]{1,0:T(8,128)(2,1)} %copy-done.171) | copy-start | bytes 786436
  2141.2 125.2 %copy-start.170 = (bf16[256,512]{1,0:T(8,128)(2,1)S(1)}, bf16[256,512]{1,0:T(8,128)(2,1)}, u32[]{:S(2)}) copy-start(bf16[256,512]{1,0:T(8,128)(2,1)} %copy-done.169) | copy-start | bytes 786436
  (166 other events, 933.7 us)
Sparse Core Ops, SparseCore 0:
  11.6 113.7 all-gather.10
  1133.3 706.7 reduce-scatter.1
  1842.9 71.6 all-gather.12
  1980.3 120.3 all-reduce.118
  2134.9 119.7 all-reduce.120
where the time goes:
time: 2300 us; the launch traced here: 2280 us
  waiting for transfers between devices  1080 us (47%)
  local copies, waits for them, and re-layouts  506 us (22%)
  blocking collectives  304 us (13%)
  other arithmetic  239 us (10%)
  matrix products  126 us (5%)
  between operations  25.2 us (1%)
    reduce_scatter x1, waiting for transfers between devices, per_device(): lax.psum_scatter(full_grads.reshape(layer_count, batch_count * block_rows...  707 us
    all_gather x8, blocking collectives, carried_in(): everything = jax.tree.map(lambda part: lax.all_gather(part, axis), x)  245 us
    slice x98, local copies, waits for them, and re-layouts, layer_back(): lax.associative_scan(linked, (next_coef, grad_states), reverse=True, axis=1)  191 us
    psum x2, waiting for transfers between devices, per_device(): lax.psum(partials.astype(jnp.bfloat16), 'batch').astype(jnp.float32)  188 us
    slice x88, local copies, waits for them, and re-layouts, layer_front(): lax.associative_scan(linked, (decay_coef, input_term), axis=1)  127 us
    all_gather x1, waiting for transfers between devices, per_device(): lax.all_gather(flat_low, ('batch', 'seq'), axis=1, tiled=True)  111 us
    all_gather x1, waiting for transfers between devices, per_device(): lax.all_gather(mom_shard.astype(jnp.bfloat16), 'seq', axis=1, tiled=True)  72.1 us
    pad x48, local copies, waits for them, and re-layouts, layer_back(): lax.associative_scan(linked, (next_coef, grad_states), reverse=True, axis=1)  66.8 us
  transfers between devices with their start and end apart: 5, of which 5 were waited for; matrix products, arithmetic and copies ran while one was open for 1% of the time, Pallas kernels for 0%

commit v1 on v0

v1 whole, which is shorter than its diff:
```python
import functools
import math

import jax
import jax.numpy as jnp
from jax import lax
from jax.experimental import pallas as pl
from jax.experimental.pallas import tpu as pltpu
from jax.sharding import PartitionSpec as P

H = 1024
FF = 2048
NS_STEPS = 2
MESH = pl.DeviceIdType.MESH
F32 = jnp.float32
BF16 = jnp.bfloat16

EPSILON = 1e-05
MOMENTUM_DECAY = 0.5
AVERAGE_DECAY = 0.9
MATRIX_RATE = 0.3
SEGMENT_RATES = (0.3, 0.3, 0.5, 2.0)
QUINTIC = (3.4445, -4.775, 2.0315)
GELU_A = 0.7978845608
GELU_B = 0.044715


class Geometry:
    def __init__(self, n_seq, n_batch):
        self.n_seq, self.n_batch = n_seq, n_batch
        self.nz, self.ny, self.stride_z, self.stride_y = {
            8: (4, 2, 2, 1),
            32: (8, 4, 1, 8),
        }.get(n_seq, (n_seq, 1, 1, n_seq))
        self.nx = n_batch // 2
        self.swaps = self.ny == self.nx
        self.nu, self.nv = self.ny, self.nx

    def seq_of(self, z, y):
        return z * self.stride_z + y * self.stride_y

    def here(self):
        seq, batch = lax.axis_index("seq"), lax.axis_index("batch")
        z = seq // self.stride_z % self.nz
        y = seq // self.stride_y % self.ny
        return seq, batch, z, y, batch // 2, batch % 2

    def to_yx(self, u, v, core):
        if not self.swaps:
            return u, v
        return u + core * (v - u), v + core * (u - v)


def dot_nn(a, b):
    return lax.dot_general(a, b, (((1,), (0,)), ((), ())), preferred_element_type=F32)


def dot_nt(a, b):
    return lax.dot_general(a, b, (((1,), (1,)), ((), ())), preferred_element_type=F32)


def dot_tn(a, b):
    return lax.dot_general(a, b, (((0,), (0,)), ((), ())), preferred_element_type=F32)


def other(mine, step, count):
    return lax.rem(mine + step, count)


def enter(geo):
    seq, batch, z, y, x, core = geo.here()
    barrier = pltpu.get_barrier_semaphore()

    def greet(seq_id, batch_id):
        pl.semaphore_signal(barrier, inc=1, device_id=(seq_id, batch_id), device_id_type=MESH)

    for step in range(1, geo.n_seq):
        greet(other(seq, step, geo.n_seq), batch)
    for step in range(1, geo.nx):
        greet(seq, other(x, step, geo.nx) * 2 + core)
    greet(seq, x * 2 + 1 - core)
    pl.semaphore_wait(barrier, geo.n_seq - 1 + geo.nx - 1 + 1)


class Gather:
    def __init__(self, geo, weights, rows, send_z, send_u, send_v, send_s, recv, recv_s):
        self.geo, self.weights, self.rows = geo, weights, rows
        self.sems = (send_z, send_u, send_v, send_s, recv, recv_s)
        self.seq, self.batch, self.z, self.y, self.x, self.core = geo.here()
        if geo.swaps:
            self.u = self.y + self.core * (self.x - self.y)
            self.v = self.x + self.core * (self.y - self.x)
        else:
            self.u, self.v = self.y, self.x

    def slot(self, layer, z, u, v):
        y, x = self.geo.to_yx(u, v, self.core)
        start = pl.multiple_of(self.geo.seq_of(z, y) * self.rows, self.rows)
        return self.weights.at[layer, x * 2 + self.core, pl.ds(start, self.rows)]

    def number(self, layer, z, u, v):
        return ((layer * self.geo.nz + z) * self.geo.nu + u) * self.geo.nv + v

    def device(self, z, u, v, core):
        y, x = self.geo.to_yx(u, v, self.core)
        return (self.geo.seq_of(z, y), x * 2 + core)

    def copy(self, layer, z, u, v, device, send, recv):
        part = self.slot(layer, z, u, v)
        return pltpu.make_async_remote_copy(
            src_ref=part, dst_ref=part, send_sem=send, recv_sem=recv, device_id=device, device_id_type=MESH
        )

    def arrived(self, layer, z, u, v):
        recv = self.sems[4]
        self.copy(
            layer, z, u, v, self.device(self.z, self.u, self.v, 1 - self.core),
            self.sems[3].at[layer], recv.at[self.number(layer, z, u, v)],
        ).wait_recv()

    def to_z(self, layer):
        geo = self.geo
        for step in range(1, geo.nz):
            self.copy(
                layer, self.z, self.u, self.v,
                self.device(other(self.z, step, geo.nz), self.u, self.v, self.core),
                self.sems[0].at[layer, step - 1], self.sems[4].at[self.number(layer, self.z, self.u, self.v)],
            ).start()

    def to_u(self, layer, z):
        geo = self.geo
        for step in range(1, geo.nu):
            self.copy(
                layer, z, self.u, self.v,
                self.device(self.z, other(self.u, step, geo.nu), self.v, self.core),
                self.sems[1].at[layer, step - 1], self.sems[4].at[self.number(layer, z, self.u, self.v)],
            ).start()

    def to_v(self, layer, z, u):
        geo = self.geo
        for step in range(1, geo.nv):
            self.copy(
                layer, z, u, self.v,
                self.device(self.z, self.u, other(self.v, step, geo.nv), self.core),
                self.sems[2].at[layer, step - 1], self.sems[4].at[self.number(layer, z, u, self.v)],
            ).start()

    def to_sibling(self, layer, z, u, v):
        self.copy(
            layer, z, u, v, self.device(self.z, self.u, self.v, 1 - self.core),
            self.sems[3].at[layer], self.sems[5].at[layer],
        ).start()

    def begin(self, layer):
        self.to_z(layer)
        self.to_u(layer, self.z)
        self.to_v(layer, self.z, self.u)
        self.to_sibling(layer, self.z, self.u, self.v)

    def column(self, layer, step):
        z = lax.rem(self.z - step + self.geo.nz, self.geo.nz)
        self.arrived(layer, z, self.u, self.v)
        self.to_u(layer, z)
        self.to_v(layer, z, self.u)
        self.to_sibling(layer, z, self.u, self.v)

    def plane(self, layer, step):
        z = lax.rem(self.z - step + self.geo.nz, self.geo.nz)

        def one(k, _):
            u = other(self.u, k, self.geo.nu)
            self.arrived(layer, z, u, self.v)
            self.to_v(layer, z, u)
            self.to_sibling(layer, z, u, self.v)
            return 0

        lax.fori_loop(1, self.geo.nu, one, 0)

    def whole(self, layer, step_u, step_z):
        z = lax.rem(self.z - step_z + self.geo.nz, self.geo.nz)
        u = other(self.u, step_u, self.geo.nu)

        def one(k, _):
            v = other(self.v, k, self.geo.nv)
            self.arrived(layer, z, u, v)
            self.to_sibling(layer, z, u, v)
            return 0

        lax.fori_loop(1, self.geo.nv, one, 0)

    def finish(self, layer):
        geo = self.geo
        send_z, send_u, send_v, send_s, recv, recv_s = self.sems
        away = self.device(self.z, self.u, self.v, 1 - self.core)

        def drain(part, sem):
            pltpu.make_async_remote_copy(
                src_ref=part, dst_ref=part, send_sem=sem, recv_sem=recv_s.at[layer], device_id=away,
                device_id_type=MESH,
            ).wait_send()

        for step in range(1, geo.nz):
            drain(self.slot(layer, self.z, self.u, self.v), send_z.at[layer, step - 1])
        for step in range(1, geo.nu):
            drain(self.weights.at[layer, 0, pl.ds(0, geo.nz * self.rows)], send_u.at[layer, step - 1])
        for step in range(1, geo.nv):
            drain(self.weights.at[layer, 0, pl.ds(0, geo.nz * geo.nu * self.rows)], send_v.at[layer, step - 1])
        family = self.weights.at[layer, pl.ds(0, geo.nx)]
        drain(family, send_s.at[layer])
        pltpu.make_async_remote_copy(
            src_ref=family, dst_ref=family, send_sem=send_s.at[layer], recv_sem=recv_s.at[layer], device_id=away,
            device_id_type=MESH,
        ).wait_recv()

    def run(self, layer):
        geo = self.geo
        self.begin(layer)
        for step in range(1, geo.nz):
            self.column(layer, step)
            self.plane(layer, step - 1)
        self.plane(layer, geo.nz - 1)

        def one(k, _):
            self.whole(layer, k // geo.nz, k % geo.nz)
            return 0

        lax.fori_loop(0, geo.nu * geo.nz, one, 0)
        self.finish(layer)


def sigmoid(values):
    return 1.0 / (1.0 + jnp.exp(-values))


def widen(column_tile, width):
    return jnp.concatenate([column_tile] * (width // 128), axis=1)


def network_scratch(geo, sizes):
    layers, streams, span, width, hid, ffn, rows, docs = sizes
    tokens, nb = streams * span, geo.n_batch
    block = 4 * hid + 2 * ffn

    def full(dtype, *shape):
        return pltpu.VMEM(shape, dtype)

    dma = pltpu.SemaphoreType.DMA
    return [
        full(BF16, layers, nb, block, width),
        full(F32, layers + 1, tokens, width),
        full(BF16, layers, tokens, width),
        full(F32, layers, nb, tokens, hid),
        full(F32, layers, nb, tokens, hid),
        full(F32, layers, nb, tokens, hid),
        full(F32, layers, nb, tokens, hid),
        full(F32, layers, tokens, width),
        full(BF16, layers, tokens, width),
        full(F32, layers, nb, tokens, ffn),
        full(F32, layers, nb, 8, hid),
        full(F32, nb, tokens, hid),
        full(F32, tokens, 128),
        full(F32, 2 * layers, nb, 8, hid),
        full(F32, 2 * layers, geo.n_seq, nb, 8, hid),
        full(F32, tokens, width),
        full(BF16, tokens, width),
        full(F32, tokens, width),
        full(F32, tokens, hid),
        full(F32, tokens, hid),
        full(F32, nb, tokens, hid),
        full(F32, nb, tokens, hid),
        full(F32, nb, 8, hid),
        full(BF16, tokens, hid),
        full(BF16, tokens, hid),
        full(BF16, tokens, hid),
        full(F32, tokens, ffn),
        full(BF16, tokens, ffn),
        full(BF16, tokens, ffn),
        full(BF16, nb, block, width),
        full(F32, layers, 2, width),
        full(F32, layers, nb, 2, hid),
        full(F32, layers, 2, width),
        full(F32, layers, nb, 2, hid),
        dma((layers, max(geo.nz - 1, 1))),
        dma((layers, max(geo.nu - 1, 1))),
        dma((layers, max(geo.nv - 1, 1))),
        dma((layers,)),
        dma((layers * geo.nz * geo.nu * geo.nv,)),
        dma((layers,)),
        dma((2 * layers, geo.n_seq)),
        dma((2 * layers, geo.n_seq)),
        dma((1,)),
    ]


def network_kernel(
    geo, sizes, mats_ref, x_ref, out_grad_ref, doc_ref, vec_ref, act_ref, dx_ref, grads_ref, vgrad_ref, *scratch
):
    (
        weights, resid, gated, fgate, igate, cand, states, middle, normed, inner, carry_in, prods, mask, summary,
        mailbox, dgrad, low_grad, acc, tmp1, tmp2, gstates, deltas, incoming, low1, low2, low3, wide, wide_low1,
        wide_low2, gstage, gains, biases, ggains, gbiases, send_z, send_u, send_v, send_s, recv, recv_s, mail_send, mail_recv, out_sem,
    ) = scratch
    layers, streams, span, width, hid, ffn, rows, docs = sizes
    tokens = streams * span
    nb = geo.n_batch
    seq, batch, z, y, x, core = geo.here()
    hid_all, tile = hid * nb, 32

    def each_tile(body):
        lax.fori_loop(0, tokens // tile, lambda k, _: body(pl.ds(pl.multiple_of(k * tile, tile), tile)) or 0, 0)

    def each_block(body):
        lax.fori_loop(0, nb, lambda b, _: body(b) or 0, 0)

    for layer in range(layers):
        weights[layer, batch, pl.ds(pl.multiple_of(seq * rows, rows), rows), :] = mats_ref[layer, 0].astype(BF16)
    enter(geo)
    gather = Gather(geo, weights, rows, send_z, send_u, send_v, send_s, recv, recv_s)
    for layer in range(layers):
        gather.run(layer)

    def each_piece(body):
        for layer in range(layers):
            for k in range(2):
                body(slice(layer, layer + 1), slice(k * width, (k + 1) * width), k, gains, ggains, (layer,))
                for b in range(nb):
                    first = 2 * width + k * hid_all + b * hid
                    body(slice(layer, layer + 1), slice(first, first + hid), k, biases, gbiases, (layer, b))

    def read_piece(row, columns, k, kept, made, at):
        kept[(*at, slice(k, k + 1), slice(None))] = vec_ref[row, columns]

    def write_piece(row, columns, k, kept, made, at):
        vgrad_ref[row, columns] = made[(*at, slice(k, k + 1), slice(None))]

    each_piece(read_piece)

    for stream in range(streams):
        position = seq * span + lax.broadcasted_iota(jnp.int32, (span, 128), 0)
        begin, keep = jnp.int32(0), jnp.ones((span, 128), F32)
        for doc in range(docs):
            keep = jnp.where(position == begin, 0.0, keep)
            begin = begin + doc_ref[stream, doc]
        mask[stream * span : (stream + 1) * span, :] = keep

    def load_input(at):
        flat = x_ref[at, :].astype(F32)
        resid[0, at, :] = flat

    each_tile(load_input)

    def mail(number, forward):
        first, last = (seq + 1, geo.n_seq) if forward else (0, seq)

        def copy(peer, source):
            return pltpu.make_async_remote_copy(
                src_ref=summary.at[number], dst_ref=mailbox.at[number, source],
                send_sem=mail_send.at[number, peer], recv_sem=mail_recv.at[number, source],
                device_id=(peer, batch), device_id_type=MESH,
            )

        def start(peer, _):
            copy(peer, seq).start()
            return 0

        lax.fori_loop(first, last, start, 0)
        hops = seq if forward else geo.n_seq - 1 - seq

        def fold(k, before):
            source = k if forward else geo.n_seq - 1 - k
            copy(source, source).wait_recv()
            packed = mailbox[number, source]
            return packed[:, 2 : 2 + streams] + packed[:, 0:streams] * before

        total = lax.fori_loop(0, hops, fold, jnp.zeros((nb, streams, hid), F32))

        def finish(peer, _):
            copy(peer, seq).wait_send()
            return 0

        lax.fori_loop(first, last, finish, 0)
        return total

    groups = span // 8
    row8 = lax.broadcasted_iota(jnp.int32, (8, hid), 0)

    def forward(layer):
        gain_one = gains[layer, 0:1, :]
        gain_two = gains[layer, 1:2, :]

        def norm_one(at):
            values = resid[layer, at, :]
            scale = lax.rsqrt(jnp.mean(values * values, axis=-1, keepdims=True) + EPSILON)
            gated[layer, at, :] = (values * scale * gain_one).astype(BF16)

        each_tile(norm_one)

        def front(b):
            shift_f = biases[layer, b, 0:1, :]
            shift_i = biases[layer, b, 1:2, :]
            source = gated[layer]
            tmp1[...] = dot_nt(source, weights[layer, b, 0:hid, :]) + shift_f
            tmp2[...] = dot_nt(source, weights[layer, b, hid : 2 * hid, :]) + shift_i
            cand[layer, b] = dot_nt(source, weights[layer, b, 2 * hid : 3 * hid, :])

            def group(k, carried):
                new = []
                for stream in range(streams):
                    at = pl.ds(pl.multiple_of(stream * span + k * 8, 8), 8)
                    f, i = sigmoid(tmp1[at, :]), sigmoid(tmp2[at, :])
                    share = 1.0 / (f + i)
                    decay = f * share * widen(mask[at, :], hid)
                    term = i * share * cand[layer, b, at, :]
                    fgate[layer, b, at, :] = f
                    igate[layer, b, at, :] = i
                    for step in (1, 2, 4):
                        reach = row8 >= step
                        term = term + decay * jnp.where(reach, pltpu.roll(term, step, 0), 0.0)
                        decay = decay * jnp.where(reach, pltpu.roll(decay, step, 0), 1.0)
                    prod_in, state_in = carried[stream]
                    term = term + decay * state_in
                    decay = decay * prod_in
                    states[layer, b, at, :] = term
                    prods[b, at, :] = decay
                    new.append((decay[7:8], term[7:8]))
                return tuple(new)

            start = tuple((jnp.ones((1, hid), F32), jnp.zeros((1, hid), F32)) for _ in range(streams))
            last = lax.fori_loop(0, groups, group, start)
            for stream in range(streams):
                summary[layer, b, stream : stream + 1, :] = last[stream][0]
                summary[layer, b, 2 + stream : 3 + stream, :] = last[stream][1]

        each_block(front)
        carry_in[layer, :, 0:streams, :] = mail(layer, True)
        acc[...] = jnp.zeros_like(acc)

        def rear(b):
            for stream in range(streams):
                at = slice(stream * span, (stream + 1) * span)
                full = states[layer, b, at, :] + prods[b, at, :] * carry_in[layer, b, stream : stream + 1, :]
                states[layer, b, at, :] = full
                low1[at, :] = full.astype(BF16)
            acc[...] += dot_nn(low1[...], weights[layer, b, 3 * hid : 4 * hid, :])

        each_block(rear)

        def norm_two(at):
            values = resid[layer, at, :] + acc[at, :]
            middle[layer, at, :] = values
            scale = lax.rsqrt(jnp.mean(values * values, axis=-1, keepdims=True) + EPSILON)
            normed[layer, at, :] = (values * scale * gain_two).astype(BF16)

        each_tile(norm_two)
        acc[...] = middle[layer]

        def mlp(b):
            inner[layer, b] = dot_nt(normed[layer], weights[layer, b, 4 * hid : 4 * hid + ffn, :])

            def act(at):
                v = inner[layer, b, at, :]
                t = jnp.tanh(GELU_A * (v + GELU_B * (v * v * v)))
                wide_low1[at, :] = (0.5 * v * (1.0 + t)).astype(BF16)

            each_tile(act)
            acc[...] += dot_nn(wide_low1[...], weights[layer, b, 4 * hid + ffn : 4 * hid + 2 * ffn, :])

        each_block(mlp)
        resid[layer + 1] = acc[...]

    def put_grad(layer, b, first, count, value):
        gstage[b, pl.ds(first, count), :] = value.astype(BF16)

    def backward(layer):
        gain_one = gains[layer, 0:1, :]
        gain_two = gains[layer, 1:2, :]
        low_grad[...] = dgrad[...].astype(BF16)
        acc[...] = jnp.zeros_like(acc)

        def mlp(b):
            wide[...] = dot_nt(low_grad[...], weights[layer, b, 4 * hid + ffn : 4 * hid + 2 * ffn, :])

            def act(at):
                v = inner[layer, b, at, :]
                square = v * v
                t = jnp.tanh(GELU_A * (v + GELU_B * (v * square)))
                half = 0.5 * (1.0 + t)
                wide_low1[at, :] = (v * half).astype(BF16)
                slope = half + 0.5 * v * (1.0 - t * t) * (GELU_A * (1.0 + 3.0 * GELU_B * square))
                wide_low2[at, :] = (wide[at, :] * slope).astype(BF16)

            each_tile(act)
            put_grad(layer, b, 4 * hid + ffn, ffn, dot_tn(wide_low1[...], low_grad[...]))
            put_grad(layer, b, 4 * hid, ffn, dot_tn(wide_low2[...], normed[layer]))
            acc[...] += dot_nn(wide_low2[...], weights[layer, b, 4 * hid : 4 * hid + ffn, :])

        each_block(mlp)
        row_sum = jnp.zeros((1, width), F32)

        def norm_two(k, total):
            at = pl.ds(pl.multiple_of(k * tile, tile), tile)
            values, grad = middle[layer, at, :], acc[at, :]
            scale = lax.rsqrt(jnp.mean(values * values, axis=-1, keepdims=True) + EPSILON)
            unit = values * scale
            gunit = grad * gain_two
            full = dgrad[at, :] + scale * (gunit - unit * jnp.mean(gunit * unit, axis=-1, keepdims=True))
            dgrad[at, :] = full
            low_grad[at, :] = full.astype(BF16)
            return total + jnp.sum(grad * unit, axis=0, keepdims=True)

        ggains[layer, 1:2, :] = lax.fori_loop(0, tokens // tile, norm_two, row_sum)
        number = layers + layer

        def front(b):
            low1[...] = states[layer, b].astype(BF16)
            put_grad(layer, b, 3 * hid, hid, dot_tn(low1[...], low_grad[...]))
            gstates[b] = dot_nt(low_grad[...], weights[layer, b, 3 * hid : 4 * hid, :])

            def group(k, carried):
                new = []
                for stream in range(streams):
                    at = pl.ds(pl.multiple_of(stream * span + (groups - 1 - k) * 8, 8), 8)
                    f, i = fgate[layer, b, at, :], igate[layer, b, at, :]
                    decay = f * (1.0 / (f + i)) * widen(mask[at, :], hid)
                    term = decay * gstates[b, at, :]
                    for step in (1, 2, 4):
                        reach = row8 < 8 - step
                        term = term + decay * jnp.where(reach, pltpu.roll(term, 8 - step, 0), 0.0)
                        decay = decay * jnp.where(reach, pltpu.roll(decay, 8 - step, 0), 1.0)
                    prod_in, state_in = carried[stream]
                    term = term + decay * state_in
                    decay = decay * prod_in
                    deltas[b, at, :] = term
                    prods[b, at, :] = decay
                    new.append((decay[0:1], term[0:1]))
                return tuple(new)

            start = tuple((jnp.ones((1, hid), F32), jnp.zeros((1, hid), F32)) for _ in range(streams))
            last = lax.fori_loop(0, groups, group, start)
            for stream in range(streams):
                summary[number, b, stream : stream + 1, :] = last[stream][0]
                summary[number, b, 2 + stream : 3 + stream, :] = last[stream][1]

        each_block(front)
        incoming[:, 0:streams, :] = mail(number, False)
        acc[...] = jnp.zeros_like(acc)
        span_row = lax.broadcasted_iota(jnp.int32, (span, hid), 0)

        def rear(b):
            sum_f, sum_i = jnp.zeros((1, hid), F32), jnp.zeros((1, hid), F32)
            for stream in range(streams):
                at = slice(stream * span, (stream + 1) * span)
                late = incoming[b, stream : stream + 1, :]
                linked = deltas[b, at, :] + prods[b, at, :] * late
                linked = jnp.where(span_row == span - 1, late, pltpu.roll(linked, span - 1, 0))
                delta = gstates[b, at, :] + linked
                early = carry_in[layer, b, stream : stream + 1, :]
                before = jnp.where(span_row == 0, early, pltpu.roll(states[layer, b, at, :], 1, 0))
                f, i = fgate[layer, b, at, :], igate[layer, b, at, :]
                share = 1.0 / (f + i)
                fshare, ishare = f * share, i * share
                gap = delta * (before * widen(mask[at, :], hid) - cand[layer, b, at, :]) * fshare * ishare
                gf = (gap * (1.0 - f)).astype(BF16)
                gi = (gap * (i - 1.0)).astype(BF16)
                low1[at, :], low2[at, :], low3[at, :] = gf, gi, (delta * ishare).astype(BF16)
                sum_f = sum_f + jnp.sum(gf.astype(F32), axis=0, keepdims=True)
                sum_i = sum_i + jnp.sum(gi.astype(F32), axis=0, keepdims=True)
            gbiases[layer, b, 0:1, :] = sum_f
            gbiases[layer, b, 1:2, :] = sum_i
            total = acc[...]
            for member, low in enumerate((low1, low2, low3)):
                put_grad(layer, b, member * hid, hid, dot_tn(low[...], gated[layer]))
                total = total + dot_nn(low[...], weights[layer, b, member * hid : (member + 1) * hid, :])
            acc[...] = total

        each_block(rear)

        def norm_one(k, total):
            at = pl.ds(pl.multiple_of(k * tile, tile), tile)
            values, grad = resid[layer, at, :], acc[at, :]
            scale = lax.rsqrt(jnp.mean(values * values, axis=-1, keepdims=True) + EPSILON)
            unit = values * scale
            gunit = grad * gain_one
            full = dgrad[at, :] + scale * (gunit - unit * jnp.mean(gunit * unit, axis=-1, keepdims=True))
            dgrad[at, :] = full
            return total + jnp.sum(grad * unit, axis=0, keepdims=True)

        ggains[layer, 0:1, :] = lax.fori_loop(0, tokens // tile, norm_one, row_sum)

    def take_out(layer):
        return pltpu.make_async_copy(gstage, grads_ref.at[layer], out_sem.at[0])

    def back_step(k, _):
        layer = layers - 1 - k

        @pl.when(k > 0)
        def _():
            take_out(layer + 1).wait()

        backward(layer)
        take_out(layer).start()
        return 0

    lax.fori_loop(0, layers, lambda layer, _: forward(layer) or 0, 0)

    def turn(at):
        act_ref[at, :] = resid[layers, at, :].astype(BF16)
        dgrad[at, :] = out_grad_ref[at, :].astype(F32)

    each_tile(turn)
    lax.fori_loop(0, layers, back_step, 0)
    dx_ref[...] = dgrad[...]
    each_piece(write_piece)
    take_out(0).wait()


def run_network(geo, mats, stream_in, out_grad, doc_lengths, vectors):
    layers, _, rows, width = mats.shape
    streams, span, _ = stream_in.shape
    hid, ffn = H // geo.n_batch, FF // geo.n_batch
    sizes = (layers, streams, span, width, hid, ffn, rows, doc_lengths.shape[1])
    tokens = streams * span
    vmem = pl.BlockSpec(memory_space=pltpu.VMEM)
    return pl.pallas_call(
        functools.partial(network_kernel, geo, sizes),
        out_shape=(
            jax.ShapeDtypeStruct((tokens, width), BF16),
            jax.ShapeDtypeStruct((tokens, width), F32),
            jax.ShapeDtypeStruct((layers, geo.n_batch, 4 * hid + 2 * ffn, width), BF16),
            jax.ShapeDtypeStruct(vectors.shape, F32),
        ),
        in_specs=[vmem, vmem, vmem, pl.BlockSpec(memory_space=pltpu.SMEM), vmem],
        out_specs=(vmem, vmem, pl.BlockSpec(memory_space=pl.ANY), vmem),
        scratch_shapes=network_scratch(geo, sizes),
        compiler_params=pltpu.CompilerParams(
            collective_id=0, has_side_effects=True, vmem_limit_bytes=62 * 2**20
        ),
        name="network",
    )(mats, stream_in.reshape(tokens, width), out_grad.reshape(tokens, width), doc_lengths, vectors)


def vector_steps(moments, model_width, hidden):
    edge_list = [0, model_width, 2 * model_width, 2 * model_width + hidden, 2 * model_width + 2 * hidden]
    pieces = []
    for member in range(4):
        segment = moments[:, edge_list[member] : edge_list[member + 1]]
        pieces.append(
            SEGMENT_RATES[member]
            * segment
            * lax.rsqrt(jnp.mean(segment * segment, axis=1, keepdims=True) + 1e-06)
        )
    return jnp.concatenate(pieces, axis=1)


def per_device(
    geo, stream_in, out_grad, doc_lengths, mats, mat_momenta, mat_averages, vectors, vec_momenta, vec_averages
):
    layer_count, _, shard_rows, model_width = mats.shape
    activations, grad_resid, full_grads, vec_part = run_network(
        geo, mats, stream_in, out_grad, doc_lengths, vectors
    )
    offsets = [0]
    for count in [H // geo.n_batch] * 4 + [FF // geo.n_batch] * 2:
        offsets.append(offsets[-1] + count)
    block_rows = offsets[6]
    grad_shard = lax.psum_scatter(
        full_grads.astype(F32).reshape(layer_count, geo.n_batch * block_rows, model_width),
        ("batch", "seq"), scatter_dimension=1, tiled=True,
    )
    vec_grads = lax.psum(vec_part, ("batch", "seq"))
    mom_shard = MOMENTUM_DECAY * mat_momenta.reshape(layer_count, shard_rows, model_width) + grad_shard
    mom_block = lax.all_gather(mom_shard.astype(BF16), "seq", axis=1, tiled=True).astype(F32)
    pieces = [
        mom_block[layer_idx, offsets[member] : offsets[member + 1]]
        for layer_idx in range(layer_count)
        for member in range(6)
    ]
    local_squares = jnp.stack([jnp.sum(piece * piece) for piece in pieces])
    frob_norms = jnp.sqrt(lax.psum(local_squares, "batch"))
    iterates = [(piece / (frob_norms[n] + 1e-07)).astype(BF16) for n, piece in enumerate(pieces)]
    for step_idx in range(NS_STEPS):
        partials = jnp.stack([dot_tn(iterate, iterate) for iterate in iterates])
        gram_sums = lax.psum(partials.astype(BF16), "batch").astype(F32)
        gram_low = gram_sums.astype(BF16)
        polynomial = QUINTIC[1] * gram_sums + QUINTIC[2] * jnp.einsum(
            "nde,nef->ndf", gram_low, gram_low, preferred_element_type=F32
        )
        poly_low = polynomial.astype(BF16)
        iterates = [
            (QUINTIC[0] * iterate.astype(F32) + dot_nn(iterate, poly_low[n])).astype(BF16)
            for n, iterate in enumerate(iterates)
        ]
    factors = [0.2 * math.sqrt(max(count, model_width)) for count in [H] * 4 + [FF] * 2]
    ortho_block = jnp.stack(
        [
            jnp.concatenate([iterates[6 * l + m].astype(F32) * factors[m] for m in range(6)], axis=0)
            for l in range(layer_count)
        ]
    )
    own_rows = lax.dynamic_slice_in_dim(ortho_block, lax.axis_index("seq") * shard_rows, shard_rows, axis=1)
    new_flat = mats.reshape(layer_count, shard_rows, model_width) - MATRIX_RATE * own_rows
    new_avg_flat = (
        AVERAGE_DECAY * mat_averages.reshape(layer_count, shard_rows, model_width)
        + (1.0 - AVERAGE_DECAY) * new_flat
    )
    new_vec_momenta = MOMENTUM_DECAY * vec_momenta + vec_grads
    new_vectors = vectors - vector_steps(new_vec_momenta, model_width, H)
    new_vec_averages = AVERAGE_DECAY * vec_averages + (1.0 - AVERAGE_DECAY) * new_vectors
    out_shape = (layer_count, 1, shard_rows, model_width)
    return (
        activations.reshape(stream_in.shape),
        grad_resid.reshape(stream_in.shape),
        grad_shard.reshape(out_shape),
        mom_block.reshape(layer_count, 1, block_rows, model_width),
        new_flat.reshape(out_shape),
        new_avg_flat.reshape(out_shape),
        vec_grads,
        new_vec_momenta,
        new_vectors,
        new_vec_averages,
    )


def solution(mesh):
    geo = Geometry(mesh.shape["seq"], mesh.shape["batch"])
    rows = P(None, "batch", "seq", None)
    tokens = P("batch", "seq", None)
    return jax.shard_map(
        functools.partial(per_device, geo),
        mesh=mesh,
        in_specs=(tokens, tokens, P("batch", None), rows, rows, rows, P(), P(), P()),
        out_specs=(tokens, tokens, rows, P(None, "batch", None, None), rows, rows, P(), P(), P(), P()),
        check_vma=False,
    )
```

time: 2300 us -> 1330 us (0.58)
  local copies, waits for them, and re-layouts: 506 us -> 12.7 us
  blocking collectives: 304 us -> 47.4 us
  other arithmetic: 239 us -> 34.1 us
  Pallas kernels: 0 us -> 168 us
  waiting for transfers between devices: 1080 us -> 978 us
  matrix products: 126 us -> 65.7 us
    slice x193 -> x1, local copies, waits for them, and re-layouts: 335 us -> 0.7 us  [per_device(): frob_norms[n] + 1e-07]
    all_gather x8 -> x0, blocking collectives: 245 us -> none  [carried_in(): everything = jax.tree.map(lambda part: lax.all_gather(part, axis), x)]
    pallas_call x0 -> x1, Pallas kernels: none -> 168 us  [run_network(): pl.pallas_call(functools.partial(network_kernel, geo, sizes), out_shape=(...]
    all_gather x2 -> x1, waiting for transfers between devices: 183 us -> 72.1 us  [per_device(): lax.all_gather(mom_shard.astype(BF16), 'seq', axis=1, tiled=True)]
    pad x96 -> x0, local copies, waits for them, and re-layouts: 99.2 us -> none  [the longest x48 66.8 us: layer_back(): lax.associative_scan(linked, (next_coef, grad_states), reverse=True, axis=1)]
    add x87 -> x0, other arithmetic: 85.3 us -> none  [the longest x28 33.4 us: layer_back(): lax.associative_scan(linked, (next_coef, grad_states), reverse=True, axis=1)]
    dot_general x86 -> x50, matrix products: 126 us -> 65.7 us  [the longest x24 33.7 us: dot_tn(): lax.dot_general(a, b, (((0,), (0,)), ((), ())), preferred_element_type=F32)]
    mul x26 -> x0, other arithmetic: 42 us -> none  [the longest x24 38.7 us: linked(): return (earlier[0] * latter[0], latter[0] * earlier[1] + latter[1])]
  transfers between devices with their start and end apart: 5 -> 4, of which waited for: 5 -> 4; matrix products, arithmetic and copies ran while one was open for 1% -> 0% of each run, Pallas kernels for 0% -> 0%
where the time goes in v1:
time: 1330 us
  waiting for transfers between devices  978 us (74%)
  Pallas kernels  168 us (13%)
  matrix products  65.7 us (5%)
  blocking collectives  47.4 us (4%)
  other arithmetic  34.1 us (3%)
  between operations  22.2 us (2%)
    reduce_scatter x1, waiting for transfers between devices, per_device(): lax.psum_scatter(full_grads.astype(F32).reshape(layer_count, geo.n_batch...  709 us
    psum x2, waiting for transfers between devices, per_device(): gram_sums = lax.psum(partials.astype(BF16), 'batch').astype(F32)  197 us
    pallas_call x1, Pallas kernels, run_network(): pl.pallas_call(functools.partial(network_kernel, geo, sizes), out_shape=(...  168 us
    all_gather x1, waiting for transfers between devices, per_device(): lax.all_gather(mom_shard.astype(BF16), 'seq', axis=1, tiled=True)  72.1 us
    psum x1, blocking collectives, per_device(): vec_grads = lax.psum(vec_part, ('batch', 'seq'))  41.5 us
    dot_general x24, matrix products, dot_tn(): lax.dot_general(a, b, (((0,), (0,)), ((), ())), preferred_element_type=F32)  33.7 us
  transfers between devices with their start and end apart: 4, of which 4 were waited for; matrix products, arithmetic and copies ran while one was open for 0% of the time, Pallas kernels for 0%

profile of v1, /device:TPU:26, one launch (start us, length us, event | category | flops | bytes accessed | tf_op | source)
XLA Modules:
  0.0 1328.2 jit_solution(9754785537389449322)
XLA Ops:
  7.2 167.6 %network.1 = (bf16[256,512]{1,0:T(8,128)(2,1)}, f32[256,512]{1,0:T(8,128)}, bf16[2,4,2048,512]{3,2,1,0:T(8,128)(2,1)}, f32[2,3072]{1,0:T(2,128)}) custom-call(f32[2,1,256,512]{3,2,1,0:T(8,128)} %mats_ref.1, bf16[256,512]{1,0:T(8,128)(2,1)} %bitcast.366, bf16[256,512]{1,0:T(8,128)(2,1)} %bitcast.367, s32[2,16]{1,0:T(2,128)} %doc_ref.1, f32[2,3072]{1,0:T(2,128)} %vec_ref.1), custom_call_target="tpu_custom_call" | custom-call | tf_op jit(solution)/shard_map/network/pallas_call | solution.py:624
  174.8 18.9 %bitcast_convert_fusion = f32[2,8192,512]{2,1,0:T(8,128)} fusion(bf16[2,4,2048,512]{3,2,1,0:T(8,128)(2,1)} %get-tuple-element.16), kind=kLoop, calls=%fused_computation | loop fusion | flops 8388608 | bytes 50331648 | tf_op jit(solution)/shard_map/reshape | solution.py:667
  193.7 708.8 %reduce-scatter.2.cloned.1.call-done = f32[2,256,512]{2,1,0:T(8,128)} async-done(((f32[2,8192,512]{2,1,0:T(8,128)}), f32[2,256,512]{2,1,0:T(8,128)}) %reduce-scatter.2.cloned.1.call-update) | async-done | bytes 1048592 | tf_op jit(solution)/shard_map/reduce_scatter | solution.py:666
  902.6 2.3 fusion.112
  904.9 72.1 %all-gather.2.cloned.1.call-done = bf16[2,2048,512]{2,1,0:T(8,128)(2,1)} async-done(((bf16[2,256,512]{2,1,0:T(8,128)(2,1)}), bf16[2,2048,512]{2,1,0:T(8,128)(2,1)}) %all-gather.2.cloned.1.call-update) | async-done | bytes 4194320 | tf_op jit(solution)/shard_map/all_gather | solution.py:672
  977.0 7.9 fusion.138
  986.1 2.0 copy-done
  989.1 7.6 stack.164
  996.7 5.9 psum.28
  1004.3 2.6 fusion.21
  1014.0 2.4 fusion.23
  1016.4 2.3 fusion.25
  1018.7 2.4 fusion.27
  1021.1 1.3 fusion.53
  1031.1 118.8 %all-reduce.3.cloned.1.call-done = bf16[12,512,512]{2,1,0:T(8,128)(2,1)} async-done(((bf16[12,512,512]{2,1,0:T(8,128)(2,1)}), bf16[12,512,512]{2,1,0:T(8,128)(2,1)}) %all-reduce.3.cloned.1.call-update) | async-done | bytes 6291472 | tf_op jit(solution)/shard_map/psum | solution.py:683
  1149.9 10.1 add_convert_fusion.1
  1160.0 2.1 fusion.3
  1162.2 2.1 fusion.2
  1173.2 1.3 fusion.61
  1174.5 1.3 fusion.63
  1183.0 41.5 %psum.31 = f32[2,3072]{1,0:T(2,128)S(1)} all-reduce(f32[2,3072]{1,0:T(2,128)S(1)} %copy-done.10), channel_id=1, replica_groups=mesh['seq'=8,'batch'=4] {'batch','seq'}, use_global_device_ids=true, to_apply=%region_16.0 | all-reduce | flops 6144 | bytes 49152 | tf_op jit(solution)/shard_map/psum | solution.py:670
  1225.7 78.3 %all-reduce.5.cloned.1.call-done = bf16[12,512,512]{2,1,0:T(8,128)(2,1)} async-done(((bf16[12,512,512]{2,1,0:T(8,128)(2,1)}), bf16[12,512,512]{2,1,0:T(8,128)(2,1)}) %all-reduce.5.cloned.1.call-update) | async-done | bytes 6291472 | tf_op jit(solution)/shard_map/psum | solution.py:683
  1304.0 10.0 add_convert_fusion
  1318.4 1.7 fusion.111
  (99 shorter events, 34.6 us)
Async XLA Ops:
  7.2 895.4 %reduce-scatter.2.cloned.1.call-start = ((), (), s32[]{:S(2)}) async-start(), calls=%async_computation.1 | async-start | bytes 34603008 | tf_op jit(solution)/shard_map/reduce_scatter | solution.py:666
  193.7 708.9 %copy-start.4 = (f32[2,1,256,512]{3,2,1,0:T(8,128)S(1)}, f32[2,1,256,512]{3,2,1,0:T(8,128)}, u32[]{:S(2)}) copy-start(f32[2,1,256,512]{3,2,1,0:T(8,128)} %param.13) | copy-start | bytes 3145732
  193.7 783.3 %all-gather.2.cloned.1.call-start = ((), (), s32[]{:S(2)}) async-start(), calls=%async_computation.2 | async-start | bytes 4718592 | tf_op jit(solution)/shard_map/all_gather | solution.py:672
  904.9 245.0 %all-reduce.3.cloned.1.call-start = ((), (), s32[]{:S(2)}) async-start(), calls=%async_computation.3 | async-start | bytes 12582912 | tf_op jit(solution)/shard_map/psum | solution.py:683
  984.8 3.2 copy-start
  1002.7 18.4 %copy-start.1 = (f32[2,2048,512]{2,1,0:T(8,128)S(1)}, f32[2,2048,512]{2,1,0:T(8,128)}, u32[]{:S(2)}) copy-start(f32[2,2048,512]{2,1,0:T(8,128)} %copy-done) | copy-start | bytes 25165828
  1030.8 273.1 %all-reduce.5.cloned.1.call-start = ((), (), s32[]{:S(2)}) async-start(), calls=%async_computation.4 | async-start | bytes 12582912 | tf_op jit(solution)/shard_map/psum | solution.py:683
  1160.0 4.3 slice-start
  1162.2 3.0 slice-start.1
  1166.6 7.9 copy-start.13
  1167.0 6.2 copy-start.15
  1178.1 4.9 copy-start.10
  1178.1 46.4 %copy-start.11 = (f32[2,3072]{1,0:T(2,128)S(1)}, f32[2,3072]{1,0:T(2,128)}, u32[]{:S(2)}) copy-start(f32[2,3072]{1,0:T(2,128)} %param.16) | copy-start | bytes 73732
  1178.1 46.9 %copy-start.9 = (f32[2,3072]{1,0:T(2,128)S(1)}, f32[2,3072]{1,0:T(2,128)}, u32[]{:S(2)}) copy-start(f32[2,3072]{1,0:T(2,128)} %vec_ref.1) | copy-start | bytes 73732
  1178.1 46.9 %copy-start.12 = (f32[2,3072]{1,0:T(2,128)S(1)}, f32[2,3072]{1,0:T(2,128)}, u32[]{:S(2)}) copy-start(f32[2,3072]{1,0:T(2,128)} %param.17) | copy-start | bytes 73732
  1224.5 89.5 %copy-start.8 = (f32[2,3072]{1,0:T(2,128)}, f32[2,3072]{1,0:T(2,128)S(1)}, u32[]{:S(2)}) copy-start(f32[2,3072]{1,0:T(2,128)S(1)} %psum.31) | copy-start | bytes 73732
  1224.5 89.5 %copy-start.7 = (f32[2,3072]{1,0:T(2,128)}, f32[2,3072]{1,0:T(2,128)S(1)}, u32[]{:S(2)}) copy-start(f32[2,3072]{1,0:T(2,128)S(1)} %multiply_add_fusion.1) | copy-start | bytes 73732
  1314.0 1.6 copy-start.16
  1314.0 2.0 copy-start.14
  1316.1 2.3 copy-start.2
  1316.1 2.3 copy-start.3
  1318.4 1.7 copy-start.6
  1318.4 2.4 copy-start.5
Sparse Core Ops, SparseCore 0:
  193.8 708.7 reduce-scatter.1
  905.3 71.6 all-gather.1
  1030.9 118.8 all-reduce.2
  1183.1 120.8 all-reduce.4

commit v2 on v1

--- a/solution.py
+++ b/solution.py
@@ -639,81 +639,556 @@
     )(mats, stream_in.reshape(tokens, width), out_grad.reshape(tokens, width), doc_lengths, vectors)
 
 
-def vector_steps(moments, model_width, hidden):
-    edge_list = [0, model_width, 2 * model_width, 2 * model_width + hidden, 2 * model_width + 2 * hidden]
-    pieces = []
-    for member in range(4):
-        segment = moments[:, edge_list[member] : edge_list[member + 1]]
-        pieces.append(
-            SEGMENT_RATES[member]
-            * segment
-            * lax.rsqrt(jnp.mean(segment * segment, axis=1, keepdims=True) + 1e-06)
+def update_scratch(geo, sizes):
+    layers, rows, width, hid, ffn = sizes
+    block = 4 * hid + 2 * ffn
+    nz, nu, nv, nx, ny = geo.nz, geo.nu, geo.nv, geo.nx, geo.ny
+    half, most = width // 2, max(ffn // rows - 1, 1)
+    vec = 2 * width + 2 * hid * geo.n_batch
+
+    def full(dtype, *shape):
+        return pltpu.VMEM(shape, dtype)
+
+    dma = pltpu.SemaphoreType.DMA
+    return [
+        full(BF16, layers, nz * nu * nv, rows, width),
+        full(BF16, layers, nv - 1, nu * nz, rows, width),
+        full(BF16, layers, nu - 1, nz, rows, width),
+        full(BF16, layers, nz - 1, rows, width),
+        full(F32, layers, rows, width),
+        full(BF16, layers, rows, width),
+        full(BF16, 3, 3, half, half),
+        full(BF16, 1, 3, half, half),
+        full(BF16, nx - 1, 3, half, half),
+        full(BF16, most, 3, half, half),
+        full(F32, 3, 8, 128),
+        full(F32, 1, 8, 128),
+        full(F32, nx - 1, 8, 128),
+        full(F32, most, 8, 128),
+        full(F32, 3, half, half),
+        full(F32, width, width),
+        full(F32, width, width),
+        full(BF16, layers, 2, width, width),
+        full(F32, layers, 8, 128),
+        full(F32, 3, layers, vec),
+        full(F32, 1, layers, vec),
+        full(F32, nx, layers, vec),
+        full(F32, geo.n_seq, layers, vec),
+        dma((layers,)),
+        dma((layers, nv - 1)),
+        dma((layers, nu - 1)),
+        dma((layers, nz - 1)),
+        dma((layers, nz * nu * nv)),
+        dma((layers, nv - 1, nu * nz)),
+        dma((layers, nu - 1, nz)),
+        dma((layers, nz - 1)),
+        dma((layers, nz - 1)),
+        dma((layers, ny - 1)),
+        dma((layers, geo.n_seq)),
+        dma((2,)),
+        dma((2, nx - 1)),
+        dma((2, most)),
+        dma((2,)),
+        dma((2, nx - 1)),
+        dma((2, most)),
+        dma((2,)),
+        dma((2,)),
+        dma((1,)),
+        dma((nx,)),
+        dma((geo.n_seq,)),
+        dma((1,)),
+        dma((nx,)),
+        dma((geo.n_seq,)),
+    ]
+
+
+def update_kernel(
+    geo, sizes, grads, old_ref, vpart_ref, vectors_ref, vmom_ref, vavg_ref,
+    shard_ref, block_ref, ortho_ref, vgrad_ref, new_vmom_ref, new_vec_ref, new_vavg_ref, *scratch
+):
+    (
+        in_s, in_v, in_u, in_z, moments, low_moments, gram_out, gram_s, gram_x, gram_g, square_out, square_s, square_x,
+        square_g, gram, even, odd, polys, inverses, vec_out, vec_s, vec_x, vec_q, send_s, send_v, send_u, send_z,
+        recv_s, recv_v, recv_u, recv_z, block_send_z, block_send_y, block_recv, gram_send_s, gram_send_x, gram_send_g,
+        gram_recv_s, gram_recv_x, gram_recv_g, poly_send, poly_recv, vec_send_s, vec_send_x, vec_send_q, vec_recv_s,
+        vec_recv_x, vec_recv_q,
+    ) = scratch
+    layers, rows, width, hid, ffn = sizes
+    nz, nu, nv, nx, ny = geo.nz, geo.nu, geo.nv, geo.nx, geo.ny
+    seq, batch, z, y, x, core = geo.here()
+    if geo.swaps:
+        u, v = y + core * (x - y), x + core * (y - x)
+    else:
+        u, v = y, x
+    half, tile = width // 2, min(rows, 32)
+    sibling = (seq, x * 2 + 1 - core)
+
+    def remote(src, dst, send, recv, device):
+        return pltpu.make_async_remote_copy(
+            src_ref=src, dst_ref=dst, send_sem=send, recv_sem=recv, device_id=device, device_id_type=MESH
         )
-    return jnp.concatenate(pieces, axis=1)
+
+    def each_tile(body):
+        lax.fori_loop(0, rows // tile, lambda k, _: body(k * tile) or 0, 0)
+
+    def count(first, last, body):
+        lax.fori_loop(first, last, lambda k, _: body(k) or 0, 0)
+
+    def offsets(k):
+        return (k // (nu * nz) + 1) % nv, (k // nz + 1) % nu, (k + 1) % nz
+
+    def place(k, side):
+        dv, du, dz = offsets(k)
+        if geo.swaps:
+            u_side, v_side = y + side * (x - y), x + side * (y - x)
+        else:
+            u_side, v_side = y, x
+        y_at, x_at = geo.to_yx(other(u_side, du, nu), other(v_side, dv, nv), side)
+        start = pl.multiple_of(geo.seq_of(other(z, dz, nz), y_at) * rows, rows)
+        return x_at * 2 + side, start
+
+    def peer(dz, du, dv):
+        y_at, x_at = geo.to_yx(other(u, du, nu), other(v, dv, nv), core)
+        return (geo.seq_of(other(z, dz, nz), y_at), x_at * 2 + core)
+
+    def slot(layer, k, side):
+        b, start = place(k, side)
+        return grads.at[layer, b, pl.ds(start, rows)]
+
+    def swap_cores(layer):
+        def one(k):
+            remote(
+                slot(layer, k, 1 - core), in_s.at[layer, k], send_s.at[layer], recv_s.at[layer, k], sibling
+            ).start()
+
+        count(0, nz * nu * nv, one)
+
+    def wait_s(layer, k):
+        remote(slot(layer, k, core), in_s.at[layer, k], send_s.at[layer], recv_s.at[layer, k], sibling).wait_recv()
+
+    def wait_v(layer, j):
+        for dv in range(1, nv):
+            remote(
+                in_v.at[layer, dv - 1, j], in_v.at[layer, dv - 1, j], send_v.at[layer, dv - 1],
+                recv_v.at[layer, dv - 1, j], sibling,
+            ).wait_recv()
+
+    def wait_u(layer, i):
+        for du in range(1, nu):
+            remote(
+                in_u.at[layer, du - 1, i], in_u.at[layer, du - 1, i], send_u.at[layer, du - 1],
+                recv_u.at[layer, du - 1, i], sibling,
+            ).wait_recv()
+
+    def add_up(layer, k, extra):
+        b, start = place(k, core)
+
+        def one(first):
+            at = pl.ds(pl.multiple_of(start + first, tile), tile)
+            inner = pl.ds(pl.multiple_of(first, tile), tile)
+            total = grads[layer, b, at, :].astype(F32) + in_s[layer, k, inner, :].astype(F32)
+            for ref, index in extra:
+                total = total + ref[(*index, inner, slice(None))].astype(F32)
+            grads[layer, b, at, :] = total.astype(BF16)
+
+        each_tile(one)
+
+    def from_v(layer, j):
+        return [(in_v, (layer, dv - 1, j)) for dv in range(1, nv)]
+
+    def from_u(layer, i):
+        return [(in_u, (layer, du - 1, i)) for du in range(1, nu)]
+
+    def stage_v(layer):
+        def one(k):
+            wait_s(layer, k)
+            add_up(layer, k, [])
+            dv = k // (nu * nz) + 1
+            j = k % (nu * nz)
+            remote(
+                slot(layer, k, core), in_v.at[layer, dv - 1, j], send_v.at[layer, dv - 1],
+                recv_v.at[layer, dv - 1, j], peer(0, 0, dv),
+            ).start()
+
+        count(0, (nv - 1) * nu * nz, one)
+
+    def stage_u(layer):
+        def one(j):
+            k = (nv - 1) * nu * nz + j
+            wait_s(layer, k)
+            wait_v(layer, j)
+            add_up(layer, k, from_v(layer, j))
+            du = j // nz + 1
+            i = j % nz
+            remote(
+                slot(layer, k, core), in_u.at[layer, du - 1, i], send_u.at[layer, du - 1],
+                recv_u.at[layer, du - 1, i], peer(0, du, 0),
+            ).start()
+
+        count(0, (nu - 1) * nz, one)
+
+    def stage_z(layer):
+        def one(i):
+            j = (nu - 1) * nz + i
+            k = (nv - 1) * nu * nz + j
+            wait_s(layer, k)
+            wait_v(layer, j)
+            wait_u(layer, i)
+            add_up(layer, k, from_v(layer, j) + from_u(layer, i))
+            remote(
+                slot(layer, k, core), in_z.at[layer, i], send_z.at[layer, i], recv_z.at[layer, i], peer(i + 1, 0, 0)
+            ).start()
+
+        count(0, nz - 1, one)
+
+    def block_slot(layer, z_at, y_at):
+        start = pl.multiple_of(geo.seq_of(z_at, y_at) * rows, rows)
+        return block_ref.at[layer, pl.ds(start, rows)]
+
+    def block_to_y(layer, z_at):
+        part = block_slot(layer, z_at, y)
+        for step in range(1, ny):
+            remote(
+                part, part, block_send_y.at[layer, step - 1], block_recv.at[layer, geo.seq_of(z_at, y)],
+                (geo.seq_of(z, other(y, step, ny)), batch),
+            ).start()
+
+    def own_grad(layer):
+        i = nz - 1
+        j = (nu - 1) * nz + i
+        k = (nv - 1) * nu * nz + j
+        wait_s(layer, k)
+        wait_v(layer, j)
+        wait_u(layer, i)
+        for dz in range(1, nz):
+            remote(
+                in_z.at[layer, dz - 1], in_z.at[layer, dz - 1], send_z.at[layer, dz - 1],
+                recv_z.at[layer, dz - 1], sibling,
+            ).wait_recv()
+        b, start = place(k, core)
+        extra = from_v(layer, j) + from_u(layer, i) + [(in_z, (layer, dz - 1)) for dz in range(1, nz)]
+
+        def one(k_tile, squares):
+            first = k_tile * tile
+            at = pl.ds(pl.multiple_of(start + first, tile), tile)
+            inner = pl.ds(pl.multiple_of(first, tile), tile)
+            total = grads[layer, b, at, :].astype(F32) + in_s[layer, k, inner, :].astype(F32)
+            for ref, index in extra:
+                total = total + ref[(*index, inner, slice(None))].astype(F32)
+            shard_ref[layer, inner, :] = total
+            moment = MOMENTUM_DECAY * old_ref[layer, 0, inner, :] + total
+            moments[layer, inner, :] = moment
+            low = moment.astype(BF16)
+            low_moments[layer, inner, :] = low
+            block_ref[layer, at, :] = low
+            return squares + jnp.sum(moment * moment, axis=0, keepdims=True)
+
+        squares = lax.fori_loop(0, rows // tile, one, jnp.zeros((1, width), F32))
+        part = block_slot(layer, z, y)
+        for step in range(1, nz):
+            remote(
+                part, part, block_send_z.at[layer, step - 1], block_recv.at[layer, seq],
+                (geo.seq_of(other(z, step, nz), y), batch),
+            ).start()
+        block_to_y(layer, z)
+        return jnp.broadcast_to(jnp.sum(squares, axis=1, keepdims=True), (8, 128))
+
+    def wait_block(layer, z_at, y_at):
+        part = block_slot(layer, z_at, y_at)
+        remote(
+            part, part, block_send_z.at[layer, 0], block_recv.at[layer, geo.seq_of(z_at, y_at)], sibling
+        ).wait_recv()
+
+    def spread_block(layer):
+        for step in range(1, nz):
+            z_at = lax.rem(z - step + nz, nz)
+            wait_block(layer, z_at, y)
+            block_to_y(layer, z_at)
+
+    def finish_block(layer):
+        for step in range(0, nz):
+            z_at = lax.rem(z - step + nz, nz)
+            count(1, ny, lambda k: wait_block(layer, z_at, other(y, k, ny)))
+
+    def vec_start():
+        vec_out[0] = vpart_ref[...]
+        remote(vec_out.at[0], vec_s.at[0], vec_send_s.at[0], vec_recv_s.at[0], sibling).start()
+
+    def vec_second():
+        remote(vec_out.at[0], vec_s.at[0], vec_send_s.at[0], vec_recv_s.at[0], sibling).wait_recv()
+        total = vec_out[0] + vec_s[0]
+        vec_out[1] = total
+        vec_x[x] = total
+        for step in range(1, nx):
+            x_at = other(x, step, nx)
+            remote(
+                vec_out.at[1], vec_x.at[x], vec_send_x.at[x_at], vec_recv_x.at[x], (seq, x_at * 2 + core)
+            ).start()
+
+    def vec_third():
+        for step in range(1, nx):
+            x_at = other(x, step, nx)
+            remote(
+                vec_out.at[1], vec_x.at[x_at], vec_send_x.at[x_at], vec_recv_x.at[x_at], sibling
+            ).wait_recv()
+        total = vec_x[0]
+        for k in range(1, nx):
+            total = total + vec_x[k]
+        vec_out[2] = total
+        vec_q[seq] = total
+
+        def one(k):
+            to = other(seq, k, geo.n_seq)
+            remote(vec_out.at[2], vec_q.at[seq], vec_send_q.at[to], vec_recv_q.at[seq], (to, batch)).start()
+
+        count(1, geo.n_seq, one)
+
+    def vec_last():
+        def one(k):
+            source = other(seq, k, geo.n_seq)
+            remote(
+                vec_out.at[2], vec_q.at[source], vec_send_q.at[source], vec_recv_q.at[source], sibling
+            ).wait_recv()
+
+        count(1, geo.n_seq, one)
+        total = lax.fori_loop(1, geo.n_seq, lambda k, t: t + vec_q[k], vec_q[0])
+        vgrad_ref[...] = total
+        new_vmom_ref[...] = MOMENTUM_DECAY * vmom_ref[...] + total
+        first = 0
+        for member, length in enumerate((width, width, hid * geo.n_batch, hid * geo.n_batch)):
+            at = slice(first, first + length)
+            segment = new_vmom_ref[:, at]
+            scale = lax.rsqrt(jnp.mean(segment * segment, axis=1, keepdims=True) + 1e-06)
+            fresh = vectors_ref[:, at] - SEGMENT_RATES[member] * segment * scale
+            new_vec_ref[:, at] = fresh
+            new_vavg_ref[:, at] = AVERAGE_DECAY * vavg_ref[:, at] + (1.0 - AVERAGE_DECAY) * fresh
+            first += length
+
+    hid_devices, ffn_devices = hid // rows, ffn // rows
+    in_group = jnp.where(seq < 4 * hid_devices, hid_devices, ffn_devices)
+    rank = lax.rem(seq, in_group)
+    group_first = seq - rank
+
+    def pack_gram(stage, value):
+        gram_out[stage, 0] = value[0:half, 0:half].astype(BF16)
+        gram_out[stage, 1] = value[0:half, half:].astype(BF16)
+        gram_out[stage, 2] = value[half:, half:].astype(BF16)
+
+    def gram_pair(stage, into, squares_into, sends, recvs, device):
+        return (
+            remote(gram_out.at[stage], into, sends[0], recvs[0], device),
+            remote(square_out.at[stage], squares_into, sends[1], recvs[1], device),
+        )
+
+    def gram_round(stage, parts, squares):
+        for n in range(3):
+            total = gram_out[stage, n].astype(F32)
+            for ref in parts:
+                total = total + ref[n].astype(F32)
+            gram[n] = total
+            gram_out[stage + 1, n] = total.astype(BF16)
+        total = square_out[stage]
+        for ref in squares:
+            total = total + ref[...]
+        square_out[stage + 1] = total
+
+    def group_copies(k):
+        here_at = lax.rem(rank - k - 1 + in_group, in_group)
+        return gram_pair(
+            2, gram_g.at[here_at], square_g.at[here_at],
+            (gram_send_g.at[0, here_at], gram_send_g.at[1, here_at]),
+            (gram_recv_g.at[0, here_at], gram_recv_g.at[1, here_at]), (group_first + k, batch),
+        )
+
+    def newton_schulz(squares):
+        mine, theirs = core, 1 - core
+        pack_gram(0, dot_tn(low_moments[theirs], low_moments[theirs]))
+        square_out[0] = jnp.where(core == 0, squares[1], squares[0])
+        to_core = gram_pair(
+            0, gram_s.at[0], square_s.at[0], (gram_send_s.at[0], gram_send_s.at[1]),
+            (gram_recv_s.at[0], gram_recv_s.at[1]), sibling,
+        )
+        for copy in to_core:
+            copy.start()
+        partial = dot_tn(low_moments[mine], low_moments[mine])
+        for copy in to_core:
+            copy.wait()
+        pack_gram(0, partial)
+        square_out[0] = jnp.where(core == 0, squares[0], squares[1])
+        gram_round(0, [gram_s.at[0]], [square_s.at[0]])
+        to_x = []
+        for step in range(1, nx):
+            to_x += gram_pair(
+                1, gram_x.at[step - 1], square_x.at[step - 1],
+                (gram_send_x.at[0, step - 1], gram_send_x.at[1, step - 1]),
+                (gram_recv_x.at[0, step - 1], gram_recv_x.at[1, step - 1]),
+                (seq, other(x, step, nx) * 2 + core),
+            )
+        for copy in to_x:
+            copy.start()
+        for copy in to_x:
+            copy.wait()
+        gram_round(1, [gram_x.at[k] for k in range(nx - 1)], [square_x.at[k] for k in range(nx - 1)])
+
+        def to_member(k):
+            for copy in group_copies(lax.rem(rank + k, in_group)):
+                copy.start()
+
+        def from_member(k):
+            k = k - 1
+            pltpu.make_async_remote_copy(
+                src_ref=gram_out.at[2], dst_ref=gram_g.at[k], send_sem=gram_send_g.at[0, k],
+                recv_sem=gram_recv_g.at[0, k], device_id=sibling, device_id_type=MESH,
+            ).wait()
+            pltpu.make_async_remote_copy(
+                src_ref=square_out.at[2], dst_ref=square_g.at[k], send_sem=gram_send_g.at[1, k],
+                recv_sem=gram_recv_g.at[1, k], device_id=sibling, device_id_type=MESH,
+            ).wait()
+
+        count(1, in_group, to_member)
+        for n in range(3):
+            gram[n] = gram_out[2, n].astype(F32)
+        count(1, in_group, from_member)
+
+        def add_member(k, total):
+            for n in range(3):
+                gram[n] += gram_g[k - 1, n].astype(F32)
+            return total + square_g[k - 1]
+
+        square = lax.fori_loop(1, in_group, add_member, square_out[2])
+        inverse = 1.0 / (jnp.sqrt(square) + 1e-07)
+        inverses[mine] = inverse
+        scale = inverse[0:1, 0:1] * inverse[0:1, 0:1]
+        even[0:half, 0:half] = gram[0] * scale
+        even[0:half, half:] = gram[1] * scale
+        even[half:, 0:half] = gram[1].T * scale
+        even[half:, half:] = gram[2] * scale
+
+        def polynomial(step):
+            low = even[...].astype(BF16)
+            value = QUINTIC[1] * even[...] + QUINTIC[2] * dot_nn(low, low)
+            polys[mine, step] = value.astype(BF16)
+
+        polynomial(0)
+        lead = QUINTIC[0]
+        high = even[...].astype(BF16)
+        rest = (even[...] - high.astype(F32)).astype(BF16)
+        poly = polys[mine, 0]
+        odd[...] = dot_nn(poly, high) + dot_nn(poly, rest)
+        high = odd[...].astype(BF16)
+        rest = (odd[...] - high.astype(F32)).astype(BF16)
+        even[...] = (
+            lead * lead * even[...] + 2.0 * lead * odd[...] + (dot_nn(poly, high) + dot_nn(poly, rest))
+        )
+        polynomial(1)
+        give = (
+            remote(polys.at[mine], polys.at[mine], poly_send.at[0], poly_recv.at[0], sibling),
+            remote(inverses.at[mine], inverses.at[mine], poly_send.at[1], poly_recv.at[1], sibling),
+        )
+        for copy in give:
+            copy.start()
+
+        def apply(layer):
+            begin = (moments[layer] * inverses[layer, 0:1, 0:1]).astype(BF16)
+            for step in range(NS_STEPS):
+                begin = (lead * begin.astype(F32) + dot_nn(begin, polys[layer, step])).astype(BF16)
+            ortho_ref[layer] = begin
+
+        apply(mine)
+        for copy in give:
+            copy.wait_send()
+        remote(polys.at[theirs], polys.at[theirs], poly_send.at[0], poly_recv.at[0], sibling).wait_recv()
+        remote(inverses.at[theirs], inverses.at[theirs], poly_send.at[1], poly_recv.at[1], sibling).wait_recv()
+        apply(theirs)
+
+    enter(geo)
+    vec_start()
+    order = list(reversed(range(layers)))
+    for layer in order:
+        swap_cores(layer)
+    squares = [None] * layers
+    vec_step = [vec_second, vec_third, vec_last]
+    for layer in order:
+        stage_v(layer)
+        if vec_step:
+            vec_step.pop(0)()
+        stage_u(layer)
+        stage_z(layer)
+        if vec_step:
+            vec_step.pop(0)()
+        squares[layer] = own_grad(layer)
+    for layer in order:
+        spread_block(layer)
+    newton_schulz(squares)
+    for layer in order:
+        finish_block(layer)
+
+    def drain(part, sem):
+        pltpu.make_async_remote_copy(
+            src_ref=part, dst_ref=part, send_sem=sem, recv_sem=vec_recv_s.at[0], device_id=sibling,
+            device_id_type=MESH,
+        ).wait_send()
+
+    for layer in range(layers):
+        drain(grads.at[layer, pl.ds(0, nx)], send_s.at[layer])
+        for dv in range(1, nv):
+            drain(grads.at[layer, 0], send_v.at[layer, dv - 1])
+        for du in range(1, nu):
+            drain(grads.at[layer, 0, pl.ds(0, nz * rows)], send_u.at[layer, du - 1])
+        for dz in range(1, nz):
+            drain(in_z.at[layer, 0], send_z.at[layer, dz - 1])
+            drain(in_z.at[layer, 0], block_send_z.at[layer, dz - 1])
+        for dy in range(1, ny):
+            drain(block_ref.at[layer, pl.ds(0, nz * rows)], block_send_y.at[layer, dy - 1])
+    drain(vec_out.at[0], vec_send_s.at[0])
+    for step in range(1, nx):
+        drain(vec_out.at[1], vec_send_x.at[other(x, step, nx)])
+    count(1, geo.n_seq, lambda k: drain(vec_out.at[2], vec_send_q.at[other(seq, k, geo.n_seq)]))
+
+
+def run_update(geo, grads, mat_momenta, vec_part, vectors, vec_momenta, vec_averages):
+    layers, _, block, width = grads.shape
+    rows = mat_momenta.shape[2]
+    sizes = (layers, rows, width, H // geo.n_batch, FF // geo.n_batch)
+    vmem = pl.BlockSpec(memory_space=pltpu.VMEM)
+    vec = jax.ShapeDtypeStruct(vectors.shape, F32)
+    return pl.pallas_call(
+        functools.partial(update_kernel, geo, sizes),
+        out_shape=(
+            jax.ShapeDtypeStruct((layers, rows, width), F32),
+            jax.ShapeDtypeStruct((layers, block, width), BF16),
+            jax.ShapeDtypeStruct((layers, rows, width), BF16),
+            vec, vec, vec, vec,
+        ),
+        in_specs=[vmem] * 6,
+        out_specs=(vmem,) * 7,
+        scratch_shapes=update_scratch(geo, sizes),
+        compiler_params=pltpu.CompilerParams(
+            collective_id=1, has_side_effects=True, vmem_limit_bytes=60 * 2**20
+        ),
+        name="update",
+    )(grads, mat_momenta, vec_part, vectors, vec_momenta, vec_averages)
 
 
 def per_device(
     geo, stream_in, out_grad, doc_lengths, mats, mat_momenta, mat_averages, vectors, vec_momenta, vec_averages
 ):
-    layer_count, _, shard_rows, model_width = mats.shape
-    activations, grad_resid, full_grads, vec_part = run_network(
-        geo, mats, stream_in, out_grad, doc_lengths, vectors
+    layers, _, rows, width = mats.shape
+    activations, grad_resid, grads, vec_part = run_network(geo, mats, stream_in, out_grad, doc_lengths, vectors)
+    shard, block, ortho, vec_grads, new_vec_momenta, new_vectors, new_vec_averages = run_update(
+        geo, grads, mat_momenta, vec_part, vectors, vec_momenta, vec_averages
     )
-    offsets = [0]
-    for count in [H // geo.n_batch] * 4 + [FF // geo.n_batch] * 2:
-        offsets.append(offsets[-1] + count)
-    block_rows = offsets[6]
-    grad_shard = lax.psum_scatter(
-        full_grads.astype(F32).reshape(layer_count, geo.n_batch * block_rows, model_width),
-        ("batch", "seq"), scatter_dimension=1, tiled=True,
-    )
-    vec_grads = lax.psum(vec_part, ("batch", "seq"))
-    mom_shard = MOMENTUM_DECAY * mat_momenta.reshape(layer_count, shard_rows, model_width) + grad_shard
-    mom_block = lax.all_gather(mom_shard.astype(BF16), "seq", axis=1, tiled=True).astype(F32)
-    pieces = [
-        mom_block[layer_idx, offsets[member] : offsets[member + 1]]
-        for layer_idx in range(layer_count)
-        for member in range(6)
-    ]
-    local_squares = jnp.stack([jnp.sum(piece * piece) for piece in pieces])
-    frob_norms = jnp.sqrt(lax.psum(local_squares, "batch"))
-    iterates = [(piece / (frob_norms[n] + 1e-07)).astype(BF16) for n, piece in enumerate(pieces)]
-    for step_idx in range(NS_STEPS):
-        partials = jnp.stack([dot_tn(iterate, iterate) for iterate in iterates])
-        gram_sums = lax.psum(partials.astype(BF16), "batch").astype(F32)
-        gram_low = gram_sums.astype(BF16)
-        polynomial = QUINTIC[1] * gram_sums + QUINTIC[2] * jnp.einsum(
-            "nde,nef->ndf", gram_low, gram_low, preferred_element_type=F32
-        )
-        poly_low = polynomial.astype(BF16)
-        iterates = [
-            (QUINTIC[0] * iterate.astype(F32) + dot_nn(iterate, poly_low[n])).astype(BF16)
-            for n, iterate in enumerate(iterates)
-        ]
-    factors = [0.2 * math.sqrt(max(count, model_width)) for count in [H] * 4 + [FF] * 2]
-    ortho_block = jnp.stack(
-        [
-            jnp.concatenate([iterates[6 * l + m].astype(F32) * factors[m] for m in range(6)], axis=0)
-            for l in range(layer_count)
-        ]
-    )
-    own_rows = lax.dynamic_slice_in_dim(ortho_block, lax.axis_index("seq") * shard_rows, shard_rows, axis=1)
-    new_flat = mats.reshape(layer_count, shard_rows, model_width) - MATRIX_RATE * own_rows
-    new_avg_flat = (
-        AVERAGE_DECAY * mat_averages.reshape(layer_count, shard_rows, model_width)
-        + (1.0 - AVERAGE_DECAY) * new_flat
-    )
-    new_vec_momenta = MOMENTUM_DECAY * vec_momenta + vec_grads
-    new_vectors = vectors - vector_steps(new_vec_momenta, model_width, H)
-    new_vec_averages = AVERAGE_DECAY * vec_averages + (1.0 - AVERAGE_DECAY) * new_vectors
-    out_shape = (layer_count, 1, shard_rows, model_width)
+    small = lax.axis_index("seq") * rows < 4 * (H // geo.n_batch)
+    factor = jnp.where(small, 0.2 * math.sqrt(max(H, width)), 0.2 * math.sqrt(max(FF, width)))
+    new_mats = mats - MATRIX_RATE * (ortho.astype(F32) * factor).reshape(mats.shape)
+    new_averages = AVERAGE_DECAY * mat_averages + (1.0 - AVERAGE_DECAY) * new_mats
     return (
         activations.reshape(stream_in.shape),
         grad_resid.reshape(stream_in.shape),
-        grad_shard.reshape(out_shape),
-        mom_block.reshape(layer_count, 1, block_rows, model_width),
-        new_flat.reshape(out_shape),
-        new_avg_flat.reshape(out_shape),
+        shard.reshape(mats.shape),
+        block.astype(F32).reshape(layers, 1, *block.shape[1:]),
+        new_mats,
+        new_averages,
         vec_grads,
         new_vec_momenta,
         new_vectors,

time: 1330 us -> 357 us (0.27)
  waiting for transfers between devices: 978 us -> 0 us
  Pallas kernels: 168 us -> 340 us
  matrix products: 65.7 us -> 0 us
  blocking collectives: 47.4 us -> 0 us
  other arithmetic: 34.1 us -> 9.68 us
  between operations: 22.2 us -> 0.73 us
    reduce_scatter x1 -> x0, waiting for transfers between devices: 709 us -> none  [per_device(): lax.psum_scatter(full_grads.astype(F32).reshape(layer_count, geo.n_batch...]
    psum x2 -> x0, waiting for transfers between devices: 197 us -> none  [per_device(): gram_sums = lax.psum(partials.astype(BF16), 'batch').astype(F32)]
    pallas_call x0 -> x1, Pallas kernels: none -> 172 us  [run_update(): pl.pallas_call(functools.partial(update_kernel, geo, sizes), out_shape=(j...]
    all_gather x1 -> x0, waiting for transfers between devices: 72.1 us -> none  [per_device(): lax.all_gather(mom_shard.astype(BF16), 'seq', axis=1, tiled=True)]
    dot_general x50 -> x0, matrix products: 65.7 us -> none  [the longest x24 33.7 us: dot_tn(): lax.dot_general(a, b, (((0,), (0,)), ((), ())), preferred_element_type=F32)]
    psum x2 -> x0, blocking collectives: 47.4 us -> none  [the longest x1 41.5 us: per_device(): vec_grads = lax.psum(vec_part, ('batch', 'seq'))]
    reshape x1 -> x0, other arithmetic: 18.9 us -> none  [per_device(): full_grads.astype(F32)]
  transfers between devices with their start and end apart: 4 -> 0, of which waited for: 4 -> 0; matrix products, arithmetic and copies ran while one was open for 0% -> 0% of each run, Pallas kernels for 0% -> 0%
where the time goes in v2:
time: 357 us; the launch traced here: 356 us
  Pallas kernels  340 us (95%)
  other arithmetic  9.68 us (3%)
  local copies, waits for them, and re-layouts  6.01 us (2%)
    pallas_call x1, Pallas kernels, run_update(): pl.pallas_call(functools.partial(update_kernel, geo, sizes), out_shape=(j...  172 us
    pallas_call x1, Pallas kernels, run_network(): pl.pallas_call(functools.partial(network_kernel, geo, sizes), out_shape=(...  168 us
    unnamed x2, other arithmetic  9.68 us

profile of v2, /device:TPU:26, one launch (start us, length us, event | category | flops | bytes accessed | tf_op | source)
XLA Modules:
  0.0 356.4 jit_solution(2434798618282246467)
XLA Ops:
  0.6 167.6 %network.1 = (bf16[256,512]{1,0:T(8,128)(2,1)}, f32[256,512]{1,0:T(8,128)}, bf16[2,4,2048,512]{3,2,1,0:T(8,128)(2,1)}, f32[2,3072]{1,0:T(2,128)}) custom-call(f32[2,1,256,512]{3,2,1,0:T(8,128)} %mats_ref.1, bf16[256,512]{1,0:T(8,128)(2,1)} %bitcast.38, bf16[256,512]{1,0:T(8,128)(2,1)} %bitcast.39, s32[2,16]{1,0:T(2,128)} %doc_ref.1, f32[2,3072]{1,0:T(2,128)} %vectors_ref.1), custom_call_target="tpu_custom_call" | custom-call | tf_op jit(solution)/shard_map/network/pallas_call | solution.py:624
  168.3 172.4 %update.1 = (f32[2,256,512]{2,1,0:T(8,128)}, bf16[2,2048,512]{2,1,0:T(8,128)(2,1)}, bf16[2,256,512]{2,1,0:T(8,128)(2,1)}, f32[2,3072]{1,0:T(2,128)}, f32[2,3072]...) custom-call(bf16[2,4,2048,512]{3,2,1,0:T(8,128)(2,1)} %get-tuple-element.23.grads, f32[2,1,256,512]{3,2,1,0:T(8,128)} %old_ref.1, ...), custom_call_target="tpu_custom_call" | custom-call | tf_op jit(solution)/shard_map/update/pallas_call | solution.py:1155
  340.7 0.0 copy-start
  340.7 0.0 copy-start.1
  340.7 0.0 copy-start.3
  340.7 0.0 copy-start.2
  340.7 0.0 copy-start.7
  340.7 0.0 copy-start.6
  340.8 0.0 copy-start.5
  340.8 0.0 copy-start.4
  340.8 6.9 %bitcast_convert_fusion = f32[2,1,2048,512]{3,2,1,0:T(8,128)} fusion(bf16[2,2048,512]{2,1,0:T(8,128)(2,1)} %get-tuple-element.26), kind=kLoop, calls=%fused_computation | loop fusion | flops 2097152 | bytes 12582912
  347.7 0.0 copy-done
  347.7 0.0 copy-done.1
  347.7 2.7 fusion.1
  350.5 0.0 copy-done.3
  350.5 0.7 copy.32
  351.2 1.9 copy.33
  353.0 0.0 copy-done.2
  353.0 1.0 copy.34
  354.0 0.6 copy.35
  354.6 0.6 copy.36
  355.2 0.0 copy-done.5
  355.2 0.6 copy.37
  355.8 0.6 copy.38
  (3 shorter events, 0.0 us)
Async XLA Ops:
  340.7 7.0 %copy-start = (f32[2,1,256,512]{3,2,1,0:T(8,128)S(1)}, f32[2,1,256,512]{3,2,1,0:T(8,128)}, u32[]{:S(2)}) copy-start(f32[2,1,256,512]{3,2,1,0:T(8,128)} %mats_ref.1) | copy-start | bytes 3145732
  340.7 7.0 %copy-start.1 = (f32[2,1,256,512]{3,2,1,0:T(8,128)S(1)}, f32[2,1,256,512]{3,2,1,0:T(8,128)}, u32[]{:S(2)}) copy-start(f32[2,1,256,512]{3,2,1,0:T(8,128)} %param.14) | copy-start | bytes 3145732
  340.7 9.7 %copy-start.3 = (bf16[256,512]{1,0:T(8,128)(2,1)S(1)}, bf16[256,512]{1,0:T(8,128)(2,1)}, u32[]{:S(2)}) copy-start(bf16[256,512]{1,0:T(8,128)(2,1)} %get-tuple-element.21) | copy-start | bytes 786436
  340.7 12.3 %copy-start.2 = (f32[2,256,512]{2,1,0:T(8,128)S(1)}, f32[2,256,512]{2,1,0:T(8,128)}, u32[]{:S(2)}) copy-start(f32[2,256,512]{2,1,0:T(8,128)} %get-tuple-element.25) | copy-start | bytes 3145732
  340.7 13.3 %copy-start.7 = (f32[2,3072]{1,0:T(2,128)S(1)}, f32[2,3072]{1,0:T(2,128)}, u32[]{:S(2)}) copy-start(f32[2,3072]{1,0:T(2,128)} %get-tuple-element.60) | copy-start | bytes 73732
  340.7 13.9 %copy-start.6 = (f32[2,3072]{1,0:T(2,128)S(1)}, f32[2,3072]{1,0:T(2,128)}, u32[]{:S(2)}) copy-start(f32[2,3072]{1,0:T(2,128)} %get-tuple-element.61) | copy-start | bytes 73732
  340.8 14.5 %copy-start.5 = (f32[2,3072]{1,0:T(2,128)S(1)}, f32[2,3072]{1,0:T(2,128)}, u32[]{:S(2)}) copy-start(f32[2,3072]{1,0:T(2,128)} %get-tuple-element.62) | copy-start | bytes 73732
  340.8 15.1 %copy-start.4 = (f32[2,3072]{1,0:T(2,128)S(1)}, f32[2,3072]{1,0:T(2,128)}, u32[]{:S(2)}) copy-start(f32[2,3072]{1,0:T(2,128)} %get-tuple-element.63) | copy-start | bytes 73732

commit v3 on v1

v3 whole, which is shorter than its diff:
```python
import functools
import math

import jax
import jax.numpy as jnp
from jax import lax
from jax.experimental import pallas as pl
from jax.experimental.pallas import tpu as pltpu
from jax.sharding import PartitionSpec as P

H = 1024
FF = 2048
NS_STEPS = 2
MESH = pl.DeviceIdType.MESH
F32 = jnp.float32
BF16 = jnp.bfloat16

EPSILON = 1e-05
MOMENTUM_DECAY = 0.5
AVERAGE_DECAY = 0.9
MATRIX_RATE = 0.3
SEGMENT_RATES = (0.3, 0.3, 0.5, 2.0)
QUINTIC = (3.4445, -4.775, 2.0315)
GELU_A = 0.7978845608
GELU_B = 0.044715


class Geometry:
    def __init__(self, n_seq, n_batch):
        self.n_seq, self.n_batch = n_seq, n_batch
        self.nz, self.ny, self.stride_z, self.stride_y = {
            8: (4, 2, 2, 1),
            32: (8, 4, 1, 8),
        }.get(n_seq, (n_seq, 1, 1, n_seq))
        self.nx = n_batch // 2
        self.swaps = self.ny == self.nx
        self.nu, self.nv = self.ny, self.nx

    def seq_of(self, z, y):
        return z * self.stride_z + y * self.stride_y

    def here(self):
        seq, batch = lax.axis_index("seq"), lax.axis_index("batch")
        z = seq // self.stride_z % self.nz
        y = seq // self.stride_y % self.ny
        return seq, batch, z, y, batch // 2, batch % 2

    def to_yx(self, u, v, core):
        if not self.swaps:
            return u, v
        return u + core * (v - u), v + core * (u - v)


def dot_nn(a, b):
    return lax.dot_general(a, b, (((1,), (0,)), ((), ())), preferred_element_type=F32)


def dot_nt(a, b):
    return lax.dot_general(a, b, (((1,), (1,)), ((), ())), preferred_element_type=F32)


def dot_tn(a, b):
    return lax.dot_general(a, b, (((0,), (0,)), ((), ())), preferred_element_type=F32)


def other(mine, step, count):
    return lax.rem(mine + step, count)


def sigmoid(values):
    return 1.0 / (1.0 + jnp.exp(-values))


def widen(column_tile, width):
    return jnp.concatenate([column_tile] * (width // 128), axis=1)


def count(first, last, body):
    lax.fori_loop(first, last, lambda k, _: body(k) or 0, 0)


def remote(src, dst, send, recv, device):
    return pltpu.make_async_remote_copy(
        src_ref=src, dst_ref=dst, send_sem=send, recv_sem=recv, device_id=device, device_id_type=MESH
    )


class Gather:
    def __init__(self, geo, weights, rows, refs):
        self.geo, self.weights, self.rows, self.half_rows = geo, weights, rows, rows // 2
        self.send_z, self.send_u, self.send_v, self.send_s = refs.send_z, refs.send_u, refs.send_v, refs.send_s
        self.recv, self.recv_s = refs.recv, refs.recv_s
        self.seq, self.batch, self.z, self.y, self.x, self.core = geo.here()
        if geo.swaps:
            self.u = self.y + self.core * (self.x - self.y)
            self.v = self.x + self.core * (self.y - self.x)
        else:
            self.u, self.v = self.y, self.x
        self.sibling = (self.seq, self.x * 2 + 1 - self.core)

    def part(self, layer, half, z, u, v):
        y, x = self.geo.to_yx(u, v, self.core)
        start = self.geo.seq_of(z, y) * self.rows + half * self.half_rows
        return self.weights.at[layer, x * 2 + self.core, pl.ds(pl.multiple_of(start, self.half_rows), self.half_rows)]

    def arrival(self, layer, half, z, u, v):
        geo = self.geo
        return self.recv.at[(((layer * 2 + half) * geo.nz + z) * geo.nu + u) * geo.nv + v]

    def device(self, z, u, v):
        y, x = self.geo.to_yx(u, v, self.core)
        return (self.geo.seq_of(z, y), x * 2 + self.core)

    def push(self, layer, half, z, u, device, send):
        part = self.part(layer, half, z, u, self.v)
        remote(part, part, send, self.arrival(layer, half, z, u, self.v), device).start()

    def arrived(self, layer, half, z, u, v):
        part = self.part(layer, half, z, u, v)
        remote(part, part, self.send_s.at[layer], self.arrival(layer, half, z, u, v), self.sibling).wait_recv()

    def along_z(self, layer, half, z, u, go):
        for way, passes, to in (
            (0, jnp.logical_and(z <= self.z, self.z + 1 < self.geo.nz), self.z + 1),
            (1, jnp.logical_and(z >= self.z, self.z >= 1), self.z - 1),
        ):
            sem = self.send_z.at[layer, (half * 2 + way) * self.geo.nz + z, u]

            @pl.when(passes)
            def _():
                go(to, sem)

    def to_z(self, layer, half, z, u):
        self.along_z(
            layer, half, z, u,
            lambda to, sem: self.push(layer, half, z, u, self.device(to, self.u, self.v), sem),
        )

    def to_u(self, layer, half, z):
        for step in range(1, self.geo.nu):
            self.push(
                layer, half, z, self.u, self.device(self.z, other(self.u, step, self.geo.nu), self.v),
                self.send_u.at[layer, half, step - 1],
            )

    def to_v(self, layer, half, z, u):
        for step in range(1, self.geo.nv):
            self.push(
                layer, half, z, u, self.device(self.z, self.u, other(self.v, step, self.geo.nv)),
                self.send_v.at[layer, step - 1],
            )

    def to_sibling(self, layer, half, z, u, v):
        part = self.part(layer, half, z, u, v)
        remote(part, part, self.send_s.at[layer], self.recv_s.at[layer], self.sibling).start()

    def begin(self, layer):
        for half in range(2):
            self.to_z(layer, half, self.z, self.u)
            self.to_u(layer, half, self.z)
            self.to_v(layer, half, self.z, self.u)
            self.to_sibling(layer, half, self.z, self.u, self.v)

        def one(k):
            u = other(self.u, k, self.geo.nu)
            self.arrived(layer, 1, self.z, u, self.v)
            self.to_z(layer, 1, self.z, u)
            self.to_v(layer, 1, self.z, u)
            self.to_sibling(layer, 1, self.z, u, self.v)

        count(1, self.geo.nu, one)

    def at_distance(self, distance, body):
        if distance == 0:
            body(self.z)
            return

        @pl.when(self.z >= distance)
        def _():
            body(self.z - distance)

        @pl.when(self.z + distance < self.geo.nz)
        def _():
            body(self.z + distance)

    def from_z(self, layer, z):
        self.arrived(layer, 0, z, self.u, self.v)
        self.to_z(layer, 0, z, self.u)
        self.to_u(layer, 0, z)
        self.to_v(layer, 0, z, self.u)
        self.to_sibling(layer, 0, z, self.u, self.v)

        def one(k):
            u = other(self.u, k, self.geo.nu)
            self.arrived(layer, 1, z, u, self.v)
            self.to_z(layer, 1, z, u)
            self.to_v(layer, 1, z, u)
            self.to_sibling(layer, 1, z, u, self.v)

        count(0, self.geo.nu, one)

    def from_u(self, layer, z):
        def one(k):
            u = other(self.u, k, self.geo.nu)
            self.arrived(layer, 0, z, u, self.v)
            self.to_v(layer, 0, z, u)
            self.to_sibling(layer, 0, z, u, self.v)

        count(1, self.geo.nu, one)

    def from_v(self, layer, z):
        def one(k):
            half = k % 2
            u = other(self.u, k // 2 // (self.geo.nv - 1), self.geo.nu)
            v = other(self.v, k // 2 % (self.geo.nv - 1) + 1, self.geo.nv)
            self.arrived(layer, half, z, u, v)
            self.to_sibling(layer, half, z, u, v)

        count(0, 2 * self.geo.nu * (self.geo.nv - 1), one)

    def step(self, layer, t):
        nz = self.geo.nz
        if t == 0:
            self.begin(layer)
        if 1 <= t < nz:
            self.at_distance(t, lambda z: self.from_z(layer, z))
        if 1 <= t <= nz:
            self.at_distance(t - 1, lambda z: self.from_u(layer, z))
        if 2 <= t <= nz + 1:
            self.at_distance(t - 2, lambda z: self.from_v(layer, z))

    def steps(self, layers):
        last = self.geo.nz + 1
        order = []
        for layer in range(layers):
            order += [(layer, t) for t in range(0 if layer == 0 else 1, last)]
            if layer + 1 < layers:
                order.append((layer + 1, 0))
            order.append((layer, last))
        return order

    def ready(self, layer):
        part = self.weights.at[layer, pl.ds(0, self.geo.nx)]
        remote(part, part, self.send_s.at[layer], self.recv_s.at[layer], self.sibling).wait_recv()

    def finish(self, layer):
        geo = self.geo

        def drain(part, sem):
            remote(part, part, sem, self.recv_s.at[layer], self.sibling).wait_send()

        one = self.part(layer, 0, self.z, self.u, self.v)
        for z in range(geo.nz):
            self.along_z(layer, 0, z, self.u, lambda to, sem: drain(one, sem))
            for u in range(geo.nu):
                self.along_z(layer, 1, z, u, lambda to, sem: drain(one, sem))
        for step in range(1, geo.nu):
            drain(self.weights.at[layer, 0, pl.ds(0, geo.nz * self.half_rows)], self.send_u.at[layer, 0, step - 1])
            drain(one, self.send_u.at[layer, 1, step - 1])
        for step in range(1, geo.nv):
            drain(self.weights.at[layer, 0, pl.ds(0, geo.nz * geo.nu * self.rows)], self.send_v.at[layer, step - 1])
        drain(self.weights.at[layer, pl.ds(0, geo.nx)], self.send_s.at[layer])


class Scratch:
    def __init__(self):
        self.names, self.shapes = [], []

    def add(self, name, kind, *shape):
        self.names.append(name)
        self.shapes.append(pltpu.SemaphoreType.DMA(shape) if kind is None else pltpu.VMEM(shape, kind))

    def bind(self, refs):
        return dict(zip(self.names, refs, strict=True))


class Sizes:
    def __init__(self, geo, layers, streams, span, width, rows, docs):
        self.layers, self.streams, self.span, self.width = layers, streams, span, width
        self.rows, self.docs = rows, docs
        self.tokens = streams * span
        self.hid, self.ffn = H // geo.n_batch, FF // geo.n_batch
        self.block = 4 * self.hid + 2 * self.ffn
        self.vec = 2 * width + 2 * H


def make_scratch(geo, sz):
    layers, tokens, width, rows, hid, ffn = sz.layers, sz.tokens, sz.width, sz.rows, sz.hid, sz.ffn
    nb, nx, ny, nz, n_seq = geo.n_batch, geo.nx, geo.ny, geo.nz, geo.n_seq
    half, most = width // 2, max(ffn // rows - 1, 1)
    s = Scratch()
    add = s.add
    add("weights", BF16, layers, nb, sz.block, width)
    add("resid", F32, layers + 1, tokens, width)
    for name in ("fgate", "igate", "cand", "states"):
        add(name, F32, layers, nb, tokens, hid)
    add("slope", F32, layers, nb, tokens, ffn)
    add("middle", F32, layers, tokens, width)
    add("gated", BF16, layers, 2 * tokens, width)
    add("normed", BF16, layers, 2 * tokens, width)
    add("states_low", BF16, layers, nx, 2 * tokens, hid)
    add("active", BF16, layers, nx, 2 * tokens, ffn)
    add("ginner", BF16, nx, 2 * tokens, ffn)
    add("gmlp", BF16, 2 * tokens, width)
    add("gy", BF16, 2 * tokens, width)
    add("ggate", BF16, 3, nx, 2 * tokens, hid)
    add("states_out", BF16, nx, tokens, hid)
    add("active_out", BF16, nx, tokens, ffn)
    add("ginner_out", BF16, nx, tokens, ffn)
    add("ggate_out", BF16, 3, nx, tokens, hid)
    add("carry_in", F32, layers, nb, sz.streams, hid)
    add("incoming", F32, nb, sz.streams, hid)
    for name in ("prods", "gstates", "deltas"):
        add(name, F32, nb, tokens, hid)
    add("mask", F32, tokens, 128)
    add("summary", F32, 2 * layers, nb, 2 * sz.streams, hid)
    add("mailbox", F32, 2 * layers, n_seq, nb, 2 * sz.streams, hid)
    add("dgrad", F32, tokens, width)
    add("acc", F32, tokens, width)
    add("wide", F32, tokens, ffn)
    add("gains", F32, layers, 2, width)
    add("biases", F32, layers, nb, 2, hid)
    add("ggains", F32, layers, 2, width)
    add("gbiases", F32, layers, nb, 2, hid)
    add("landing", BF16, nx, sz.block, width)
    add("low_moments", BF16, layers, rows, width)
    add("gram_out", BF16, 3, 3, half, half)
    add("gram_s", BF16, 1, 3, half, half)
    add("gram_x", BF16, nx - 1, 3, half, half)
    add("gram_g", BF16, most, 3, half, half)
    add("square_own", F32, layers, 8, 128)
    add("square_out", F32, 3, 8, 128)
    add("square_s", F32, 1, 8, 128)
    add("square_x", F32, nx - 1, 8, 128)
    add("square_g", F32, most, 8, 128)
    add("odd", F32, width, width)
    add("polys", BF16, layers, 2, width, width)
    add("inverses", F32, layers, 8, 128)
    add("vec_out", F32, 3, layers, sz.vec)
    add("vec_s", F32, 1, layers, sz.vec)
    add("vec_x", F32, nx, layers, sz.vec)
    add("vec_q", F32, n_seq, layers, sz.vec)
    for name, shape in (
        ("load", (4,)),
        ("send_z", (layers, 4 * nz, geo.nu)),
        ("send_u", (layers, 2, geo.nu - 1)),
        ("send_v", (layers, geo.nv - 1)),
        ("send_s", (layers,)),
        ("recv", (layers * 2 * nz * geo.nu * geo.nv,)),
        ("recv_s", (layers,)),
        ("mail_send", (2 * layers, n_seq)),
        ("mail_recv", (2 * layers, n_seq)),
        ("gated_send", (layers,)),
        ("gated_recv", (layers,)),
        ("normed_send", (layers,)),
        ("normed_recv", (layers,)),
        ("states_send", (nx,)),
        ("states_recv", (layers, nx)),
        ("active_send", (nx,)),
        ("active_recv", (layers, nx)),
        ("gmlp_send", (1,)),
        ("gmlp_recv", (1,)),
        ("gy_send", (1,)),
        ("gy_recv", (1,)),
        ("ginner_send", (nx,)),
        ("ginner_recv", (nx,)),
        ("ggate_send", (3, nx)),
        ("ggate_recv", (3, nx)),
        ("sum_send_x", (layers, nx - 1, n_seq)),
        ("sum_send_y", (layers, ny - 1)),
        ("sum_send_z", (layers, nz - 1)),
        ("sum_recv_x", (layers, nx - 1, n_seq)),
        ("sum_recv_y", (layers, ny - 1, nz)),
        ("sum_recv_z", (layers, nz - 1)),
        ("block_send_z", (layers, nz, 2)),
        ("block_send_y", (layers, ny - 1)),
        ("block_recv", (layers, n_seq)),
        ("block_own", (layers,)),
        ("gram_send_s", (2,)),
        ("gram_send_x", (2, nx - 1)),
        ("gram_send_g", (2, most)),
        ("gram_recv_s", (2,)),
        ("gram_recv_x", (2, nx - 1)),
        ("gram_recv_g", (2, most)),
        ("poly_send", (2,)),
        ("poly_recv", (2,)),
        ("vec_send_s", (1,)),
        ("vec_send_x", (nx,)),
        ("vec_send_q", (n_seq,)),
        ("vec_recv_s", (1,)),
        ("vec_recv_x", (nx,)),
        ("vec_recv_q", (n_seq,)),
        ("store", (4,)),
    ):
        add(name, None, *shape)
    for name in ("credit_mlp", "credit_gate", "credit_x", "credit_y", "credit_z"):
        s.names.append(name)
        s.shapes.append(pltpu.SemaphoreType.REGULAR)
    return s

WINDOW = 3
DELAYS = (3, 6, 12)


def step_kernel(
    geo, sz, names, mats_ref, old_ref, x_ref, out_grad_ref, doc_ref, vec_ref, vmom_ref, vavg_ref,
    act_ref, dx_ref, shard_ref, block_ref, ortho_ref, vgrad_ref, new_vmom_ref, new_vec_ref, new_vavg_ref, *scratch
):
    r = type("Refs", (), names.bind(scratch))
    layers, streams, span, width, rows = sz.layers, sz.streams, sz.span, sz.width, sz.rows
    tokens, hid, ffn = sz.tokens, sz.hid, sz.ffn
    nb, nx, ny, nz, n_seq = geo.n_batch, geo.nx, geo.ny, geo.nz, geo.n_seq
    seq, batch, z, y, x, core = geo.here()
    sibling = (seq, x * 2 + 1 - core)
    tile, half, groups = 32, width // 2, span // 8
    weights = r.weights
    at_out, at_up, at_down = 3 * hid, 4 * hid, 4 * hid + ffn
    own_part, far_part = slice(0, tokens), slice(tokens, 2 * tokens)

    def rows_at(k, size):
        return pl.ds(pl.multiple_of(k * size, size), size)

    def each_tile(body):
        count(0, tokens // tile, lambda k: body(rows_at(k, tile)))

    barrier = pltpu.get_barrier_semaphore()

    def greet(seq_id, batch_id):
        pl.semaphore_signal(barrier, inc=1, device_id=(seq_id, batch_id), device_id_type=MESH)

    for step in range(1, n_seq):
        greet(other(seq, step, n_seq), batch)
    for step in range(1, nx):
        greet(seq, other(x, step, nx) * 2 + core)
    greet(*sibling)
    for layer in range(layers):
        pltpu.make_async_copy(
            mats_ref.at[layer, 0], r.resid.at[layer, pl.ds(0, rows)], r.load.at[layer]
        ).start()
    for layer in range(layers):
        pltpu.make_async_copy(
            mats_ref.at[layer, 0], r.resid.at[layer, pl.ds(0, rows)], r.load.at[layer]
        ).wait()
        weights[layer, batch, rows_at(seq, rows), :] = r.resid[layer, 0:rows, :].astype(BF16)
    pl.semaphore_wait(barrier, n_seq - 1 + nx - 1 + 1)

    gather = Gather(geo, weights, rows, r)
    gather_steps = gather.steps(layers)

    def advance(steps):
        for _ in range(min(steps, len(gather_steps))):
            gather.step(*gather_steps.pop(0))

    def need(layer):
        while any(step[0] == layer for step in gather_steps):
            advance(1)
        gather.ready(layer)

    advance(1)

    def each_piece(body):
        for layer in range(layers):
            for k in range(2):
                body(slice(layer, layer + 1), slice(k * width, (k + 1) * width), k, r.gains, r.ggains, (layer,))
                for b in range(nb):
                    first = 2 * width + k * H + b * hid
                    body(slice(layer, layer + 1), slice(first, first + hid), k, r.biases, r.gbiases, (layer, b))

    def read_piece(row, columns, k, kept, made, at):
        kept[(*at, slice(k, k + 1), slice(None))] = vec_ref[row, columns]

    def write_piece(row, columns, k, kept, made, at):
        r.vec_out[0, row, columns] = made[(*at, slice(k, k + 1), slice(None))]

    each_piece(read_piece)
    for stream in range(streams):
        position = seq * span + lax.broadcasted_iota(jnp.int32, (span, 128), 0)
        begin, keep = jnp.int32(0), jnp.ones((span, 128), F32)
        for doc in range(sz.docs):
            keep = jnp.where(position == begin, 0.0, keep)
            begin = begin + doc_ref[stream, doc]
        r.mask[stream * span : (stream + 1) * span, :] = keep

    def load_input(at):
        r.resid[0, at, :] = x_ref[at, :].astype(F32)

    each_tile(load_input)

    def give(src, dst, send, recv):
        remote(src, dst, send, recv, sibling).start()

    def given(dst, recv):
        remote(dst, dst, r.gmlp_send.at[0], recv, sibling).wait_recv()

    def gone(src, send):
        remote(src, src, send, r.gmlp_recv.at[0], sibling).wait_send()

    def blocks(k):
        f = other(x, k + 1, nx)
        return f, 2 * f + core, 2 * f + 1 - core

    def mail(number, forward):
        first, last = (seq + 1, n_seq) if forward else (0, seq)

        def copy(peer, source):
            return remote(
                r.summary.at[number], r.mailbox.at[number, source], r.mail_send.at[number, peer],
                r.mail_recv.at[number, source], (peer, batch),
            )

        hops = seq if forward else n_seq - 1 - seq

        def fold(k, before):
            source = k if forward else n_seq - 1 - k
            copy(source, source).wait_recv()
            packed = r.mailbox[number, source]
            return packed[:, streams:] + packed[:, 0:streams] * before

        def post():
            count(first, last, lambda peer: copy(peer, seq).start())

        def collect():
            total = lax.fori_loop(0, hops, fold, jnp.zeros((nb, streams, hid), F32))
            count(first, last, lambda peer: copy(peer, seq).wait_send())
            return total

        return post, collect

    row8 = lax.broadcasted_iota(jnp.int32, (8, hid), 0)
    start_scan = tuple((jnp.ones((1, hid), F32), jnp.zeros((1, hid), F32)) for _ in range(streams))

    def put_summary(number, b, last):
        for stream in range(streams):
            r.summary[number, b, stream : stream + 1, :] = last[stream][0]
            r.summary[number, b, streams + stream : streams + stream + 1, :] = last[stream][1]

    def forward(layer, pumps):
        gain_one, gain_two = r.gains[layer, 0:1, :], r.gains[layer, 1:2, :]

        def norm_one(at):
            values = r.resid[layer, at, :]
            scale = lax.rsqrt(jnp.mean(values * values, axis=-1, keepdims=True) + EPSILON)
            r.gated[layer, at, :] = (values * scale * gain_one).astype(BF16)

        each_tile(norm_one)
        near = r.gated.at[layer, own_part]
        give(near, r.gated.at[layer, far_part], r.gated_send.at[layer], r.gated_recv.at[layer])
        need(layer)

        def front(b):
            source = r.gated[layer, own_part, :]
            r.wide[:, 0:hid] = dot_nt(source, weights[layer, b, 0:hid, :]) + r.biases[layer, b, 0:1, :]
            r.wide[:, hid : 2 * hid] = dot_nt(source, weights[layer, b, hid : 2 * hid, :]) + r.biases[layer, b, 1:2, :]
            r.cand[layer, b] = dot_nt(source, weights[layer, b, 2 * hid : at_out, :])

            def group(k, carried):
                new = []
                for stream in range(streams):
                    at = pl.ds(pl.multiple_of(stream * span + k * 8, 8), 8)
                    f, i = sigmoid(r.wide[at, 0:hid]), sigmoid(r.wide[at, hid : 2 * hid])
                    share = 1.0 / (f + i)
                    decay = f * share * widen(r.mask[at, :], hid)
                    term = i * share * r.cand[layer, b, at, :]
                    r.fgate[layer, b, at, :] = f
                    r.igate[layer, b, at, :] = i
                    for step in (1, 2, 4):
                        reach = row8 >= step
                        term = term + decay * jnp.where(reach, pltpu.roll(term, step, 0), 0.0)
                        decay = decay * jnp.where(reach, pltpu.roll(decay, step, 0), 1.0)
                    prod_in, state_in = carried[stream]
                    term = term + decay * state_in
                    decay = decay * prod_in
                    r.states[layer, b, at, :] = term
                    r.prods[b, at, :] = decay
                    new.append((decay[7:8], term[7:8]))
                return tuple(new)

            put_summary(layer, b, lax.fori_loop(0, groups, group, start_scan))

        count(0, nb // 2, front)
        pumps[0]()
        count(nb // 2, nb, front)
        post, collect = mail(layer, True)
        post()
        pumps[1]()
        r.carry_in[layer] = collect()
        r.acc[...] = jnp.zeros_like(r.acc)

        def rear(k):
            f, b_own, b_far = blocks(k)

            def states_of(b, put):
                for stream in range(streams):
                    at = slice(stream * span, (stream + 1) * span)
                    full = r.states[layer, b, at, :] + r.prods[b, at, :] * r.carry_in[layer, b, stream : stream + 1, :]
                    r.states[layer, b, at, :] = full
                    put(at, full.astype(BF16))

            def put_far(at, low):
                r.states_out[f, at, :] = low

            def put_own(at, low):
                r.states_low[layer, f, at, :] = low

            states_of(b_far, put_far)
            give(
                r.states_out.at[f], r.states_low.at[layer, f, far_part], r.states_send.at[f],
                r.states_recv.at[layer, f],
            )
            states_of(b_own, put_own)
            r.acc[...] += dot_nn(r.states_out[f], weights[layer, b_far, at_out:at_up, :]) + dot_nn(
                r.states_low[layer, f, own_part, :], weights[layer, b_own, at_out:at_up, :]
            )

        count(0, nx, rear)
        pumps[2]()

        def norm_two(at):
            values = r.resid[layer, at, :] + r.acc[at, :]
            r.middle[layer, at, :] = values
            scale = lax.rsqrt(jnp.mean(values * values, axis=-1, keepdims=True) + EPSILON)
            r.normed[layer, at, :] = (values * scale * gain_two).astype(BF16)

        each_tile(norm_two)
        near = r.normed.at[layer, own_part]
        give(near, r.normed.at[layer, far_part], r.normed_send.at[layer], r.normed_recv.at[layer])
        r.acc[...] = r.middle[layer]

        def mlp(k):
            f, b_own, b_far = blocks(k)

            def active_of(b, put):
                r.wide[...] = dot_nt(r.normed[layer, own_part, :], weights[layer, b, at_up:at_down, :])

                def act(at):
                    v = r.wide[at, :]
                    square = v * v
                    t = jnp.tanh(GELU_A * (v + GELU_B * (v * square)))
                    share = 0.5 * (1.0 + t)
                    put(at, (v * share).astype(BF16))
                    r.slope[layer, b, at, :] = share + 0.5 * v * (1.0 - t * t) * (
                        GELU_A * (1.0 + 3.0 * GELU_B * square)
                    )

                each_tile(act)

            def put_far(at, low):
                r.active_out[f, at, :] = low

            def put_own(at, low):
                r.active[layer, f, at, :] = low

            active_of(b_far, put_far)
            give(r.active_out.at[f], r.active.at[layer, f, far_part], r.active_send.at[f], r.active_recv.at[layer, f])
            r.acc[...] += dot_nn(r.active_out[f], weights[layer, b_far, at_down:, :])
            active_of(b_own, put_own)
            r.acc[...] += dot_nn(r.active[layer, f, own_part, :], weights[layer, b_own, at_down:, :])

        count(0, nx - 1, mlp)
        pumps[3]()
        count(nx - 1, nx, mlp)
        pumps[4]()
        r.resid[layer + 1] = r.acc[...]
        gone(r.gated.at[layer, own_part], r.gated_send.at[layer])
        gone(r.normed.at[layer, own_part], r.normed_send.at[layer])
        for f in range(nx):
            gone(r.states_out.at[f], r.states_send.at[f])
            gone(r.active_out.at[f], r.active_send.at[f])

    def landing_at(layer, j, at):
        blk, first = j // n_seq, pl.multiple_of(j % n_seq * rows, rows)
        if layer == layers - 1:
            return r.landing, (blk, pl.ds(pl.multiple_of(first + at[0], at[1]), at[1]))
        return weights, (layer + 1, 2 * blk + 1 - core, pl.ds(pl.multiple_of(first + at[0], at[1]), at[1]))

    def landing(layer, j):
        ref, index = landing_at(layer, j, (0, rows))
        return ref.at[index]

    base_y, base_z = (nx - 1) * n_seq, (nx - 1) * n_seq + (ny - 1) * nz

    def credit(sem, peers):
        for device in peers:
            pl.semaphore_signal(sem, inc=1, device_id=device, device_id_type=MESH)

    def line_x():
        return [(seq, other(x, step, nx) * 2 + core) for step in range(1, nx)]

    def line_y():
        return [(geo.seq_of(z, other(y, step, ny)), batch) for step in range(1, ny)]

    def line_z():
        return [(geo.seq_of(other(z, step, nz), y), batch) for step in range(1, nz)]

    taken = set()

    def take_credit(name, sem, layer, amount):
        if layer < layers - 1 and (name, layer) not in taken:
            taken.add((name, layer))
            pl.semaphore_wait(sem, amount)

    def slot(layer, s):
        return weights.at[layer, batch, rows_at(s, rows)]

    per_layer, window = n_seq * (nx - 1), WINDOW

    def entry(idx):
        return idx % (nx - 1), n_seq - 1 - idx // (nx - 1)

    def copy_x(layer, idx):
        k, s = entry(idx)
        f, b_own, _ = blocks(k)
        return remote(
            weights.at[layer, b_own, rows_at(s, rows)], landing(layer, k * n_seq + s), r.sum_send_x.at[layer, k, s],
            r.sum_recv_x.at[layer, k, s], (seq, b_own),
        )

    def arrival_x(layer, idx):
        k, s = entry(idx)

        @pl.when(k == nx - 2)
        def _():
            wait_x(layer, s)
            z_at, y_at = s // geo.stride_z % nz, s // geo.stride_y % ny

            @pl.when(y_at != y)
            def _():
                sum_y(layer, z_at, y_at, s)

    def last_index(z_at):
        return max((n_seq - 1 - geo.seq_of(z_at, y_at)) * (nx - 1) + nx - 2 for y_at in range(ny))

    queue = [0, []]

    def place(g):
        return layers - 1 - g // per_layer, g % per_layer

    def x_steps(steps):
        for _ in range(steps):
            g = queue[0]
            if g >= layers * per_layer + window:
                break
            if g >= window:
                copy_x(*place(g - window)).wait_send()
            if g < layers * per_layer:
                layer, idx = place(g)
                if idx == 0:
                    take_credit("x", r.credit_x, layer, nx - 1)
                    take_credit("y", r.credit_y, layer, ny - 1)
                copy_x(layer, idx).start()
            if g >= window:
                layer, idx = place(g - window)
                arrival_x(layer, idx)
                for z_at in reversed(range(nz)):
                    if last_index(z_at) == idx:
                        queue[1].append((g + DELAYS[0], sum_z, layer, z_at))
                        queue[1].append((g + DELAYS[1], own_sum, layer, z_at))
                        queue[1].append((g + DELAYS[2], spread_block, layer, z_at))
            queue[0] += 1
            due = [event for event in queue[1] if event[0] <= g]
            queue[1] = [event for event in queue[1] if event[0] > g]
            for _, body, layer, z_at in due:
                body(layer, z_at)

    def put_grad(layer, b, first, size, value):
        weights[layer, b, first : first + size, :] = value.astype(BF16)

    def backward(layer, pumps):
        gain_one, gain_two = r.gains[layer, 0:1, :], r.gains[layer, 1:2, :]

        def low_grad(at):
            r.gmlp[at, :] = r.dgrad[at, :].astype(BF16)

        each_tile(low_grad)
        take_credit("mlp", r.credit_mlp, layer, 1)
        give(r.gmlp.at[own_part], r.gmlp.at[far_part], r.gmlp_send.at[0], r.gmlp_recv.at[0])
        r.acc[...] = jnp.zeros_like(r.acc)

        def mlp(k):
            f, b_own, b_far = blocks(k)

            def inner_of(b, put):
                r.wide[...] = dot_nt(r.gmlp[own_part, :], weights[layer, b, at_down:, :])

                def act(at):
                    put(at, (r.wide[at, :] * r.slope[layer, b, at, :]).astype(BF16))

                each_tile(act)

            def put_far(at, low):
                r.ginner_out[f, at, :] = low

            def put_own(at, low):
                r.ginner[f, at, :] = low

            inner_of(b_far, put_far)
            give(r.ginner_out.at[f], r.ginner.at[f, far_part], r.ginner_send.at[f], r.ginner_recv.at[f])
            r.acc[...] += dot_nn(r.ginner_out[f], weights[layer, b_far, at_up:at_down, :])
            inner_of(b_own, put_own)
            r.acc[...] += dot_nn(r.ginner[f, own_part, :], weights[layer, b_own, at_up:at_down, :])

            @pl.when(k == 0)
            def _():
                given(r.gmlp.at[far_part], r.gmlp_recv.at[0])
                given(r.normed.at[layer, far_part], r.normed_recv.at[layer])

            given(r.active.at[layer, f, far_part], r.active_recv.at[layer, f])
            put_grad(layer, b_own, at_down, ffn, dot_tn(r.active[layer, f], r.gmlp[...]))
            given(r.ginner.at[f, far_part], r.ginner_recv.at[f])
            put_grad(layer, b_own, at_up, ffn, dot_tn(r.ginner[f], r.normed[layer]))

        count(0, nx, mlp)
        gone(r.gmlp.at[own_part], r.gmlp_send.at[0])
        for f in range(nx):
            gone(r.ginner_out.at[f], r.ginner_send.at[f])
        if layer > 0:
            credit(r.credit_mlp, [sibling])
        pumps[0]()

        def norm_two(k, total):
            at = rows_at(k, tile)
            values, grad = r.middle[layer, at, :], r.acc[at, :]
            scale = lax.rsqrt(jnp.mean(values * values, axis=-1, keepdims=True) + EPSILON)
            unit = values * scale
            gunit = grad * gain_two
            full = r.dgrad[at, :] + scale * (gunit - unit * jnp.mean(gunit * unit, axis=-1, keepdims=True))
            r.dgrad[at, :] = full
            r.gy[at, :] = full.astype(BF16)
            return total + jnp.sum(grad * unit, axis=0, keepdims=True)

        row_sum = jnp.zeros((1, width), F32)
        r.ggains[layer, 1:2, :] = lax.fori_loop(0, tokens // tile, norm_two, row_sum)
        take_credit("gate", r.credit_gate, layer, 1)
        give(r.gy.at[own_part], r.gy.at[far_part], r.gy_send.at[0], r.gy_recv.at[0])
        number = layers + layer

        def front(k):
            f, b_own, b_far = blocks(k)

            def scan(b):
                r.gstates[b] = dot_nt(r.gy[own_part, :], weights[layer, b, at_out:at_up, :])

                def group(k, carried):
                    new = []
                    for stream in range(streams):
                        at = pl.ds(pl.multiple_of(stream * span + (groups - 1 - k) * 8, 8), 8)
                        f, i = r.fgate[layer, b, at, :], r.igate[layer, b, at, :]
                        decay = f * (1.0 / (f + i)) * widen(r.mask[at, :], hid)
                        term = decay * r.gstates[b, at, :]
                        for step in (1, 2, 4):
                            reach = row8 < 8 - step
                            term = term + decay * jnp.where(reach, pltpu.roll(term, 8 - step, 0), 0.0)
                            decay = decay * jnp.where(reach, pltpu.roll(decay, 8 - step, 0), 1.0)
                        prod_in, state_in = carried[stream]
                        term = term + decay * state_in
                        decay = decay * prod_in
                        r.deltas[b, at, :] = term
                        r.prods[b, at, :] = decay
                        new.append((decay[0:1], term[0:1]))
                    return tuple(new)

                put_summary(number, b, lax.fori_loop(0, groups, group, start_scan))

            scan(b_far)
            scan(b_own)

            @pl.when(k == 0)
            def _():
                given(r.gy.at[far_part], r.gy_recv.at[0])

            given(r.states_low.at[layer, f, far_part], r.states_recv.at[layer, f])
            put_grad(layer, b_own, at_out, hid, dot_tn(r.states_low[layer, f], r.gy[...]))

        count(0, nx, front)
        post, collect = mail(number, False)
        post()
        pumps[1]()
        r.incoming[...] = collect()
        r.acc[...] = jnp.zeros_like(r.acc)
        span_row = lax.broadcasted_iota(jnp.int32, (span, hid), 0)
        given(r.gated.at[layer, far_part], r.gated_recv.at[layer])

        def rear(k):
            f, b_own, b_far = blocks(k)

            def gates_of(b, put):
                sum_f, sum_i = jnp.zeros((1, hid), F32), jnp.zeros((1, hid), F32)
                for stream in range(streams):
                    at = slice(stream * span, (stream + 1) * span)
                    late = r.incoming[b, stream : stream + 1, :]
                    linked = r.deltas[b, at, :] + r.prods[b, at, :] * late
                    linked = jnp.where(span_row == span - 1, late, pltpu.roll(linked, span - 1, 0))
                    delta = r.gstates[b, at, :] + linked
                    early = r.carry_in[layer, b, stream : stream + 1, :]
                    before = jnp.where(span_row == 0, early, pltpu.roll(r.states[layer, b, at, :], 1, 0))
                    fg, ig = r.fgate[layer, b, at, :], r.igate[layer, b, at, :]
                    share = 1.0 / (fg + ig)
                    fshare, ishare = fg * share, ig * share
                    gap = delta * (before * widen(r.mask[at, :], hid) - r.cand[layer, b, at, :]) * fshare * ishare
                    gf = (gap * (1.0 - fg)).astype(BF16)
                    gi = (gap * (ig - 1.0)).astype(BF16)
                    put(at, (gf, gi, (delta * ishare).astype(BF16)))
                    sum_f = sum_f + jnp.sum(gf.astype(F32), axis=0, keepdims=True)
                    sum_i = sum_i + jnp.sum(gi.astype(F32), axis=0, keepdims=True)
                r.gbiases[layer, b, 0:1, :] = sum_f
                r.gbiases[layer, b, 1:2, :] = sum_i

            def put_far(at, lows):
                for member in range(3):
                    r.ggate_out[member, f, at, :] = lows[member]

            def put_own(at, lows):
                for member in range(3):
                    r.ggate[member, f, at, :] = lows[member]

            gates_of(b_far, put_far)
            for member in range(3):
                give(
                    r.ggate_out.at[member, f], r.ggate.at[member, f, far_part], r.ggate_send.at[member, f],
                    r.ggate_recv.at[member, f],
                )
            gates_of(b_own, put_own)
            total = r.acc[...]
            for member in range(3):
                at = slice(member * hid, (member + 1) * hid)
                total = total + dot_nn(r.ggate_out[member, f], weights[layer, b_far, at, :])
                total = total + dot_nn(r.ggate[member, f, own_part, :], weights[layer, b_own, at, :])
            r.acc[...] = total
            for member in range(3):
                given(r.ggate.at[member, f, far_part], r.ggate_recv.at[member, f])
                put_grad(layer, b_own, member * hid, hid, dot_tn(r.ggate[member, f], r.gated[layer]))

        count(0, nx, rear)
        gone(r.gy.at[own_part], r.gy_send.at[0])
        for f in range(nx):
            for member in range(3):
                gone(r.ggate_out.at[member, f], r.ggate_send.at[member, f])
        if layer > 0:
            credit(r.credit_gate, [sibling])
            credit(r.credit_x, line_x())
            credit(r.credit_y, line_y())
            credit(r.credit_z, line_z())

        def norm_one(k, total):
            at = rows_at(k, tile)
            values, grad = r.resid[layer, at, :], r.acc[at, :]
            scale = lax.rsqrt(jnp.mean(values * values, axis=-1, keepdims=True) + EPSILON)
            unit = values * scale
            gunit = grad * gain_one
            full = r.dgrad[at, :] + scale * (gunit - unit * jnp.mean(gunit * unit, axis=-1, keepdims=True))
            r.dgrad[at, :] = full
            return total + jnp.sum(grad * unit, axis=0, keepdims=True)

        r.ggains[layer, 0:1, :] = lax.fori_loop(0, tokens // tile, norm_one, row_sum)
        if layer > 0:
            load_old(layer - 1).start()
        pumps[3]()

    def load_old(layer):
        return pltpu.make_async_copy(old_ref.at[layer, 0], r.resid.at[layer + 1, pl.ds(0, rows)], r.load.at[layer])

    def wait_x(layer, s):
        for k in range(nx - 1):
            part = landing(layer, k * n_seq + s)
            remote(part, part, r.sum_send_x.at[layer, k], r.sum_recv_x.at[layer, k, s], sibling).wait_recv()

    def from_x(s):
        return [k * n_seq + s for k in range(nx - 1)]

    def wait_y(layer, z_at):
        for dy in range(1, ny):
            part = landing(layer, base_y + (dy - 1) * nz + z_at)
            remote(
                part, part, r.sum_send_y.at[layer, dy - 1], r.sum_recv_y.at[layer, dy - 1, z_at], sibling
            ).wait_recv()

    def from_y(z_at):
        return [base_y + (dy - 1) * nz + z_at for dy in range(1, ny)]

    part_rows = min(rows, tile)

    def total_of(layer, s, sources, first):
        total = weights[layer, batch, pl.ds(pl.multiple_of(s * rows + first, part_rows), part_rows), :].astype(F32)
        for j in sources:
            ref, index = landing_at(layer, j, (first, part_rows))
            total = total + ref[(*index, slice(None))].astype(F32)
        return total

    def add_up(layer, s, sources):
        def one(k):
            first = k * part_rows
            weights[layer, batch, pl.ds(pl.multiple_of(s * rows + first, part_rows), part_rows), :] = total_of(
                layer, s, sources, first
            ).astype(BF16)

        count(0, rows // part_rows, one)

    def sum_y(layer, z_at, y_at, s):
        add_up(layer, s, from_x(s))
        away = lax.rem(y_at - y + ny, ny) - 1
        remote(
            slot(layer, s), landing(layer, base_y + away * nz + z_at), r.sum_send_y.at[layer, away],
            r.sum_recv_y.at[layer, away, z_at], (geo.seq_of(z, y_at), batch),
        ).start()

    def sum_z(layer, z_at):
        take_credit("z", r.credit_z, layer, nz - 1)
        s = geo.seq_of(z_at, y)
        wait_y(layer, z_at)

        @pl.when(z != z_at)
        def _():
            add_up(layer, s, from_x(s) + from_y(z_at))
            away = lax.rem(z_at - z + nz, nz) - 1
            remote(
                slot(layer, s), landing(layer, base_z + away), r.sum_send_z.at[layer, away],
                r.sum_recv_z.at[layer, away], (s, batch),
            ).start()

    def block_slot(layer, z_at, y_at):
        return block_ref.at[layer, rows_at(geo.seq_of(z_at, y_at), rows)]

    def block_to_y(layer, z_at, part):
        for step in range(1, ny):
            remote(
                part, block_slot(layer, z_at, y), r.block_send_y.at[layer, step - 1],
                r.block_recv.at[layer, geo.seq_of(z_at, y)], (geo.seq_of(z, other(y, step, ny)), batch),
            ).start()

    def own_sum(layer, z_at):
        @pl.when(z == z_at)
        def _():
            for dz in range(1, nz):
                part = landing(layer, base_z + dz - 1)
                remote(
                    part, part, r.sum_send_z.at[layer, dz - 1], r.sum_recv_z.at[layer, dz - 1], sibling
                ).wait_recv()
            load_old(layer).wait()
            sources = from_x(seq) + from_y(z_at) + [base_z + dz - 1 for dz in range(1, nz)]

            def one(k, squares):
                first = k * part_rows
                at = rows_at(k, part_rows)
                total = total_of(layer, seq, sources, first)
                r.middle[layer, at, :] = total
                moment = MOMENTUM_DECAY * r.resid[layer + 1, at, :] + total
                r.resid[layer + 1, at, :] = moment
                r.low_moments[layer, at, :] = moment.astype(BF16)
                return squares + jnp.sum(moment * moment, axis=0, keepdims=True)

            squares = lax.fori_loop(0, rows // part_rows, one, jnp.zeros((1, width), F32))
            r.square_own[layer] = jnp.broadcast_to(jnp.sum(squares, axis=1, keepdims=True), (8, 128))
            part = r.low_moments.at[layer]
            block_to_z(layer, z, part)
            block_to_y(layer, z, part)
            pltpu.make_async_copy(part, block_slot(layer, z, y), r.block_own.at[layer]).start()
            pltpu.make_async_copy(
                r.middle.at[layer, pl.ds(0, rows)], shard_ref.at[layer], r.store.at[layer]
            ).start()

    def along_z(layer, z_at, go):
        for way, passes, to in (
            (0, jnp.logical_and(z_at <= z, z + 1 < nz), z + 1),
            (1, jnp.logical_and(z_at >= z, z >= 1), z - 1),
        ):
            sem = r.block_send_z.at[layer, z_at, way]

            @pl.when(passes)
            def _():
                go(to, sem)

    def block_to_z(layer, z_at, part):
        along_z(
            layer, z_at,
            lambda to, sem: remote(
                part, block_slot(layer, z_at, y), sem, r.block_recv.at[layer, geo.seq_of(z_at, y)],
                (geo.seq_of(to, y), batch),
            ).start(),
        )

    def wait_block(layer, z_at, y_at):
        part = block_slot(layer, z_at, y_at)
        remote(
            part, part, r.block_send_z.at[layer, 0, 0], r.block_recv.at[layer, geo.seq_of(z_at, y_at)], sibling
        ).wait_recv()

    def spread_block(layer, z_at):
        @pl.when(z != z_at)
        def _():
            wait_block(layer, z_at, y)
            block_to_z(layer, z_at, block_slot(layer, z_at, y))
            block_to_y(layer, z_at, block_slot(layer, z_at, y))

    def finish_block(layer):
        for z_at in range(nz):
            count(1, ny, lambda k: wait_block(layer, z_at, other(y, k, ny)))
        pltpu.make_async_copy(r.low_moments.at[layer], block_slot(layer, z, y), r.block_own.at[layer]).wait()
        pltpu.make_async_copy(r.middle.at[layer, pl.ds(0, rows)], shard_ref.at[layer], r.store.at[layer]).wait()

    def vec_start():
        each_piece(write_piece)
        remote(r.vec_out.at[0], r.vec_s.at[0], r.vec_send_s.at[0], r.vec_recv_s.at[0], sibling).start()

    def vec_second():
        remote(r.vec_out.at[0], r.vec_s.at[0], r.vec_send_s.at[0], r.vec_recv_s.at[0], sibling).wait_recv()
        total = r.vec_out[0] + r.vec_s[0]
        r.vec_out[1] = total
        r.vec_x[x] = total
        for step in range(1, nx):
            x_at = other(x, step, nx)
            remote(
                r.vec_out.at[1], r.vec_x.at[x], r.vec_send_x.at[x_at], r.vec_recv_x.at[x], (seq, x_at * 2 + core)
            ).start()

    def vec_third():
        for step in range(1, nx):
            x_at = other(x, step, nx)
            remote(
                r.vec_out.at[1], r.vec_x.at[x_at], r.vec_send_x.at[x_at], r.vec_recv_x.at[x_at], sibling
            ).wait_recv()
        total = r.vec_x[0]
        for k in range(1, nx):
            total = total + r.vec_x[k]
        r.vec_out[2] = total
        r.vec_q[seq] = total

        def one(k):
            to = other(seq, k, n_seq)
            remote(r.vec_out.at[2], r.vec_q.at[seq], r.vec_send_q.at[to], r.vec_recv_q.at[seq], (to, batch)).start()

        count(1, n_seq, one)

    def vec_last():
        def one(k):
            source = other(seq, k, n_seq)
            remote(
                r.vec_out.at[2], r.vec_q.at[source], r.vec_send_q.at[source], r.vec_recv_q.at[source], sibling
            ).wait_recv()

        count(1, n_seq, one)
        total = lax.fori_loop(1, n_seq, lambda k, t: t + r.vec_q[k], r.vec_q[0])
        vgrad_ref[...] = total
        new_vmom_ref[...] = MOMENTUM_DECAY * vmom_ref[...] + total
        first = 0
        for member, length in enumerate((width, width, H, H)):
            at = slice(first, first + length)
            segment = new_vmom_ref[:, at]
            scale = lax.rsqrt(jnp.mean(segment * segment, axis=1, keepdims=True) + 1e-06)
            fresh = vec_ref[:, at] - SEGMENT_RATES[member] * segment * scale
            new_vec_ref[:, at] = fresh
            new_vavg_ref[:, at] = AVERAGE_DECAY * vavg_ref[:, at] + (1.0 - AVERAGE_DECAY) * fresh
            first += length

    hid_devices, ffn_devices = hid // rows, ffn // rows
    in_group = jnp.where(seq < 4 * hid_devices, hid_devices, ffn_devices)
    rank = lax.rem(seq, in_group)
    group_first = seq - rank

    def pack_gram(stage, value):
        r.gram_out[stage, 0] = value[0:half, 0:half].astype(BF16)
        r.gram_out[stage, 1] = value[0:half, half:].astype(BF16)
        r.gram_out[stage, 2] = value[half:, half:].astype(BF16)

    def gram_pair(stage, into, squares_into, sends, recvs, device):
        return (
            remote(r.gram_out.at[stage], into, sends[0], recvs[0], device),
            remote(r.square_out.at[stage], squares_into, sends[1], recvs[1], device),
        )

    def gram_round(stage, parts, squares):
        for n in range(3):
            total = r.gram_out[stage, n].astype(F32)
            for ref in parts:
                total = total + ref[n].astype(F32)
            r.gram_out[stage + 1, n] = total.astype(BF16)
        total = r.square_out[stage]
        for ref in squares:
            total = total + ref[...]
        r.square_out[stage + 1] = total

    def group_copies(k):
        here_at = lax.rem(rank - k - 1 + in_group, in_group)
        return gram_pair(
            2, r.gram_g.at[here_at], r.square_g.at[here_at],
            (r.gram_send_g.at[0, here_at], r.gram_send_g.at[1, here_at]),
            (r.gram_recv_g.at[0, here_at], r.gram_recv_g.at[1, here_at]), (group_first + k, batch),
        )

    def even():
        return jnp.concatenate([r.acc[...], r.resid[0]], axis=0)

    def put_even(value):
        r.acc[...] = value[0:half]
        r.resid[0] = value[half:]

    def newton_schulz(pumps):
        mine, theirs = core, 1 - core
        pack_gram(0, dot_tn(r.low_moments[theirs], r.low_moments[theirs]))
        r.square_out[0] = r.square_own[theirs]
        to_core = gram_pair(
            0, r.gram_s.at[0], r.square_s.at[0], (r.gram_send_s.at[0], r.gram_send_s.at[1]),
            (r.gram_recv_s.at[0], r.gram_recv_s.at[1]), sibling,
        )
        for copy in to_core:
            copy.start()
        put_even(dot_tn(r.low_moments[mine], r.low_moments[mine]))
        for copy in to_core:
            copy.wait()
        pack_gram(0, even())
        r.square_out[0] = r.square_own[mine]
        gram_round(0, [r.gram_s.at[0]], [r.square_s.at[0]])
        to_x = []
        for step in range(1, nx):
            to_x += gram_pair(
                1, r.gram_x.at[step - 1], r.square_x.at[step - 1],
                (r.gram_send_x.at[0, step - 1], r.gram_send_x.at[1, step - 1]),
                (r.gram_recv_x.at[0, step - 1], r.gram_recv_x.at[1, step - 1]),
                (seq, other(x, step, nx) * 2 + core),
            )
        for copy in to_x:
            copy.start()
        pumps[0]()
        for copy in to_x:
            copy.wait()
        gram_round(1, [r.gram_x.at[k] for k in range(nx - 1)], [r.square_x.at[k] for k in range(nx - 1)])

        def to_member(k):
            for copy in group_copies(lax.rem(rank + k, in_group)):
                copy.start()

        def from_member(k):
            k = k - 1
            remote(r.gram_out.at[2], r.gram_g.at[k], r.gram_send_g.at[0, k], r.gram_recv_g.at[0, k], sibling).wait()
            remote(
                r.square_out.at[2], r.square_g.at[k], r.gram_send_g.at[1, k], r.gram_recv_g.at[1, k], sibling
            ).wait()

        count(1, in_group, to_member)
        pumps[1]()
        count(1, in_group, from_member)
        square = lax.fori_loop(1, in_group, lambda k, t: t + r.square_g[k - 1], r.square_out[2])
        inverse = 1.0 / (jnp.sqrt(square) + 1e-07)
        r.inverses[mine] = inverse
        scale = inverse[0:1, 0:1] * inverse[0:1, 0:1]

        def corner(n):
            total = r.gram_out[2, n].astype(F32)
            return lax.fori_loop(1, in_group, lambda k, t: t + r.gram_g[k - 1, n].astype(F32), total) * scale

        r.acc[:, 0:half] = corner(0)
        r.acc[:, half:] = corner(1)
        r.resid[0, :, 0:half] = r.acc[:, half:].T
        r.resid[0, :, half:] = corner(2)

        def polynomial(step):
            low = even().astype(BF16)
            r.polys[mine, step] = (QUINTIC[1] * even() + QUINTIC[2] * dot_nn(low, low)).astype(BF16)

        def precise(low, value):
            high = value.astype(BF16)
            rest = (value - high.astype(F32)).astype(BF16)
            return dot_nn(low, high) + dot_nn(low, rest)

        polynomial(0)
        lead = QUINTIC[0]
        poly = r.polys[mine, 0]
        r.odd[...] = precise(poly, even())
        put_even(lead * lead * even() + 2.0 * lead * r.odd[...] + precise(poly, r.odd[...]))
        polynomial(1)
        out = (
            remote(r.polys.at[mine], r.polys.at[mine], r.poly_send.at[0], r.poly_recv.at[0], sibling),
            remote(r.inverses.at[mine], r.inverses.at[mine], r.poly_send.at[1], r.poly_recv.at[1], sibling),
        )
        for copy in out:
            copy.start()

        def apply(layer):
            begin = (r.resid[layer + 1, 0:rows, :] * r.inverses[layer, 0:1, 0:1]).astype(BF16)
            for step in range(NS_STEPS):
                begin = (lead * begin.astype(F32) + dot_nn(begin, r.polys[layer, step])).astype(BF16)
            ortho_ref[layer] = begin

        apply(mine)
        for copy in out:
            copy.wait_send()
        remote(r.polys.at[theirs], r.polys.at[theirs], r.poly_send.at[0], r.poly_recv.at[0], sibling).wait_recv()
        remote(
            r.inverses.at[theirs], r.inverses.at[theirs], r.poly_send.at[1], r.poly_recv.at[1], sibling
        ).wait_recv()
        apply(theirs)

    def ahead(steps):
        return lambda: advance(steps)

    def nothing():
        pass

    for layer in range(layers):
        pump = ahead(1) if layer < layers - 1 else nothing
        forward(layer, [pump] * 5)
    for layer in range(layers):
        gather.finish(layer)

    def turn(at):
        act_ref[at, :] = r.resid[layers, at, :].astype(BF16)
        r.dgrad[at, :] = out_grad_ref[at, :].astype(F32)

    each_tile(turn)
    load_old(layers - 1).start()

    def starts(steps):
        return lambda: x_steps(steps)

    share = per_layer // 8
    for layer in reversed(range(layers)):
        backward(layer, [starts(2 * share), starts(2 * share), nothing, starts(2 * share)])
    out_dx = pltpu.make_async_copy(r.dgrad, dx_ref, r.store.at[layers])
    out_dx.start()
    vec_start()
    x_steps(share)
    vec_second()
    x_steps(share)
    vec_third()
    x_steps(layers * per_layer + window)
    held = [event for event in queue[1] if event[1] is spread_block]
    for _, body, layer, z_at in sorted(queue[1], key=lambda event: event[0]):
        if body is not spread_block:
            body(layer, z_at)

    def spread(events):
        for _, body, layer, z_at in events:
            body(layer, z_at)

    cut = len(held) // 2
    newton_schulz([lambda: spread(held[:cut]), lambda: spread(held[cut:])])
    vec_last()
    for layer in range(layers):
        finish_block(layer)
    out_dx.wait()

    def drain(part, sem):
        remote(part, part, sem, r.vec_recv_s.at[0], sibling).wait_send()

    for layer in range(layers):
        for dy in range(1, ny):
            drain(weights.at[layer, 0, pl.ds(0, nz * rows)], r.sum_send_y.at[layer, dy - 1])
            drain(weights.at[layer, 0, pl.ds(0, nz * rows)], r.block_send_y.at[layer, dy - 1])
        for dz in range(1, nz):
            drain(r.low_moments.at[layer], r.sum_send_z.at[layer, dz - 1])
        for z_at in range(nz):
            along_z(layer, z_at, lambda to, sem: drain(r.low_moments.at[layer], sem))
    drain(r.vec_out.at[0], r.vec_send_s.at[0])
    for step in range(1, nx):
        drain(r.vec_out.at[1], r.vec_send_x.at[other(x, step, nx)])
    count(1, n_seq, lambda k: drain(r.vec_out.at[2], r.vec_send_q.at[other(seq, k, n_seq)]))


def run_step(geo, stream_in, out_grad, doc_lengths, mats, mat_momenta, vectors, vec_momenta, vec_averages):
    layers, _, rows, width = mats.shape
    streams, span, _ = stream_in.shape
    sz = Sizes(geo, layers, streams, span, width, rows, doc_lengths.shape[1])
    names = make_scratch(geo, sz)
    vmem, anywhere = pl.BlockSpec(memory_space=pltpu.VMEM), pl.BlockSpec(memory_space=pl.ANY)
    smem = pl.BlockSpec(memory_space=pltpu.SMEM)
    vec = jax.ShapeDtypeStruct(vectors.shape, F32)
    return pl.pallas_call(
        functools.partial(step_kernel, geo, sz, names),
        out_shape=(
            jax.ShapeDtypeStruct((sz.tokens, width), BF16),
            jax.ShapeDtypeStruct((sz.tokens, width), F32),
            jax.ShapeDtypeStruct((layers, rows, width), F32),
            jax.ShapeDtypeStruct((layers, sz.block, width), BF16),
            jax.ShapeDtypeStruct((layers, rows, width), BF16),
            vec, vec, vec, vec,
        ),
        in_specs=[anywhere, anywhere, vmem, vmem, smem, vmem, vmem, vmem],
        out_specs=(vmem, anywhere, anywhere, anywhere, vmem, vmem, vmem, vmem, vmem),
        scratch_shapes=names.shapes,
        compiler_params=pltpu.CompilerParams(
            collective_id=0, has_side_effects=True, vmem_limit_bytes=63 * 2**20
        ),
        name="step",
    )(
        mats, mat_momenta, stream_in.reshape(sz.tokens, width), out_grad.reshape(sz.tokens, width), doc_lengths,
        vectors, vec_momenta, vec_averages,
    )


def closing_kernel(
    small_rows, act, dx, shard, block, ortho, mats, averages, vgrad, vmom, vec, vavg,
    act_out, dx_out, shard_out, block_out, mats_out, averages_out, vgrad_out, vmom_out, vec_out, vavg_out,
):
    act_out[...] = act[...]
    dx_out[...] = dx[...]
    shard_out[:, 0] = shard[...]
    block_out[:, 0] = block[...].astype(F32)
    rows, width = mats_out.shape[2] * pl.num_programs(0), mats_out.shape[3]
    small = lax.axis_index("seq") * rows < small_rows
    factor = jnp.where(small, 0.2 * math.sqrt(max(H, width)), 0.2 * math.sqrt(max(FF, width)))
    fresh = mats[:, 0] - MATRIX_RATE * (ortho[...].astype(F32) * factor)
    mats_out[:, 0] = fresh
    averages_out[:, 0] = AVERAGE_DECAY * averages[:, 0] + (1.0 - AVERAGE_DECAY) * fresh
    vgrad_out[...] = vgrad[...]
    vmom_out[...] = vmom[...]
    vec_out[...] = vec[...]
    vavg_out[...] = vavg[...]


def run_closing(geo, act, dx, shard, block, ortho, mats, averages, vecs):
    layers, _, rows, width = mats.shape
    tokens, block_rows = act.shape[0], block.shape[1]
    grid = max(min(8, rows // 16), 1)

    def flat(count):
        return pl.BlockSpec((count // grid, width), lambda k: (k, 0))

    def deep(count):
        return pl.BlockSpec((layers, count // grid, width), lambda k: (0, k, 0))

    def boxed(count):
        return pl.BlockSpec((layers, 1, count // grid, width), lambda k: (0, 0, k, 0))

    vec = pl.BlockSpec(vecs[0].shape, lambda k: (0, 0))
    vec_shape = jax.ShapeDtypeStruct(vecs[0].shape, F32)
    box = jax.ShapeDtypeStruct(mats.shape, F32)
    return pl.pallas_call(
        functools.partial(closing_kernel, 4 * (H // geo.n_batch)),
        grid=(grid,),
        out_shape=(
            jax.ShapeDtypeStruct(act.shape, BF16),
            jax.ShapeDtypeStruct(dx.shape, F32),
            box,
            jax.ShapeDtypeStruct((layers, 1, block_rows, width), F32),
            box,
            box,
            *[vec_shape] * 4,
        ),
        in_specs=[
            flat(tokens), flat(tokens), deep(rows), deep(block_rows), deep(rows), boxed(rows), boxed(rows), *[vec] * 4
        ],
        out_specs=(
            flat(tokens), flat(tokens), boxed(rows), boxed(block_rows), boxed(rows), boxed(rows), *[vec] * 4
        ),
        compiler_params=pltpu.CompilerParams(vmem_limit_bytes=60 * 2**20),
        name="closing",
    )(act, dx, shard, block, ortho, mats, averages, *vecs)


def per_device(
    geo, stream_in, out_grad, doc_lengths, mats, mat_momenta, mat_averages, vectors, vec_momenta, vec_averages
):
    act, dx, shard, block, ortho, *vecs = run_step(
        geo, stream_in, out_grad, doc_lengths, mats, mat_momenta, vectors, vec_momenta, vec_averages
    )
    act, dx, *rest = run_closing(geo, act, dx, shard, block, ortho, mats, mat_averages, vecs)
    return (act.reshape(stream_in.shape), dx.reshape(stream_in.shape), *rest)


def solution(mesh):
    geo = Geometry(mesh.shape["seq"], mesh.shape["batch"])
    rows = P(None, "batch", "seq", None)
    tokens = P("batch", "seq", None)
    return jax.shard_map(
        functools.partial(per_device, geo),
        mesh=mesh,
        in_specs=(tokens, tokens, P("batch", None), rows, rows, rows, P(), P(), P()),
        out_specs=(tokens, tokens, rows, P(None, "batch", None, None), rows, rows, P(), P(), P(), P()),
        check_vma=False,
    )
```

time: 1330 us -> 275 us (0.21)
  waiting for transfers between devices: 978 us -> 0 us
  Pallas kernels: 168 us -> 274 us
  matrix products: 65.7 us -> 0 us
  blocking collectives: 47.4 us -> 0 us
  other arithmetic: 34.1 us -> 0 us
  between operations: 22.2 us -> 0.81 us
    reduce_scatter x1 -> x0, waiting for transfers between devices: 709 us -> none  [per_device(): lax.psum_scatter(full_grads.astype(F32).reshape(layer_count, geo.n_batch...]
    psum x2 -> x0, waiting for transfers between devices: 197 us -> none  [per_device(): gram_sums = lax.psum(partials.astype(BF16), 'batch').astype(F32)]
    pallas_call x1 -> x2, Pallas kernels: 168 us -> 274 us  [the longest x1 264 us: run_step(): pl.pallas_call(functools.partial(step_kernel, geo, sz, names), out_shape=...]
    all_gather x1 -> x0, waiting for transfers between devices: 72.1 us -> none  [per_device(): lax.all_gather(mom_shard.astype(BF16), 'seq', axis=1, tiled=True)]
    dot_general x50 -> x0, matrix products: 65.7 us -> none  [the longest x24 33.7 us: dot_tn(): lax.dot_general(a, b, (((0,), (0,)), ((), ())), preferred_element_type=F32)]
    psum x2 -> x0, blocking collectives: 47.4 us -> none  [the longest x1 41.5 us: per_device(): vec_grads = lax.psum(vec_part, ('batch', 'seq'))]
    reshape x1 -> x0, other arithmetic: 18.9 us -> none  [per_device(): full_grads.astype(F32)]
  transfers between devices with their start and end apart: 4 -> 0, of which waited for: 4 -> 0; matrix products, arithmetic and copies ran while one was open for 0% -> 0% of each run, Pallas kernels for 0% -> 0%
where the time goes in v3:
time: 275 us
  Pallas kernels  274 us (100%)
    pallas_call x1, Pallas kernels, run_step(): pl.pallas_call(functools.partial(step_kernel, geo, sz, names), out_shape=...  264 us
    pallas_call x1, Pallas kernels, run_closing(): pl.pallas_call(functools.partial(closing_kernel, 4 * (H // geo.n_batch)),...  9.86 us

profile of v3, /device:TPU:26, one launch (start us, length us, event | category | flops | bytes accessed | tf_op | source)
XLA Modules:
  0.0 274.9 jit_solution(16826942750434638731)
XLA Ops:
  0.6 264.2 %step.1 = (bf16[256,512]{1,0:T(8,128)(2,1)}, f32[256,512]{1,0:T(8,128)}, f32[2,256,512]{2,1,0:T(8,128)}, bf16[2,2048,512]{2,1,0:T(8,128)(2,1)}, bf16[2,256,512]{...) custom-call(f32[2,1,256,512]{3,2,1,0:T(8,128)} %mats.1, ...), custom_call_target="tpu_custom_call" | custom-call | tf_op jit(solution)/shard_map/step/pallas_call | solution.py:1366
  264.9 9.9 %closing.1 = (bf16[256,512]{1,0:T(8,128)(2,1)}, f32[256,512]{1,0:T(8,128)}, f32[2,1,256,512]{3,2,1,0:T(8,128)}, f32[2,1,2048,512]{3,2,1,0:T(8,128)}, f32[2,1,256...) custom-call(bf16[256,512]{1,0:T(8,128)(2,1)} %get-tuple-element.29.a, ...), custom_call_target="tpu_custom_call" | custom-call | tf_op jit(solution)/shard_map/closing/pallas_call | solution.py:1426

commit v4 on v3

--- a/solution.py
+++ b/solution.py
@@ -323,6 +323,7 @@
     add("ggains", F32, layers, 2, width)
     add("gbiases", F32, layers, nb, 2, hid)
     add("landing", BF16, nx, sz.block, width)
+    add("landing_below", BF16, layers, rows, width)
     add("low_moments", BF16, layers, rows, width)
     add("gram_out", BF16, 3, 3, half, half)
     add("gram_s", BF16, 1, 3, half, half)
@@ -368,13 +369,13 @@
         ("ggate_recv", (3, nx)),
         ("sum_send_x", (layers, nx - 1, n_seq)),
         ("sum_send_y", (layers, ny - 1)),
-        ("sum_send_z", (layers, nz - 1)),
+        ("sum_send_z", (layers, nz, PIECES)),
         ("sum_recv_x", (layers, nx - 1, n_seq)),
         ("sum_recv_y", (layers, ny - 1, nz)),
-        ("sum_recv_z", (layers, nz - 1)),
-        ("block_send_z", (layers, nz, 2)),
+        ("sum_recv_z", (layers, nz + 1, PIECES)),
+        ("block_send_z", (layers, 2, nz, PIECES)),
         ("block_send_y", (layers, ny - 1)),
-        ("block_recv", (layers, n_seq)),
+        ("block_recv", (layers, n_seq, PIECES)),
         ("block_own", (layers,)),
         ("gram_send_s", (2,)),
         ("gram_send_x", (2, nx - 1)),
@@ -399,7 +400,9 @@
     return s
 
 WINDOW = 3
-DELAYS = (3, 6, 12)
+PIECES = 2
+DELAYS = (1, 2, 3, 2)
+PUMPS = ((1, 1, 1, 1, 1), (2, 1, 1, 1, 1))
 
 
 def step_kernel(
@@ -528,6 +531,14 @@
 
     row8 = lax.broadcasted_iota(jnp.int32, (8, hid), 0)
     start_scan = tuple((jnp.ones((1, hid), F32), jnp.zeros((1, hid), F32)) for _ in range(streams))
+
+    def in_fours(group):
+        def four(k, carried):
+            for step in range(4):
+                carried = group(k * 4 + step, carried)
+            return carried
+
+        return lax.fori_loop(0, groups // 4, four, start_scan)
 
     def put_summary(number, b, last):
         for stream in range(streams):
@@ -575,7 +586,7 @@
                     new.append((decay[7:8], term[7:8]))
                 return tuple(new)
 
-            put_summary(layer, b, lax.fori_loop(0, groups, group, start_scan))
+            put_summary(layer, b, in_fours(group))
 
         count(0, nb // 2, front)
         pumps[0]()
@@ -625,6 +636,7 @@
         near = r.normed.at[layer, own_part]
         give(near, r.normed.at[layer, far_part], r.normed_send.at[layer], r.normed_recv.at[layer])
         r.acc[...] = r.middle[layer]
+
 
         def mlp(k):
             f, b_own, b_far = blocks(k)
@@ -667,30 +679,30 @@
             gone(r.states_out.at[f], r.states_send.at[f])
             gone(r.active_out.at[f], r.active_send.at[f])
 
+    u, v = gather.u, gather.v
+
+    def at_device(z_at, u_at, v_at):
+        y_at, x_at = geo.to_yx(u_at, v_at, core)
+        return (geo.seq_of(z_at, y_at), 2 * x_at + core)
+
     def landing_at(layer, j, at):
         blk, first = j // n_seq, pl.multiple_of(j % n_seq * rows, rows)
+        part = pl.ds(pl.multiple_of(first + at[0], at[1]), at[1])
         if layer == layers - 1:
-            return r.landing, (blk, pl.ds(pl.multiple_of(first + at[0], at[1]), at[1]))
-        return weights, (layer + 1, 2 * blk + 1 - core, pl.ds(pl.multiple_of(first + at[0], at[1]), at[1]))
+            return r.landing, (blk, part)
+        return weights, (layer + 1, 2 * blk + 1 - core, part)
 
     def landing(layer, j):
         ref, index = landing_at(layer, j, (0, rows))
         return ref.at[index]
 
-    base_y, base_z = (nx - 1) * n_seq, (nx - 1) * n_seq + (ny - 1) * nz
+    base_y = (nx - 1) * n_seq
+    base_z = base_y + (ny - 1) * nz
+    below = None
 
     def credit(sem, peers):
         for device in peers:
             pl.semaphore_signal(sem, inc=1, device_id=device, device_id_type=MESH)
-
-    def line_x():
-        return [(seq, other(x, step, nx) * 2 + core) for step in range(1, nx)]
-
-    def line_y():
-        return [(geo.seq_of(z, other(y, step, ny)), batch) for step in range(1, ny)]
-
-    def line_z():
-        return [(geo.seq_of(other(z, step, nz), y), batch) for step in range(1, nz)]
 
     taken = set()
 
@@ -699,68 +711,109 @@
             taken.add((name, layer))
             pl.semaphore_wait(sem, amount)
 
-    def slot(layer, s):
-        return weights.at[layer, batch, rows_at(s, rows)]
-
-    per_layer, window = n_seq * (nx - 1), WINDOW
+    def slot(layer, z_at, u_at, v_at):
+        s, b = at_device(z_at, u_at, v_at)
+        return weights.at[layer, b, rows_at(s, rows)]
+
+    z_groups = [[z_at for z_at in reversed(range(nz)) if z_at >= nz // 2], list(range(nz // 2))]
+    order = [
+        (z_at, du, dv)
+        for group in z_groups
+        for du in [*range(1, ny), 0]
+        for z_at in group
+        for dv in range(1, nx)
+    ]
+    per_layer, window = len(order), WINDOW
 
     def entry(idx):
-        return idx % (nx - 1), n_seq - 1 - idx // (nx - 1)
+        return order[idx]
+
+    def leading(good):
+        return next((n for n, one in enumerate(order) if not good(*one)), per_layer)
+
+    def from_mlp(z_at):
+        return all(geo.seq_of(z_at, y_at) * rows >= at_up for y_at in range(ny))
+
+    started = (
+        leading(lambda z_at, du, dv: du and from_mlp(z_at)),
+        leading(lambda z_at, du, dv: from_mlp(z_at)),
+        leading(lambda z_at, du, dv: du or from_mlp(z_at)),
+        per_layer,
+    )
 
     def copy_x(layer, idx):
-        k, s = entry(idx)
-        f, b_own, _ = blocks(k)
+        z_at, du, dv = entry(idx)
+        u_at, v_at = other(u, du, ny), other(v, dv, nx)
+        s = z_at * ny + u_at
         return remote(
-            weights.at[layer, b_own, rows_at(s, rows)], landing(layer, k * n_seq + s), r.sum_send_x.at[layer, k, s],
-            r.sum_recv_x.at[layer, k, s], (seq, b_own),
+            slot(layer, z_at, u_at, v_at), landing(layer, (dv - 1) * n_seq + s),
+            r.sum_send_x.at[layer, dv - 1, z_at * ny + du], r.sum_recv_x.at[layer, dv - 1, s],
+            at_device(z, u, v_at),
         )
 
+    def from_x(z_at, u_at):
+        return [(dv - 1) * n_seq + z_at * ny + u_at for dv in range(1, nx)]
+
     def arrival_x(layer, idx):
-        k, s = entry(idx)
-
-        @pl.when(k == nx - 2)
-        def _():
-            wait_x(layer, s)
-            z_at, y_at = s // geo.stride_z % nz, s // geo.stride_y % ny
-
-            @pl.when(y_at != y)
-            def _():
-                sum_y(layer, z_at, y_at, s)
-
-    def last_index(z_at):
-        return max((n_seq - 1 - geo.seq_of(z_at, y_at)) * (nx - 1) + nx - 2 for y_at in range(ny))
+        z_at, du, dv = entry(idx)
+        if dv < nx - 1:
+            return
+        u_at = other(u, du, ny)
+        s = z_at * ny + u_at
+        for dv in range(1, nx):
+            part = landing(layer, (dv - 1) * n_seq + s)
+            remote(part, part, r.sum_send_x.at[layer, 0, 0], r.sum_recv_x.at[layer, dv - 1, s], sibling).wait_recv()
+        if du:
+            add_up(layer, z_at, u_at, from_x(z_at, u_at))
+            remote(
+                slot(layer, z_at, u_at, v), landing(layer, base_y + (du - 1) * nz + z_at),
+                r.sum_send_y.at[layer, du - 1], r.sum_recv_y.at[layer, du - 1, z_at], at_device(z, u_at, v),
+            ).start()
 
     queue = [0, []]
 
     def place(g):
         return layers - 1 - g // per_layer, g % per_layer
 
-    def x_steps(steps):
+    def plan(g, layer, z_at):
+        far = max(z_at, nz - 1 - z_at)
+        at = g + DELAYS[0]
+        for distance in range(far, 0, -1):
+            queue[1].append((at, functools.partial(sum_z, layer, z_at, distance), False))
+            at += DELAYS[1]
+        queue[1].append((at, functools.partial(own_sum, layer, z_at), False))
+        at += DELAYS[2]
+        for distance in range(1, far + 1):
+            queue[1].append((at, functools.partial(spread_block, layer, z_at, distance), layer == 0))
+            at += DELAYS[3]
+
+    def x_steps(steps, layer=0, limit=per_layer + window):
         for _ in range(steps):
             g = queue[0]
-            if g >= layers * per_layer + window:
+            if g >= (layers - 1 - layer) * per_layer + limit:
                 break
             if g >= window:
                 copy_x(*place(g - window)).wait_send()
             if g < layers * per_layer:
-                layer, idx = place(g)
+                to, idx = place(g)
                 if idx == 0:
-                    take_credit("x", r.credit_x, layer, nx - 1)
-                    take_credit("y", r.credit_y, layer, ny - 1)
-                copy_x(layer, idx).start()
+                    take_credit("x", r.credit_x, to, nx - 1)
+                    take_credit("y", r.credit_y, to, ny - 1)
+                copy_x(to, idx).start()
             if g >= window:
-                layer, idx = place(g - window)
-                arrival_x(layer, idx)
-                for z_at in reversed(range(nz)):
-                    if last_index(z_at) == idx:
-                        queue[1].append((g + DELAYS[0], sum_z, layer, z_at))
-                        queue[1].append((g + DELAYS[1], own_sum, layer, z_at))
-                        queue[1].append((g + DELAYS[2], spread_block, layer, z_at))
+                to, idx = place(g - window)
+                arrival_x(to, idx)
+                z_at, du, dv = order[idx]
+                if not du and dv == nx - 1:
+                    plan(g, to, z_at)
             queue[0] += 1
-            due = [event for event in queue[1] if event[0] <= g]
-            queue[1] = [event for event in queue[1] if event[0] > g]
-            for _, body, layer, z_at in due:
-                body(layer, z_at)
+            run_events(g)
+
+    def run_events(until, held=False):
+        due = sorted((e for e in queue[1] if e[0] <= until and (held or not e[2])), key=lambda e: e[0])
+        queue[1] = [e for e in queue[1] if not (e[0] <= until and (held or not e[2]))]
+        for event in due:
+            event[1]()
 
     def put_grad(layer, b, first, size, value):
         weights[layer, b, first : first + size, :] = value.astype(BF16)
@@ -809,13 +862,15 @@
             given(r.ginner.at[f, far_part], r.ginner_recv.at[f])
             put_grad(layer, b_own, at_up, ffn, dot_tn(r.ginner[f], r.normed[layer]))
 
-        count(0, nx, mlp)
+        count(0, nx - 1, mlp)
+        pumps[0]()
+        count(nx - 1, nx, mlp)
         gone(r.gmlp.at[own_part], r.gmlp_send.at[0])
         for f in range(nx):
             gone(r.ginner_out.at[f], r.ginner_send.at[f])
         if layer > 0:
             credit(r.credit_mlp, [sibling])
-        pumps[0]()
+        pumps[1]()
 
         def norm_two(k, total):
             at = rows_at(k, tile)
@@ -859,7 +914,7 @@
                         new.append((decay[0:1], term[0:1]))
                     return tuple(new)
 
-                put_summary(number, b, lax.fori_loop(0, groups, group, start_scan))
+                put_summary(number, b, in_fours(group))
 
             scan(b_far)
             scan(b_own)
@@ -874,7 +929,7 @@
         count(0, nx, front)
         post, collect = mail(number, False)
         post()
-        pumps[1]()
+        pumps[2]()
         r.incoming[...] = collect()
         r.acc[...] = jnp.zeros_like(r.acc)
         span_row = lax.broadcasted_iota(jnp.int32, (span, hid), 0)
@@ -930,16 +985,23 @@
                 given(r.ggate.at[member, f, far_part], r.ggate_recv.at[member, f])
                 put_grad(layer, b_own, member * hid, hid, dot_tn(r.ggate[member, f], r.gated[layer]))
 
-        count(0, nx, rear)
+        count(0, nx - 1, rear)
+        pumps[3]()
+        count(nx - 1, nx, rear)
         gone(r.gy.at[own_part], r.gy_send.at[0])
         for f in range(nx):
             for member in range(3):
                 gone(r.ggate_out.at[member, f], r.ggate_send.at[member, f])
         if layer > 0:
             credit(r.credit_gate, [sibling])
-            credit(r.credit_x, line_x())
-            credit(r.credit_y, line_y())
-            credit(r.credit_z, line_z())
+            credit(r.credit_x, [(seq, 2 * other(x, step, nx) + core) for step in range(1, nx)])
+            credit(r.credit_y, [(geo.seq_of(z, other(y, step, ny)), batch) for step in range(1, ny)])
+            for way, ends in ((1, z + 1 < nz), (-1, z >= 1)):
+
+                @pl.when(ends)
+                def _():
+                    credit(r.credit_z, [(geo.seq_of(z + way, y), batch)])
+
 
         def norm_one(k, total):
             at = rows_at(k, tile)
@@ -954,18 +1016,38 @@
         r.ggains[layer, 0:1, :] = lax.fori_loop(0, tokens // tile, norm_one, row_sum)
         if layer > 0:
             load_old(layer - 1).start()
-        pumps[3]()
+        pumps[4]()
 
     def load_old(layer):
         return pltpu.make_async_copy(old_ref.at[layer, 0], r.resid.at[layer + 1, pl.ds(0, rows)], r.load.at[layer])
 
-    def wait_x(layer, s):
-        for k in range(nx - 1):
-            part = landing(layer, k * n_seq + s)
-            remote(part, part, r.sum_send_x.at[layer, k], r.sum_recv_x.at[layer, k, s], sibling).wait_recv()
-
-    def from_x(s):
-        return [k * n_seq + s for k in range(nx - 1)]
+    part_rows = min(rows // PIECES, tile)
+    piece_rows = rows // PIECES
+
+    def total_of(layer, z_at, u_at, sources, first):
+        s, b = at_device(z_at, u_at, v)
+        total = weights[layer, b, pl.ds(pl.multiple_of(s * rows + first, part_rows), part_rows), :].astype(F32)
+        for j in sources:
+            if j is None:
+                total = total + r.landing_below[layer, pl.ds(pl.multiple_of(first, part_rows), part_rows), :].astype(F32)
+            else:
+                ref, index = landing_at(layer, j, (first, part_rows))
+                total = total + ref[(*index, slice(None))].astype(F32)
+        return total
+
+    def add_up(layer, z_at, u_at, sources, start=0, size=rows):
+        s, b = at_device(z_at, u_at, v)
+
+        def one(k):
+            first = start + k * part_rows
+            weights[layer, b, pl.ds(pl.multiple_of(s * rows + first, part_rows), part_rows), :] = total_of(
+                layer, z_at, u_at, sources, first
+            ).astype(BF16)
+
+        count(0, size // part_rows, one)
+
+    def from_y(z_at):
+        return [base_y + (dy - 1) * nz + z_at for dy in range(1, ny)]
 
     def wait_y(layer, z_at):
         for dy in range(1, ny):
@@ -974,127 +1056,129 @@
                 part, part, r.sum_send_y.at[layer, dy - 1], r.sum_recv_y.at[layer, dy - 1, z_at], sibling
             ).wait_recv()
 
-    def from_y(z_at):
-        return [base_y + (dy - 1) * nz + z_at for dy in range(1, ny)]
-
-    part_rows = min(rows, tile)
-
-    def total_of(layer, s, sources, first):
-        total = weights[layer, batch, pl.ds(pl.multiple_of(s * rows + first, part_rows), part_rows), :].astype(F32)
-        for j in sources:
-            ref, index = landing_at(layer, j, (first, part_rows))
-            total = total + ref[(*index, slice(None))].astype(F32)
-        return total
-
-    def add_up(layer, s, sources):
-        def one(k):
-            first = k * part_rows
-            weights[layer, batch, pl.ds(pl.multiple_of(s * rows + first, part_rows), part_rows), :] = total_of(
-                layer, s, sources, first
-            ).astype(BF16)
-
-        count(0, rows // part_rows, one)
-
-    def sum_y(layer, z_at, y_at, s):
-        add_up(layer, s, from_x(s))
-        away = lax.rem(y_at - y + ny, ny) - 1
-        remote(
-            slot(layer, s), landing(layer, base_y + away * nz + z_at), r.sum_send_y.at[layer, away],
-            r.sum_recv_y.at[layer, away, z_at], (geo.seq_of(z, y_at), batch),
-        ).start()
-
-    def sum_z(layer, z_at):
-        take_credit("z", r.credit_z, layer, nz - 1)
-        s = geo.seq_of(z_at, y)
-        wait_y(layer, z_at)
-
-        @pl.when(z != z_at)
-        def _():
-            add_up(layer, s, from_x(s) + from_y(z_at))
-            away = lax.rem(z_at - z + nz, nz) - 1
-            remote(
-                slot(layer, s), landing(layer, base_z + away), r.sum_send_z.at[layer, away],
-                r.sum_recv_z.at[layer, away], (s, batch),
-            ).start()
+    def piece(ref, k):
+        return ref.at[pl.ds(k * piece_rows, piece_rows)]
+
+    def wait_z(layer, number, k):
+        part = piece(r.landing_below.at[layer], k)
+        remote(part, part, r.sum_send_z.at[layer, 0, k], r.sum_recv_z.at[layer, number, k], sibling).wait_recv()
+
+    def sum_z(layer, z_at, distance):
+        def step(z_here, way):
+            if not 0 <= z_here < nz:
+                return
+
+            @pl.when(z == z_here)
+            def _():
+                sources = from_x(z_at, u) + from_y(z_at)
+                wait_y(layer, z_at)
+                inner = 0 <= z_here + way < nz
+                if inner:
+                    sources = sources + [base_z + z_at]
+                to = z_here - way
+                if way < 0 and to == z_at:
+                    into, number = r.landing_below.at[layer], nz
+                else:
+                    into, number = landing(layer, base_z + z_at), z_at
+                for k in range(PIECES):
+                    if inner:
+                        wait_z(layer, z_at, k)
+                    add_up(layer, z_at, u, sources, k * piece_rows, piece_rows)
+                    remote(
+                        piece(slot(layer, z_at, u, v), k), piece(into, k), r.sum_send_z.at[layer, z_at, k],
+                        r.sum_recv_z.at[layer, number, k], at_device(to, u, v),
+                    ).start()
+
+        if ("z", layer) not in taken:
+            both = lax.convert_element_type(z + 1 < nz, jnp.int32) + lax.convert_element_type(z >= 1, jnp.int32)
+            take_credit("z", r.credit_z, layer, both)
+        step(z_at + distance, 1)
+        step(z_at - distance, -1)
 
     def block_slot(layer, z_at, y_at):
         return block_ref.at[layer, rows_at(geo.seq_of(z_at, y_at), rows)]
 
-    def block_to_y(layer, z_at, part):
-        for step in range(1, ny):
-            remote(
-                part, block_slot(layer, z_at, y), r.block_send_y.at[layer, step - 1],
-                r.block_recv.at[layer, geo.seq_of(z_at, y)], (geo.seq_of(z, other(y, step, ny)), batch),
-            ).start()
-
-    def own_sum(layer, z_at):
-        @pl.when(z == z_at)
-        def _():
-            for dz in range(1, nz):
-                part = landing(layer, base_z + dz - 1)
-                remote(
-                    part, part, r.sum_send_z.at[layer, dz - 1], r.sum_recv_z.at[layer, dz - 1], sibling
-                ).wait_recv()
-            load_old(layer).wait()
-            sources = from_x(seq) + from_y(z_at) + [base_z + dz - 1 for dz in range(1, nz)]
-
-            def one(k, squares):
-                first = k * part_rows
-                at = rows_at(k, part_rows)
-                total = total_of(layer, seq, sources, first)
-                r.middle[layer, at, :] = total
-                moment = MOMENTUM_DECAY * r.resid[layer + 1, at, :] + total
-                r.resid[layer + 1, at, :] = moment
-                r.low_moments[layer, at, :] = moment.astype(BF16)
-                return squares + jnp.sum(moment * moment, axis=0, keepdims=True)
-
-            squares = lax.fori_loop(0, rows // part_rows, one, jnp.zeros((1, width), F32))
-            r.square_own[layer] = jnp.broadcast_to(jnp.sum(squares, axis=1, keepdims=True), (8, 128))
-            part = r.low_moments.at[layer]
-            block_to_z(layer, z, part)
-            block_to_y(layer, z, part)
-            pltpu.make_async_copy(part, block_slot(layer, z, y), r.block_own.at[layer]).start()
-            pltpu.make_async_copy(
-                r.middle.at[layer, pl.ds(0, rows)], shard_ref.at[layer], r.store.at[layer]
-            ).start()
-
-    def along_z(layer, z_at, go):
+    def block_arrival(layer, z_at, y_at, k):
+        return r.block_recv.at[layer, geo.seq_of(z_at, y_at), k]
+
+    def along_z(layer, z_at, k, go):
         for way, passes, to in (
             (0, jnp.logical_and(z_at <= z, z + 1 < nz), z + 1),
             (1, jnp.logical_and(z_at >= z, z >= 1), z - 1),
         ):
-            sem = r.block_send_z.at[layer, z_at, way]
+            sem = r.block_send_z.at[layer, way, z_at, k]
 
             @pl.when(passes)
             def _():
                 go(to, sem)
 
-    def block_to_z(layer, z_at, part):
+    def pass_block(layer, z_at, part, k):
+        into, arrival = piece(block_slot(layer, z_at, y), k), block_arrival(layer, z_at, y, k)
         along_z(
-            layer, z_at,
-            lambda to, sem: remote(
-                part, block_slot(layer, z_at, y), sem, r.block_recv.at[layer, geo.seq_of(z_at, y)],
-                (geo.seq_of(to, y), batch),
-            ).start(),
+            layer, z_at, k,
+            lambda to, sem: remote(part, into, sem, arrival, (geo.seq_of(to, y), batch)).start(),
         )
-
-    def wait_block(layer, z_at, y_at):
-        part = block_slot(layer, z_at, y_at)
-        remote(
-            part, part, r.block_send_z.at[layer, 0, 0], r.block_recv.at[layer, geo.seq_of(z_at, y_at)], sibling
-        ).wait_recv()
-
-    def spread_block(layer, z_at):
-        @pl.when(z != z_at)
+        for step in range(1, ny):
+            remote(
+                part, into, r.block_send_y.at[layer, step - 1], arrival, (geo.seq_of(z, other(y, step, ny)), batch)
+            ).start()
+
+    def wait_block(layer, z_at, y_at, k):
+        part = piece(block_slot(layer, z_at, y_at), k)
+        remote(part, part, r.block_send_y.at[layer, 0], block_arrival(layer, z_at, y_at, k), sibling).wait_recv()
+
+    def spread_block(layer, z_at, distance):
+        far_away = jnp.logical_or(z == z_at + distance, z == z_at - distance)
+
+        @pl.when(far_away)
         def _():
-            wait_block(layer, z_at, y)
-            block_to_z(layer, z_at, block_slot(layer, z_at, y))
-            block_to_y(layer, z_at, block_slot(layer, z_at, y))
+            for k in range(PIECES):
+                wait_block(layer, z_at, y, k)
+                pass_block(layer, z_at, piece(block_slot(layer, z_at, y), k), k)
+
+    def own_sum(layer, z_at):
+        @pl.when(z == z_at)
+        def _():
+            wait_y(layer, z_at)
+            sources = from_x(z_at, u) + from_y(z_at)
+            if z_at < nz - 1:
+                sources = sources + [base_z + z_at]
+            if z_at > 0:
+                sources = sources + [below]
+            load_old(layer).wait()
+            squares = jnp.zeros((1, width), F32)
+            for k in range(PIECES):
+                if z_at < nz - 1:
+                    wait_z(layer, z_at, k)
+                if z_at > 0:
+                    wait_z(layer, nz, k)
+
+                def one(n, squares):
+                    first = k * piece_rows + n * part_rows
+                    at = pl.ds(pl.multiple_of(first, part_rows), part_rows)
+                    total = total_of(layer, z_at, u, sources, first)
+                    r.middle[layer, at, :] = total
+                    moment = MOMENTUM_DECAY * r.resid[layer + 1, at, :] + total
+                    r.resid[layer + 1, at, :] = moment
+                    r.low_moments[layer, at, :] = moment.astype(BF16)
+                    return squares + jnp.sum(moment * moment, axis=0, keepdims=True)
+
+                squares = lax.fori_loop(0, piece_rows // part_rows, one, squares)
+                pass_block(layer, z_at, piece(r.low_moments.at[layer], k), k)
+            r.square_own[layer] = jnp.broadcast_to(jnp.sum(squares, axis=1, keepdims=True), (8, 128))
+            pltpu.make_async_copy(r.low_moments.at[layer], own_block(layer), r.block_own.at[layer]).start()
+            pltpu.make_async_copy(
+                r.middle.at[layer, pl.ds(0, rows)], shard_ref.at[layer], r.store.at[layer]
+            ).start()
+
+    def own_block(layer):
+        return block_ref.at[layer, rows_at(seq, rows)]
 
     def finish_block(layer):
         for z_at in range(nz):
-            count(1, ny, lambda k: wait_block(layer, z_at, other(y, k, ny)))
-        pltpu.make_async_copy(r.low_moments.at[layer], block_slot(layer, z, y), r.block_own.at[layer]).wait()
+            for k in range(PIECES):
+                count(1, ny, lambda step: wait_block(layer, z_at, other(y, step, ny), k))
+        pltpu.make_async_copy(r.low_moments.at[layer], own_block(layer), r.block_own.at[layer]).wait()
         pltpu.make_async_copy(r.middle.at[layer, pl.ds(0, rows)], shard_ref.at[layer], r.store.at[layer]).wait()
 
     def vec_start():
@@ -1296,8 +1380,7 @@
         pass
 
     for layer in range(layers):
-        pump = ahead(1) if layer < layers - 1 else nothing
-        forward(layer, [pump] * 5)
+        forward(layer, [ahead(1)] * 5)
     for layer in range(layers):
         gather.finish(layer)
 
@@ -1308,12 +1391,17 @@
     each_tile(turn)
     load_old(layers - 1).start()
 
-    def starts(steps):
-        return lambda: x_steps(steps)
-
-    share = per_layer // 8
+    def starts(layer):
+        limits = (started[0], started[1], started[1], started[2], started[3])
+        wanted = PUMPS[layer == layers - 1]
+        return [
+            functools.partial(x_steps, n * max(per_layer // 8, 1), layer, limit)
+            for n, limit in zip(wanted, limits, strict=True)
+        ]
+
+    share = max(per_layer // 8, 1)
     for layer in reversed(range(layers)):
-        backward(layer, [starts(2 * share), starts(2 * share), nothing, starts(2 * share)])
+        backward(layer, starts(layer))
     out_dx = pltpu.make_async_copy(r.dgrad, dx_ref, r.store.at[layers])
     out_dx.start()
     vec_start()
@@ -1322,17 +1410,11 @@
     x_steps(share)
     vec_third()
     x_steps(layers * per_layer + window)
-    held = [event for event in queue[1] if event[1] is spread_block]
-    for _, body, layer, z_at in sorted(queue[1], key=lambda event: event[0]):
-        if body is not spread_block:
-            body(layer, z_at)
-
-    def spread(events):
-        for _, body, layer, z_at in events:
-            body(layer, z_at)
-
-    cut = len(held) // 2
-    newton_schulz([lambda: spread(held[:cut]), lambda: spread(held[cut:])])
+    end = max(event[0] for event in queue[1] if not event[2])
+    run_events(end)
+    held = sorted({event[0] for event in queue[1]})
+    cut = held[len(held) // 2]
+    newton_schulz([lambda: run_events(cut, True), lambda: run_events(held[-1], True)])
     vec_last()
     for layer in range(layers):
         finish_block(layer)
@@ -1345,10 +1427,15 @@
         for dy in range(1, ny):
             drain(weights.at[layer, 0, pl.ds(0, nz * rows)], r.sum_send_y.at[layer, dy - 1])
             drain(weights.at[layer, 0, pl.ds(0, nz * rows)], r.block_send_y.at[layer, dy - 1])
-        for dz in range(1, nz):
-            drain(r.low_moments.at[layer], r.sum_send_z.at[layer, dz - 1])
-        for z_at in range(nz):
-            along_z(layer, z_at, lambda to, sem: drain(r.low_moments.at[layer], sem))
+        for k in range(PIECES):
+            part = piece(r.low_moments.at[layer], k)
+            for z_at in range(nz):
+                along_z(layer, z_at, k, lambda to, sem: drain(part, sem))
+
+                @pl.when(z != z_at)
+                def _():
+                    drain(part, r.sum_send_z.at[layer, z_at, k])
+
     drain(r.vec_out.at[0], r.vec_send_s.at[0])
     for step in range(1, nx):
         drain(r.vec_out.at[1], r.vec_send_x.at[other(x, step, nx)])
@@ -1409,7 +1496,7 @@
 def run_closing(geo, act, dx, shard, block, ortho, mats, averages, vecs):
     layers, _, rows, width = mats.shape
     tokens, block_rows = act.shape[0], block.shape[1]
-    grid = max(min(8, rows // 16), 1)
+    grid = max(min(2, rows // 16), 1)
 
     def flat(count):
         return pl.BlockSpec((count // grid, width), lambda k: (k, 0))

time: 275 us -> 238 us (0.87)
  Pallas kernels: 274 us -> 237 us
    pallas_call x1, Pallas kernels: 264 us -> 230 us  [run_step(): pl.pallas_call(functools.partial(step_kernel, geo, sz, names), out_shape=...]
where the time goes in v4:
time: 238 us
  Pallas kernels  237 us (100%)
    pallas_call x1, Pallas kernels, run_step(): pl.pallas_call(functools.partial(step_kernel, geo, sz, names), out_shape=...  230 us
    pallas_call x1, Pallas kernels, run_closing(): pl.pallas_call(functools.partial(closing_kernel, 4 * (H // geo.n_batch)),...  7.17 us

profile of v4, /device:TPU:26, one launch (start us, length us, event | category | flops | bytes accessed | tf_op | source)
XLA Modules:
  0.0 237.6 jit_solution(7818358882920816973)
XLA Ops:
  0.6 229.6 %step.1 = (bf16[256,512]{1,0:T(8,128)(2,1)}, f32[256,512]{1,0:T(8,128)}, f32[2,256,512]{2,1,0:T(8,128)}, bf16[2,2048,512]{2,1,0:T(8,128)(2,1)}, bf16[2,256,512]{...) custom-call(f32[2,1,256,512]{3,2,1,0:T(8,128)} %mats.1, ...), custom_call_target="tpu_custom_call" | custom-call | tf_op jit(solution)/shard_map/step/pallas_call | solution.py:1453
  230.3 7.2 %closing.1 = (bf16[256,512]{1,0:T(8,128)(2,1)}, f32[256,512]{1,0:T(8,128)}, f32[2,1,256,512]{3,2,1,0:T(8,128)}, f32[2,1,2048,512]{3,2,1,0:T(8,128)}, f32[2,1,256...) custom-call(bf16[256,512]{1,0:T(8,128)(2,1)} %get-tuple-element.29.a, ...), custom_call_target="tpu_custom_call" | custom-call | tf_op jit(solution)/shard_map/closing/pallas_call | solution.py:1513

commit v5 on v4

--- a/solution.py
+++ b/solution.py
@@ -325,18 +325,18 @@
     add("landing", BF16, nx, sz.block, width)
     add("landing_below", BF16, layers, rows, width)
     add("low_moments", BF16, layers, rows, width)
-    add("gram_out", BF16, 3, 3, half, half)
-    add("gram_s", BF16, 1, 3, half, half)
-    add("gram_x", BF16, nx - 1, 3, half, half)
-    add("gram_g", BF16, most, 3, half, half)
+    add("gram_full", BF16, layers, 2, 3, half // 2, half)
+    add("gram_out", BF16, layers, 2, 3, half // 2, half)
+    add("gram_s", BF16, layers, 3, half // 2, half)
+    add("gram_x", BF16, layers, nx - 1, 3, half // 2, half)
+    add("gram_g", BF16, layers, most, 3, half // 2, half)
+    add("gram_sum", F32, layers, 2, 3, half // 2, half)
     add("square_own", F32, layers, 8, 128)
-    add("square_out", F32, 3, 8, 128)
-    add("square_s", F32, 1, 8, 128)
-    add("square_x", F32, nx - 1, 8, 128)
-    add("square_g", F32, most, 8, 128)
+    add("square_out", F32, layers, 2, 8, 128)
+    add("square_s", F32, layers, 8, 128)
+    add("square_x", F32, layers, nx - 1, 8, 128)
+    add("square_g", F32, layers, most, 8, 128)
     add("odd", F32, width, width)
-    add("polys", BF16, layers, 2, width, width)
-    add("inverses", F32, layers, 8, 128)
     add("vec_out", F32, 3, layers, sz.vec)
     add("vec_s", F32, 1, layers, sz.vec)
     add("vec_x", F32, nx, layers, sz.vec)
@@ -377,14 +377,14 @@
         ("block_send_y", (layers, ny - 1)),
         ("block_recv", (layers, n_seq, PIECES)),
         ("block_own", (layers,)),
-        ("gram_send_s", (2,)),
-        ("gram_send_x", (2, nx - 1)),
-        ("gram_send_g", (2, most)),
-        ("gram_recv_s", (2,)),
-        ("gram_recv_x", (2, nx - 1)),
-        ("gram_recv_g", (2, most)),
-        ("poly_send", (2,)),
-        ("poly_recv", (2,)),
+        ("gram_send_s", (layers, 2)),
+        ("gram_send_x", (layers, nx - 1, 2)),
+        ("gram_send_g", (layers, most, 2)),
+        ("gram_recv_s", (layers, 2)),
+        ("gram_recv_x", (layers, nx - 1, 2)),
+        ("gram_recv_g", (layers, most, 2)),
+        ("gram_send_e", (layers,)),
+        ("gram_recv_e", (layers,)),
         ("vec_send_s", (1,)),
         ("vec_send_x", (nx,)),
         ("vec_send_q", (n_seq,)),
@@ -401,6 +401,9 @@
 
 WINDOW = 3
 PIECES = 2
+CROSSED = 1
+LAST_AHEAD = 16
+NS_PLACES = (1, 2, 4, 6)
 DELAYS = (1, 2, 3, 2)
 PUMPS = ((1, 1, 1, 1, 1), (2, 1, 1, 1, 1))
 
@@ -415,7 +418,7 @@
     nb, nx, ny, nz, n_seq = geo.n_batch, geo.nx, geo.ny, geo.nz, geo.n_seq
     seq, batch, z, y, x, core = geo.here()
     sibling = (seq, x * 2 + 1 - core)
-    tile, half, groups = 32, width // 2, span // 8
+    tile, half, groups = 64, width // 2, span // 8
     weights = r.weights
     at_out, at_up, at_down = 3 * hid, 4 * hid, 4 * hid + ffn
     own_part, far_part = slice(0, tokens), slice(tokens, 2 * tokens)
@@ -532,13 +535,13 @@
     row8 = lax.broadcasted_iota(jnp.int32, (8, hid), 0)
     start_scan = tuple((jnp.ones((1, hid), F32), jnp.zeros((1, hid), F32)) for _ in range(streams))
 
-    def in_fours(group):
-        def four(k, carried):
-            for step in range(4):
-                carried = group(k * 4 + step, carried)
+    def in_eights(group):
+        def eight(k, carried):
+            for step in range(8):
+                carried = group(k * 8 + step, carried)
             return carried
 
-        return lax.fori_loop(0, groups // 4, four, start_scan)
+        return lax.fori_loop(0, groups // 8, eight, start_scan)
 
     def put_summary(number, b, last):
         for stream in range(streams):
@@ -586,7 +589,7 @@
                     new.append((decay[7:8], term[7:8]))
                 return tuple(new)
 
-            put_summary(layer, b, in_fours(group))
+            put_summary(layer, b, in_eights(group))
 
         count(0, nb // 2, front)
         pumps[0]()
@@ -679,10 +682,14 @@
             gone(r.states_out.at[f], r.states_send.at[f])
             gone(r.active_out.at[f], r.active_send.at[f])
 
-    u, v = gather.u, gather.v
-
-    def at_device(z_at, u_at, v_at):
-        y_at, x_at = geo.to_yx(u_at, v_at, core)
+    def crossed(layer):
+        return geo.swaps and layer >= CROSSED
+
+    def axes(layer):
+        return (gather.u, gather.v) if crossed(layer) else (y, x)
+
+    def at_device(layer, z_at, u_at, v_at):
+        y_at, x_at = geo.to_yx(u_at, v_at, core) if crossed(layer) else (u_at, v_at)
         return (geo.seq_of(z_at, y_at), 2 * x_at + core)
 
     def landing_at(layer, j, at):
@@ -712,7 +719,7 @@
             pl.semaphore_wait(sem, amount)
 
     def slot(layer, z_at, u_at, v_at):
-        s, b = at_device(z_at, u_at, v_at)
+        s, b = at_device(layer, z_at, u_at, v_at)
         return weights.at[layer, b, rows_at(s, rows)]
 
     z_groups = [[z_at for z_at in reversed(range(nz)) if z_at >= nz // 2], list(range(nz // 2))]
@@ -743,12 +750,13 @@
 
     def copy_x(layer, idx):
         z_at, du, dv = entry(idx)
+        u, v = axes(layer)
         u_at, v_at = other(u, du, ny), other(v, dv, nx)
         s = z_at * ny + u_at
         return remote(
             slot(layer, z_at, u_at, v_at), landing(layer, (dv - 1) * n_seq + s),
             r.sum_send_x.at[layer, dv - 1, z_at * ny + du], r.sum_recv_x.at[layer, dv - 1, s],
-            at_device(z, u, v_at),
+            at_device(layer, z, u, v_at),
         )
 
     def from_x(z_at, u_at):
@@ -758,6 +766,7 @@
         z_at, du, dv = entry(idx)
         if dv < nx - 1:
             return
+        u, v = axes(layer)
         u_at = other(u, du, ny)
         s = z_at * ny + u_at
         for dv in range(1, nx):
@@ -767,10 +776,10 @@
             add_up(layer, z_at, u_at, from_x(z_at, u_at))
             remote(
                 slot(layer, z_at, u_at, v), landing(layer, base_y + (du - 1) * nz + z_at),
-                r.sum_send_y.at[layer, du - 1], r.sum_recv_y.at[layer, du - 1, z_at], at_device(z, u_at, v),
+                r.sum_send_y.at[layer, du - 1], r.sum_recv_y.at[layer, du - 1, z_at], at_device(layer, z, u_at, v),
             ).start()
 
-    queue = [0, []]
+    queue = [0, [], 0]
 
     def place(g):
         return layers - 1 - g // per_layer, g % per_layer
@@ -784,8 +793,17 @@
         queue[1].append((at, functools.partial(own_sum, layer, z_at), False))
         at += DELAYS[2]
         for distance in range(1, far + 1):
-            queue[1].append((at, functools.partial(spread_block, layer, z_at, distance), layer == 0))
+            queue[1].append((at, functools.partial(spread_block, layer, z_at, distance), layer == 0 and z_at < nz // 2))
             at += DELAYS[3]
+
+    def start_x(until):
+        for g in range(queue[2], min(until, layers * per_layer)):
+            to, idx = place(g)
+            if idx == 0:
+                take_credit("x", r.credit_x, to, nx - 1)
+                take_credit("y", r.credit_y, to, ny - 1)
+            copy_x(to, idx).start()
+            queue[2] = g + 1
 
     def x_steps(steps, layer=0, limit=per_layer + window):
         for _ in range(steps):
@@ -794,12 +812,7 @@
                 break
             if g >= window:
                 copy_x(*place(g - window)).wait_send()
-            if g < layers * per_layer:
-                to, idx = place(g)
-                if idx == 0:
-                    take_credit("x", r.credit_x, to, nx - 1)
-                    take_credit("y", r.credit_y, to, ny - 1)
-                copy_x(to, idx).start()
+            start_x(g + 1)
             if g >= window:
                 to, idx = place(g - window)
                 arrival_x(to, idx)
@@ -914,7 +927,7 @@
                         new.append((decay[0:1], term[0:1]))
                     return tuple(new)
 
-                put_summary(number, b, in_fours(group))
+                put_summary(number, b, in_eights(group))
 
             scan(b_far)
             scan(b_own)
@@ -1025,7 +1038,7 @@
     piece_rows = rows // PIECES
 
     def total_of(layer, z_at, u_at, sources, first):
-        s, b = at_device(z_at, u_at, v)
+        s, b = at_device(layer, z_at, u_at, axes(layer)[1])
         total = weights[layer, b, pl.ds(pl.multiple_of(s * rows + first, part_rows), part_rows), :].astype(F32)
         for j in sources:
             if j is None:
@@ -1036,7 +1049,7 @@
         return total
 
     def add_up(layer, z_at, u_at, sources, start=0, size=rows):
-        s, b = at_device(z_at, u_at, v)
+        s, b = at_device(layer, z_at, u_at, axes(layer)[1])
 
         def one(k):
             first = start + k * part_rows
@@ -1070,6 +1083,7 @@
 
             @pl.when(z == z_here)
             def _():
+                u, v = axes(layer)
                 sources = from_x(z_at, u) + from_y(z_at)
                 wait_y(layer, z_at)
                 inner = 0 <= z_here + way < nz
@@ -1086,7 +1100,7 @@
                     add_up(layer, z_at, u, sources, k * piece_rows, piece_rows)
                     remote(
                         piece(slot(layer, z_at, u, v), k), piece(into, k), r.sum_send_z.at[layer, z_at, k],
-                        r.sum_recv_z.at[layer, number, k], at_device(to, u, v),
+                        r.sum_recv_z.at[layer, number, k], at_device(layer, to, u, v),
                     ).start()
 
         if ("z", layer) not in taken:
@@ -1140,6 +1154,7 @@
         @pl.when(z == z_at)
         def _():
             wait_y(layer, z_at)
+            u = axes(layer)[0]
             sources = from_x(z_at, u) + from_y(z_at)
             if z_at < nz - 1:
                 sources = sources + [base_z + z_at]
@@ -1239,139 +1254,128 @@
     in_group = jnp.where(seq < 4 * hid_devices, hid_devices, ffn_devices)
     rank = lax.rem(seq, in_group)
     group_first = seq - rank
-
-    def pack_gram(stage, value):
-        r.gram_out[stage, 0] = value[0:half, 0:half].astype(BF16)
-        r.gram_out[stage, 1] = value[0:half, half:].astype(BF16)
-        r.gram_out[stage, 2] = value[half:, half:].astype(BF16)
-
-    def gram_pair(stage, into, squares_into, sends, recvs, device):
+    lead = QUINTIC[0]
+
+    def gram_pair(pair, into, squares_into, sends, recvs, device):
         return (
-            remote(r.gram_out.at[stage], into, sends[0], recvs[0], device),
-            remote(r.square_out.at[stage], squares_into, sends[1], recvs[1], device),
+            remote(pair[0], into, sends.at[0], recvs.at[0], device),
+            remote(pair[1], squares_into, sends.at[1], recvs.at[1], device),
         )
 
-    def gram_round(stage, parts, squares):
-        for n in range(3):
-            total = r.gram_out[stage, n].astype(F32)
-            for ref in parts:
-                total = total + ref[n].astype(F32)
-            r.gram_out[stage + 1, n] = total.astype(BF16)
-        total = r.square_out[stage]
-        for ref in squares:
-            total = total + ref[...]
-        r.square_out[stage + 1] = total
-
-    def group_copies(k):
-        here_at = lax.rem(rank - k - 1 + in_group, in_group)
+    def to_core(layer):
         return gram_pair(
-            2, r.gram_g.at[here_at], r.square_g.at[here_at],
-            (r.gram_send_g.at[0, here_at], r.gram_send_g.at[1, here_at]),
-            (r.gram_recv_g.at[0, here_at], r.gram_recv_g.at[1, here_at]), (group_first + k, batch),
+            (r.gram_full.at[layer, 1 - core], r.square_own.at[layer]), r.gram_s.at[layer], r.square_s.at[layer],
+            r.gram_send_s.at[layer], r.gram_recv_s.at[layer], sibling,
         )
+
+    def to_x(layer):
+        out = r.gram_out.at[layer, 0], r.square_out.at[layer, 0]
+        return [
+            copy
+            for step in range(1, nx)
+            for copy in gram_pair(
+                out, r.gram_x.at[layer, step - 1], r.square_x.at[layer, step - 1],
+                r.gram_send_x.at[layer, step - 1], r.gram_recv_x.at[layer, step - 1],
+                (seq, other(x, step, nx) * 2 + core),
+            )
+        ]
+
+    def to_group(layer, here_at, device):
+        return gram_pair(
+            (r.gram_out.at[layer, 1], r.square_out.at[layer, 1]), r.gram_g.at[layer, here_at],
+            r.square_g.at[layer, here_at], r.gram_send_g.at[layer, here_at], r.gram_recv_g.at[layer, here_at], device,
+        )
+
+    def hand_over(layer):
+        part = r.gram_sum.at[layer, core]
+        return remote(part, part, r.gram_send_e.at[layer], r.gram_recv_e.at[layer], sibling)
+
+    def gram_start(layer):
+        value = dot_tn(r.low_moments[layer], r.low_moments[layer])
+        quarter = half // 2
+        for c in range(2):
+            at = slice(c * quarter, (c + 1) * quarter)
+            low = slice(half + c * quarter, half + (c + 1) * quarter)
+            r.gram_full[layer, c, 0] = value[at, 0:half].astype(BF16)
+            r.gram_full[layer, c, 1] = value[at, half:].astype(BF16)
+            r.gram_full[layer, c, 2] = value[low, half:].astype(BF16)
+        for copy in to_core(layer):
+            copy.start()
+
+    def gram_chip(layer):
+        for copy in to_core(layer):
+            copy.wait()
+        r.gram_out[layer, 0] = (r.gram_full[layer, core].astype(F32) + r.gram_s[layer].astype(F32)).astype(BF16)
+        r.square_out[layer, 0] = r.square_own[layer] + r.square_s[layer]
+        for copy in to_x(layer):
+            copy.start()
+
+    def gram_line(layer):
+        for copy in to_x(layer):
+            copy.wait()
+        total, square = r.gram_out[layer, 0].astype(F32), r.square_out[layer, 0]
+        for k in range(nx - 1):
+            total = total + r.gram_x[layer, k].astype(F32)
+            square = square + r.square_x[layer, k]
+        r.gram_out[layer, 1] = total.astype(BF16)
+        r.square_out[layer, 1] = square
+
+        def one(k):
+            to = lax.rem(rank + k, in_group)
+            here_at = lax.rem(rank - to - 1 + in_group, in_group)
+            for copy in to_group(layer, here_at, (group_first + to, batch)):
+                copy.start()
+
+        count(1, in_group, one)
+
+    def gram_group(layer):
+        def one(k):
+            for copy in to_group(layer, k - 1, sibling):
+                copy.wait()
+
+        count(1, in_group, one)
+        r.gram_sum[layer, core] = r.gram_out[layer, 1].astype(F32)
+
+        def add(k):
+            r.gram_sum[layer, core] += r.gram_g[layer, k - 1].astype(F32)
+            r.square_out[layer, 1] += r.square_g[layer, k - 1]
+
+        count(1, in_group, add)
+        hand_over(layer).start()
 
     def even():
         return jnp.concatenate([r.acc[...], r.resid[0]], axis=0)
 
-    def put_even(value):
-        r.acc[...] = value[0:half]
-        r.resid[0] = value[half:]
-
-    def newton_schulz(pumps):
-        mine, theirs = core, 1 - core
-        pack_gram(0, dot_tn(r.low_moments[theirs], r.low_moments[theirs]))
-        r.square_out[0] = r.square_own[theirs]
-        to_core = gram_pair(
-            0, r.gram_s.at[0], r.square_s.at[0], (r.gram_send_s.at[0], r.gram_send_s.at[1]),
-            (r.gram_recv_s.at[0], r.gram_recv_s.at[1]), sibling,
-        )
-        for copy in to_core:
-            copy.start()
-        put_even(dot_tn(r.low_moments[mine], r.low_moments[mine]))
-        for copy in to_core:
-            copy.wait()
-        pack_gram(0, even())
-        r.square_out[0] = r.square_own[mine]
-        gram_round(0, [r.gram_s.at[0]], [r.square_s.at[0]])
-        to_x = []
-        for step in range(1, nx):
-            to_x += gram_pair(
-                1, r.gram_x.at[step - 1], r.square_x.at[step - 1],
-                (r.gram_send_x.at[0, step - 1], r.gram_send_x.at[1, step - 1]),
-                (r.gram_recv_x.at[0, step - 1], r.gram_recv_x.at[1, step - 1]),
-                (seq, other(x, step, nx) * 2 + core),
-            )
-        for copy in to_x:
-            copy.start()
-        pumps[0]()
-        for copy in to_x:
-            copy.wait()
-        gram_round(1, [r.gram_x.at[k] for k in range(nx - 1)], [r.square_x.at[k] for k in range(nx - 1)])
-
-        def to_member(k):
-            for copy in group_copies(lax.rem(rank + k, in_group)):
-                copy.start()
-
-        def from_member(k):
-            k = k - 1
-            remote(r.gram_out.at[2], r.gram_g.at[k], r.gram_send_g.at[0, k], r.gram_recv_g.at[0, k], sibling).wait()
-            remote(
-                r.square_out.at[2], r.square_g.at[k], r.gram_send_g.at[1, k], r.gram_recv_g.at[1, k], sibling
-            ).wait()
-
-        count(1, in_group, to_member)
-        pumps[1]()
-        count(1, in_group, from_member)
-        square = lax.fori_loop(1, in_group, lambda k, t: t + r.square_g[k - 1], r.square_out[2])
-        inverse = 1.0 / (jnp.sqrt(square) + 1e-07)
-        r.inverses[mine] = inverse
-        scale = inverse[0:1, 0:1] * inverse[0:1, 0:1]
+    def polynomial():
+        low = even().astype(BF16)
+        return (QUINTIC[1] * even() + QUINTIC[2] * dot_nn(low, low)).astype(BF16)
+
+    def precise(low, value):
+        high = value.astype(BF16)
+        rest = (value - high.astype(F32)).astype(BF16)
+        return dot_nn(low, high) + dot_nn(low, rest)
+
+    def gram_use(layer):
+        hand_over(layer).wait()
+        inverse = 1.0 / (jnp.sqrt(r.square_out[layer, 1]) + 1e-07)
+        inverse = inverse[0:1, 0:1]
+        scale = inverse * inverse
 
         def corner(n):
-            total = r.gram_out[2, n].astype(F32)
-            return lax.fori_loop(1, in_group, lambda k, t: t + r.gram_g[k - 1, n].astype(F32), total) * scale
+            return jnp.concatenate([r.gram_sum[layer, 0, n], r.gram_sum[layer, 1, n]], axis=0) * scale
 
         r.acc[:, 0:half] = corner(0)
         r.acc[:, half:] = corner(1)
         r.resid[0, :, 0:half] = r.acc[:, half:].T
         r.resid[0, :, half:] = corner(2)
-
-        def polynomial(step):
-            low = even().astype(BF16)
-            r.polys[mine, step] = (QUINTIC[1] * even() + QUINTIC[2] * dot_nn(low, low)).astype(BF16)
-
-        def precise(low, value):
-            high = value.astype(BF16)
-            rest = (value - high.astype(F32)).astype(BF16)
-            return dot_nn(low, high) + dot_nn(low, rest)
-
-        polynomial(0)
-        lead = QUINTIC[0]
-        poly = r.polys[mine, 0]
-        r.odd[...] = precise(poly, even())
-        put_even(lead * lead * even() + 2.0 * lead * r.odd[...] + precise(poly, r.odd[...]))
-        polynomial(1)
-        out = (
-            remote(r.polys.at[mine], r.polys.at[mine], r.poly_send.at[0], r.poly_recv.at[0], sibling),
-            remote(r.inverses.at[mine], r.inverses.at[mine], r.poly_send.at[1], r.poly_recv.at[1], sibling),
-        )
-        for copy in out:
-            copy.start()
-
-        def apply(layer):
-            begin = (r.resid[layer + 1, 0:rows, :] * r.inverses[layer, 0:1, 0:1]).astype(BF16)
-            for step in range(NS_STEPS):
-                begin = (lead * begin.astype(F32) + dot_nn(begin, r.polys[layer, step])).astype(BF16)
-            ortho_ref[layer] = begin
-
-        apply(mine)
-        for copy in out:
-            copy.wait_send()
-        remote(r.polys.at[theirs], r.polys.at[theirs], r.poly_send.at[0], r.poly_recv.at[0], sibling).wait_recv()
-        remote(
-            r.inverses.at[theirs], r.inverses.at[theirs], r.poly_send.at[1], r.poly_recv.at[1], sibling
-        ).wait_recv()
-        apply(theirs)
+        first = polynomial()
+        begin = (r.resid[layer + 1, 0:rows, :] * inverse).astype(BF16)
+        begin = (lead * begin.astype(F32) + dot_nn(begin, first)).astype(BF16)
+        r.odd[...] = precise(first, even())
+        value = lead * lead * even() + 2.0 * lead * r.odd[...] + precise(first, r.odd[...])
+        r.acc[...] = value[0:half]
+        r.resid[0] = value[half:]
+        ortho_ref[layer] = (lead * begin.astype(F32) + dot_nn(begin, polynomial())).astype(BF16)
 
     def ahead(steps):
         return lambda: advance(steps)
@@ -1402,19 +1406,36 @@
     share = max(per_layer // 8, 1)
     for layer in reversed(range(layers)):
         backward(layer, starts(layer))
+    start_x(queue[0] + LAST_AHEAD * share)
     out_dx = pltpu.make_async_copy(r.dgrad, dx_ref, r.store.at[layers])
     out_dx.start()
     vec_start()
-    x_steps(share)
+    x_steps(layers * per_layer + window)
     vec_second()
-    x_steps(share)
-    vec_third()
-    x_steps(layers * per_layer + window)
     end = max(event[0] for event in queue[1] if not event[2])
+    upper = list(range(layers - 1, 0, -1))
+    for step, body in zip(NS_PLACES, (gram_start, gram_chip, gram_line, gram_group), strict=True):
+        run_events(queue[0] - 1 + step)
+        for layer in upper:
+            body(layer)
     run_events(end)
     held = sorted({event[0] for event in queue[1]})
-    cut = held[len(held) // 2]
-    newton_schulz([lambda: run_events(cut, True), lambda: run_events(held[-1], True)])
+
+    def spread(share_done):
+        if held:
+            run_events(held[min(int(share_done * len(held)), len(held) - 1)], True)
+
+    gram_start(0)
+    vec_third()
+    gram_chip(0)
+    spread(0.3)
+    for layer in upper:
+        gram_use(layer)
+    spread(0.6)
+    gram_line(0)
+    spread(1.0)
+    gram_group(0)
+    gram_use(0)
     vec_last()
     for layer in range(layers):
         finish_block(layer)
@@ -1464,7 +1485,7 @@
         out_specs=(vmem, anywhere, anywhere, anywhere, vmem, vmem, vmem, vmem, vmem),
         scratch_shapes=names.shapes,
         compiler_params=pltpu.CompilerParams(
-            collective_id=0, has_side_effects=True, vmem_limit_bytes=63 * 2**20
+            collective_id=0, has_side_effects=True, vmem_limit_bytes=66584576
         ),
         name="step",
     )(

time: 238 us -> 236 us (level)
  no operation moved by 1% of the time
where the time goes in v5:
time: 236 us
  Pallas kernels  235 us (100%)
    pallas_call x1, Pallas kernels, run_step(): pl.pallas_call(functools.partial(step_kernel, geo, sz, names), out_shape=...  228 us
    pallas_call x1, Pallas kernels, run_closing(): pl.pallas_call(functools.partial(closing_kernel, 4 * (H // geo.n_batch)),...  7.17 us

profile of v5, /device:TPU:26, one launch (start us, length us, event | category | flops | bytes accessed | tf_op | source)
XLA Modules:
  0.0 236.0 jit_solution(455248924880337466)
XLA Ops:
  0.6 228.0 %step.1 = (bf16[256,512]{1,0:T(8,128)(2,1)}, f32[256,512]{1,0:T(8,128)}, f32[2,256,512]{2,1,0:T(8,128)}, bf16[2,2048,512]{2,1,0:T(8,128)(2,1)}, bf16[2,256,512]{...) custom-call(f32[2,1,256,512]{3,2,1,0:T(8,128)} %mats.1, ...), custom_call_target="tpu_custom_call" | custom-call | tf_op jit(solution)/shard_map/step/pallas_call | solution.py:1474
  228.7 7.2 %closing.1 = (bf16[256,512]{1,0:T(8,128)(2,1)}, f32[256,512]{1,0:T(8,128)}, f32[2,1,256,512]{3,2,1,0:T(8,128)}, f32[2,1,2048,512]{3,2,1,0:T(8,128)}, f32[2,1,256...) custom-call(bf16[256,512]{1,0:T(8,128)(2,1)} %get-tuple-element.29.a, ...), custom_call_target="tpu_custom_call" | custom-call | tf_op jit(solution)/shard_map/closing/pallas_call | solution.py:1534
